TPU v7x, 128 devices: a whole 4x4x4 slice. The times are simulated.
128 devices in a mesh: row: 4 (over y), col: 32 (over z, x, core).
Axes of the slice: x: 4, y: 4, z: 4, core: 2. Of those that a mesh axis runs over, the one named last changes fastest.
Arguments:
- features: bfloat16 [32768, 128], P(('row', 'col')), may hold values from -6 to 6
- weight: bfloat16 [128, 256], replicated, may hold values from -0.5 to 0.5
- cotangent: bfloat16 [32768, 256], P(('row', 'col')), may hold values from -6 to 6
- tile_values: bfloat16 [4, 32, 320, 128, 128], P('row', 'col'), may hold values from -0.1875 to 0.1875
- tile_rows: int32 [4, 32, 320], P('row', 'col'), may hold values from 0 to 63
- tile_cols: int32 [4, 32, 320], P('row', 'col'), may hold values from 0 to 7
- tile_counts: int32 [4, 32], P('row', 'col'), may hold values from 40 to 320, as said below
Outputs:
- output: bfloat16 [32768, 256], P(('row', 'col'))
- grad_features: bfloat16 [32768, 128], P(('row', 'col'))
- grad_weight: float32 [128, 256], replicated
Inputs may be any that keep to these rules, and one draw needn't show every extreme that they name: Slots 0 to tile_counts - 1 of a grid cell are live and the rest are ignored; the (row tile, column tile) pairs of a cell's live slots are distinct; some cells hold 320 live slots.
All inputs are finite; a program needn't handle non-finite values.
Results may differ from a plain program's by a relative error of at most 0.0049.
Values may be sent and summed in bfloat16 or wider, within the bound.
No kernel may reach another device: no remote copies, remote signals or barrier semaphores. Data moves between devices by JAX's collectives and lax.ppermute only.
A program may use at most 128 MiB of HBM per device.

v0:
```python
import math

import jax
import jax.numpy as jnp
from jax import lax
from jax.sharding import PartitionSpec as P


def silu_slope(values):
    sigmoid_part = jax.nn.sigmoid(values)
    return sigmoid_part * (1.0 + values * (1.0 - sigmoid_part))


def tile_sums(slot_values, slot_rows, slot_cols, live_count, source, out_tiles, flipped):
    slot_total = slot_values.shape[0]
    tile_size = slot_values.shape[1]
    feature_width = source.shape[-1]
    group_size = math.gcd(slot_total, 32)
    block_turns = (live_count + group_size - 1) // group_size
    pattern = "gji,gjh->gih" if flipped else "gij,gjh->gih"
    wide_source = source.dtype == jnp.float32

    def add_group(step_index, running):
        first_slot = step_index * group_size
        group_values = lax.dynamic_slice_in_dim(slot_values, first_slot, group_size, 0)
        group_rows = lax.dynamic_slice_in_dim(slot_rows, first_slot, group_size, 0)
        group_cols = lax.dynamic_slice_in_dim(slot_cols, first_slot, group_size, 0)
        live_mask = first_slot + jnp.arange(group_size) < live_count
        group_values = jnp.where(
            live_mask[:, None, None], group_values, jnp.zeros((), group_values.dtype)
        )
        picked = jnp.take(source, group_cols, axis=0)
        if wide_source:
            products = jnp.einsum(
                pattern,
                group_values.astype(jnp.float32),
                picked,
                precision=lax.Precision.HIGHEST,
                preferred_element_type=jnp.float32,
            )
        else:
            products = jnp.einsum(pattern, group_values, picked, preferred_element_type=jnp.float32)
        return running.at[group_rows].add(products)

    empty = jnp.zeros((out_tiles, tile_size, feature_width), jnp.float32)
    return lax.fori_loop(0, block_turns, add_group, empty)


def local(features, weight, cotangent, tile_values, tile_rows, tile_cols, tile_counts):
    row_count = lax.axis_size("row")
    col_count = lax.axis_size("col")
    node_rows = features.shape[0]
    out_width = weight.shape[1]
    tile_size = tile_values.shape[-1]
    slot_values = tile_values[0, 0]
    slot_rows = tile_rows[0, 0]
    slot_cols = tile_cols[0, 0]
    live_count = tile_counts[0, 0]
    weight_wide = weight.astype(jnp.float32)
    row_tiles = col_count * node_rows // tile_size
    mixed = jnp.dot(features, weight, preferred_element_type=jnp.float32)
    column_block = lax.all_gather(mixed, "row", axis=0, tiled=True)
    source_tiles = column_block.reshape(-1, tile_size, out_width)
    partial_value = tile_sums(
        slot_values, slot_rows, slot_cols, live_count, source_tiles, row_tiles, False
    )
    partial_value = partial_value.reshape(-1, partial_value.shape[-1])
    summed = lax.psum(partial_value, "col")
    own_rows = lax.dynamic_slice_in_dim(summed, lax.axis_index("col") * node_rows, node_rows, 0)
    full_cot = lax.all_gather(cotangent, "col", axis=0, tiled=True)
    grad_rows = (full_cot.astype(jnp.float32) * silu_slope(summed)).astype(jnp.bfloat16)
    output = jax.nn.silu(own_rows).astype(jnp.bfloat16)
    grad_tiles = grad_rows.reshape(-1, tile_size, out_width)
    col_tiles = row_count * node_rows // tile_size
    grad_cols = tile_sums(
        slot_values, slot_cols, slot_rows, live_count, grad_tiles, col_tiles, True
    ).reshape(-1, out_width)
    grad_mixed = lax.psum_scatter(grad_cols, "row", scatter_dimension=0, tiled=True)
    grad_in = jnp.dot(grad_mixed, weight_wide.T, precision=lax.Precision.HIGHEST)
    weight_term = jnp.dot(
        features.astype(jnp.float32).T, grad_mixed, precision=lax.Precision.HIGHEST
    )
    node_total = node_rows * row_count * col_count
    grad_weight = lax.psum(weight_term, ("row", "col")) * node_total ** (-0.5)
    return (output, grad_in.astype(jnp.bfloat16), grad_weight)


def solution(mesh):
    placed = (
        P(("row", "col"), None),
        P(),
        P(("row", "col"), None),
        P("row", "col", None, None, None),
        P("row", "col", None),
        P("row", "col", None),
        P("row", "col"),
    )
    return jax.shard_map(
        local,
        mesh=mesh,
        in_specs=placed,
        out_specs=(P(("row", "col"), None), P(("row", "col"), None), P()),
        check_vma=False,
    )
```

profile of v0, /device:TPU:1, one launch (start us, length us, event | category | flops | bytes accessed | tf_op | source)
XLA Modules:
  0.0 744.5 jit_solution(10563416301105799785)
XLA Ops:
  11.9 24.3 %all-gather.3.cloned.1.call-done = f32[1024,256]{1,0:T(8,128)} async-done(((f32[256,256]{1,0:T(8,128)}), f32[1024,256]{1,0:T(8,128)}) %all-gather.3.cloned.1.call-update) | async-done | bytes 1048592 | tf_op jit(solution)/shard_map/all_gather | solution.py:62
  36.2 4.4 broadcast_in_dim.58
  40.6 104.1 %while.20 = (s32[]{:T(128)}, f32[64,128,256]{2,1,0:T(8,128)}, s32[]{:T(128)}, s32[320]{0:T(512)S(1)}, s32[]{:T(128)}, /*index=5*/bf16[320,128,128]{2,1,0:T(8,128...) while((s32[]{:T(128)}, f32[64,128,256]{2,1,0:T(8,128)}, ...), condition=%wide.region_2.3_spmd, body=%wide.region_0.2_spmd.sunk | while | flops 1613235584 | bytes 30414008 | solution.py:46
  44.2 7.1 fusion.37
  51.2 10.3 %scatter_fusion = f32[64,128,256]{2,1,0:T(8,128)} fusion(f32[64,128,256]{2,1,0:T(8,128)} %get-tuple-element.265, s32[32]{0:T(128)S(1)} %compare_select_fusion.8, f32[32,128,256]{2,1,0:T(8,128)} %fusion.37), kind=kCustom, calls=%fused_computation.2.clone.1 | custom fusion | flops 1048576 | bytes 12583040 | tf_op jit(solution)/shard_map/while/body/scatter-add | solution.py:43
  65.1 7.1 fusion.37
  72.2 10.2 %scatter_fusion = f32[64,128,256]{2,1,0:T(8,128)} fusion(f32[64,128,256]{2,1,0:T(8,128)} %get-tuple-element.265, s32[32]{0:T(128)S(1)} %compare_select_fusion.8, f32[32,128,256]{2,1,0:T(8,128)} %fusion.37), kind=kCustom, calls=%fused_computation.2.clone.1 | custom fusion | flops 1048576 | bytes 12583040 | tf_op jit(solution)/shard_map/while/body/scatter-add | solution.py:43
  86.0 7.1 fusion.37
  93.1 10.0 %scatter_fusion = f32[64,128,256]{2,1,0:T(8,128)} fusion(f32[64,128,256]{2,1,0:T(8,128)} %get-tuple-element.265, s32[32]{0:T(128)S(1)} %compare_select_fusion.8, f32[32,128,256]{2,1,0:T(8,128)} %fusion.37), kind=kCustom, calls=%fused_computation.2.clone.1 | custom fusion | flops 1048576 | bytes 12583040 | tf_op jit(solution)/shard_map/while/body/scatter-add | solution.py:43
  106.6 7.1 fusion.37
  113.7 10.2 %scatter_fusion = f32[64,128,256]{2,1,0:T(8,128)} fusion(f32[64,128,256]{2,1,0:T(8,128)} %get-tuple-element.265, s32[32]{0:T(128)S(1)} %compare_select_fusion.8, f32[32,128,256]{2,1,0:T(8,128)} %fusion.37), kind=kCustom, calls=%fused_computation.2.clone.1 | custom fusion | flops 1048576 | bytes 12583040 | tf_op jit(solution)/shard_map/while/body/scatter-add | solution.py:43
  127.5 7.1 fusion.37
  134.5 10.1 %scatter_fusion = f32[64,128,256]{2,1,0:T(8,128)} fusion(f32[64,128,256]{2,1,0:T(8,128)} %get-tuple-element.265, s32[32]{0:T(128)S(1)} %compare_select_fusion.8, f32[32,128,256]{2,1,0:T(8,128)} %fusion.37), kind=kCustom, calls=%fused_computation.2.clone.1 | custom fusion | flops 1048576 | bytes 12583040 | tf_op jit(solution)/shard_map/while/body/scatter-add | solution.py:43
  145.5 14.4 %copy.10 = bf16[1,1,320,128,128]{3,4,2,1,0:T(8,128)(2,1)} copy(bf16[1,1,320,128,128]{4,3,2,1,0:T(8,128)(2,1)} %bitcast.21) | data formatting | bytes 20971520 | tf_op args[3]
  159.9 209.9 %all-reduce.3.cloned.1.call-done = f32[8192,256]{1,0:T(8,128)} async-done(((f32[8192,256]{1,0:T(8,128)}), f32[8192,256]{1,0:T(8,128)}) %all-reduce.3.cloned.1.call-update) | async-done | bytes 8388624 | tf_op jit(solution)/shard_map/psum | solution.py:68
  369.7 49.0 %all-gather.5.cloned.1.call-done = bf16[8192,256]{1,0:T(8,128)(2,1)} async-done(((bf16[256,256]{1,0:T(8,128)(2,1)}), bf16[8192,256]{1,0:T(8,128)(2,1)}) %all-gather.5.cloned.1.call-update) | async-done | bytes 4194320 | tf_op jit(solution)/shard_map/all_gather | solution.py:70
  418.7 7.6 %multiply_convert_fusion = bf16[8192,256]{1,0:T(8,128)(2,1)} fusion(f32[8192,256]{1,0:T(8,128)} %all-reduce.3.cloned.1.call-done, bf16[8192,256]{1,0:T(8,128)(2,1)} %all-gather.5.cloned.1.call-done), kind=kLoop, calls=%fused_computation.36 | loop fusion | flops 20971520 | bytes 16777216 | tf_op jit(solution)/shard_map/convert_element_type | solution.py:71
  426.4 71.0 %while.21 = (s32[]{:T(128)}, f32[8,128,256]{2,1,0:T(8,128)S(1)}, s32[]{:T(128)}, s32[320]{0:T(512)S(1)}, s32[]{:T(128)}, /*index=5*/bf16[320,128,128]{1,2,0:T(8,...) while((s32[]{:T(128)}, f32[8,128,256]{2,1,0:T(8,128)S(1)}, ...), condition=%wide.region_6.7_spmd, body=%wide.region_4.6_spmd.sunk | while | flops 271058272 | bytes 24122552 | solution.py:46
  427.2 2.9 gather_fusion.1
  430.1 4.0 fusion.40
  434.1 6.4 scatter_fusion.1
  441.4 2.9 gather_fusion.1
  444.3 4.0 fusion.40
  448.3 6.5 scatter_fusion.1
  458.5 4.0 fusion.40
  462.5 6.4 scatter_fusion.1
  472.7 4.0 fusion.40
  476.7 6.5 scatter_fusion.1
  486.9 4.0 fusion.40
  490.9 6.4 scatter_fusion.1
  500.1 89.2 %reduce-scatter.2.cloned.1.call-done = f32[256,256]{1,0:T(8,128)} async-done(((f32[1024,256]{1,0:T(8,128)}), f32[256,256]{1,0:T(8,128)}) %reduce-scatter.2.cloned.1.call-update) | async-done | bytes 262160 | tf_op jit(solution)/shard_map/reduce_scatter | solution.py:78
  593.2 143.1 %all-reduce.5.cloned.1.call-done = f32[128,256]{0,1:T(8,128)} async-done(((f32[128,256]{0,1:T(8,128)}), f32[128,256]{0,1:T(8,128)}) %all-reduce.5.cloned.1.call-update) | async-done | bytes 131088 | tf_op jit(solution)/shard_map/psum | solution.py:84
  (65 shorter events, 43.7 us)
Async XLA Ops:
  7.2 0.8 copy-start
  7.2 29.0 %all-gather.3.cloned.1.call-start = ((), (), s32[]{:S(2)}) async-start(), calls=%async_computation.1 | async-start | bytes 1310720 | tf_op jit(solution)/shard_map/all_gather | solution.py:62
  9.8 360.0 %all-reduce.3.cloned.1.call-start = ((), (), s32[]{:S(2)}) async-start(), calls=%async_computation.2 | async-start | bytes 16777216 | tf_op jit(solution)/shard_map/psum | solution.py:68
  36.2 4.4 copy-start.2
  144.7 274.0 %all-gather.5.cloned.1.call-start = ((), (), s32[]{:S(2)}) async-start(), calls=%async_computation.3 | async-start | bytes 4325376 | tf_op jit(solution)/shard_map/all_gather | solution.py:70
  145.4 443.9 %reduce-scatter.2.cloned.1.call-start = ((), (), s32[]{:S(2)}) async-start(), calls=%async_computation.4 | async-start | bytes 1310720 | tf_op jit(solution)/shard_map/reduce_scatter | solution.py:78
  426.4 165.0 %copy-start.3 = (bf16[128,256]{1,0:T(8,128)(2,1)S(1)}, bf16[128,256]{1,0:T(8,128)(2,1)}, u32[]{:S(2)}) copy-start(bf16[128,256]{1,0:T(8,128)(2,1)} %param.12) | copy-start | bytes 196612
  497.4 1.0 copy-start.1
  498.4 237.9 %all-reduce.5.cloned.1.call-start = ((), (), s32[]{:S(2)}) async-start(), calls=%async_computation.5 | async-start | bytes 262144 | tf_op jit(solution)/shard_map/psum | solution.py:84
Sparse Core Ops, SparseCore 0:
  9.9 26.2 all-gather.2
  144.8 224.8 all-reduce.2
  372.3 46.4 all-gather.4
  498.5 90.7 reduce-scatter.1
  594.5 141.7 all-reduce.4
where the time goes:
time: 747 us; the launch traced here: 745 us
  waiting for transfers between devices  516 us (69%)
  other arithmetic  103 us (14%)
  matrix products  61 us (8%)
  local copies, waits for them, and re-layouts  49.7 us (7%)
  between operations  14.5 us (2%)
    psum x1, waiting for transfers between devices, local(): summed = lax.psum(partial_value, 'col')  210 us
    psum x1, waiting for transfers between devices, local(): grad_weight = lax.psum(weight_term, ('row', 'col')) * node_total ** (-0.5)  143 us
    reduce_scatter x1, waiting for transfers between devices, local(): lax.psum_scatter(grad_cols, 'row', scatter_dimension=0, tiled=True)  89.2 us
    scatter-add x10, other arithmetic, add_group(): return running.at[group_rows].add(products)  83 us
    all_gather x1, waiting for transfers between devices, local(): full_cot = lax.all_gather(cotangent, 'col', axis=0, tiled=True)  49 us
    dot_general x5, matrix products, add_group(): jnp.einsum(pattern, group_values.astype(jnp.float32), picked, precision=l...  35.3 us
    gather x10, local copies, waits for them, and re-layouts, add_group(): picked = jnp.take(source, group_cols, axis=0)  28.3 us
    all_gather x1, waiting for transfers between devices, local(): column_block = lax.all_gather(mixed, 'row', axis=0, tiled=True)  24.3 us
  transfers between devices with their start and end apart: 5, of which 5 were waited for; matrix products, arithmetic and copies ran while one was open for 3% of the time, Pallas kernels for 0%

commit v1 on v0

v1 whole, which is shorter than its diff:
```python
import functools

import jax
import jax.numpy as jnp
from jax import lax
from jax.experimental import pallas as pl
from jax.experimental.pallas import tpu as pltpu
from jax.sharding import PartitionSpec as P

BF = jnp.bfloat16
F32 = jnp.float32
VM = pl.BlockSpec(memory_space=pltpu.VMEM)
SM = pl.BlockSpec(memory_space=pltpu.SMEM)
PARAMS = pltpu.CompilerParams(vmem_limit_bytes=24 << 20)

FWD_TILES = 4
BWD_UNROLL = 4


def sds(shape, dtype):
    return jax.ShapeDtypeStruct(shape, dtype)


def dot(a, b):
    return jnp.dot(a, b, preferred_element_type=F32)


def split(v):
    high = v.astype(BF)
    return high, (v - high.astype(F32)).astype(BF)


def joined(ref, at):
    return ref[at].astype(F32) + ref[at + 1].astype(F32)


def tile(values, slot):
    found = values[jnp.maximum(slot, 0)]
    return jnp.where(slot >= 0, found, jnp.zeros_like(found))


def forward_kernel(half, table, values, x0, x1, x2, x3, out):
    sources = (x0, x1, x2, x3)
    rows = FWD_TILES * 128

    @pl.loop(0, 32 // FWD_TILES)
    def _(step):
        total = None
        for k in range(4):
            left = []
            for r in range(FWD_TILES):
                base = (half * 32 + step * FWD_TILES + r) * 8 + 2 * k
                left.append(
                    jnp.concatenate(
                        [tile(values, table[base]), tile(values, table[base + 1])], axis=1
                    )
                )
            term = dot(jnp.concatenate(left, axis=0), sources[k][...])
            total = term if total is None else total + term
        out[pl.ds(pl.multiple_of(step * rows, rows), rows), :] = total.astype(out.dtype)


def forward_half(half, dtype, table, values, sources):
    return pl.pallas_call(
        functools.partial(forward_kernel, half),
        out_shape=sds((4096, 128), dtype),
        in_specs=[SM] + [VM] * 5,
        out_specs=VM,
        name=f"forward_{half}",
        cost_estimate=pl.CostEstimate(
            flops=2 * 4096 * 1024 * 128, bytes_accessed=6 << 20, transcendentals=0
        ),
        compiler_params=PARAMS,
    )(table, values, *sources)


def first_sum_kernel(own, got, mine, s1, s2, s3):
    for a, out in enumerate((mine, s1, s2, s3)):
        part = pl.ds(a * 1024, 1024)
        out[...] = (own[part, :] + got[part, :].astype(F32)).astype(out.dtype)


def first_sum(own, got):
    return pl.pallas_call(
        first_sum_kernel,
        out_shape=(sds((1024, 128), F32),) + (sds((1024, 128), BF),) * 3,
        in_specs=[VM] * 2,
        out_specs=(VM,) * 4,
        name="first_sum",
        compiler_params=PARAMS,
    )(own, got)


def second_sum_kernel(own, g1, g2, g3, mine, s1, s2, s3):
    for b, out in enumerate((mine, s1, s2, s3)):
        part = pl.ds(b * 256, 256)
        total = own[part, :] + g1[part, :].astype(F32)
        total = total + g2[part, :].astype(F32) + g3[part, :].astype(F32)
        out[...] = total.astype(out.dtype)


def second_sum(own, got):
    return pl.pallas_call(
        second_sum_kernel,
        out_shape=(sds((256, 128), F32),) + (sds((256, 128), BF),) * 3,
        in_specs=[VM] * 4,
        out_specs=(VM,) * 4,
        name="second_sum",
        compiler_params=PARAMS,
    )(own, *got)


def middle_kernel(own, g1, g2, g3, weight, cotangent, out, message):
    mixed = own[...] + g1[...].astype(F32) + g2[...].astype(F32) + g3[...].astype(F32)
    high, low = split(mixed)
    w = weight[...]
    summed = dot(high, w) + dot(low, w)
    gate = 1.0 / (1.0 + jnp.exp(-summed))
    out[...] = (summed * gate).astype(BF)
    slope = gate * (1.0 + summed * (1.0 - gate))
    grad = (cotangent[...].astype(F32) * slope).astype(BF)
    back = lax.dot_general(w, grad, (((1,), (1,)), ((), ())), preferred_element_type=F32)
    message[0] = back.astype(BF)
    over_rows = (((0,), (0,)), ((), ()))
    term = lax.dot_general(high, grad, over_rows, preferred_element_type=F32)
    term = term + lax.dot_general(low, grad, over_rows, preferred_element_type=F32)
    message[1], message[2] = split(term)


def middle(own, got, weight, cotangent):
    return pl.pallas_call(
        middle_kernel,
        out_shape=(sds((256, 256), BF), sds((3, 128, 256), BF)),
        in_specs=[VM] * 6,
        out_specs=(VM,) * 2,
        name="middle",
        compiler_params=PARAMS,
    )(own, *got, weight, cotangent)


def ring_sum(own, g1, g2, g3, at):
    return (joined(own, at) + joined(g2, at)) + (joined(g1, at) + joined(g3, at))


def gather_kernel(own, g1, g2, g3, message):
    for b, ref in enumerate((own, g1, g2, g3)):
        message[b] = ref[0]
    message[4], message[5] = split(ring_sum(own, g1, g2, g3, 1))


def gather_step(own, got):
    return pl.pallas_call(
        gather_kernel,
        out_shape=sds((6, 128, 256), BF),
        in_specs=[VM] * 4,
        out_specs=VM,
        name="gather_step",
        compiler_params=PARAMS,
    )(own, *got)


def backward_tiles(half, table, values, parts, emit):
    for q in range(4):
        total = jnp.zeros((128, 256), F32)
        for a, part in enumerate(parts):
            for b in range(4):
                base = (half * 32 + a * 8 + b * 2) * 8 + 2 * q
                upper = [tile(values, table[base]), tile(values, table[base + 1])]
                lower = [tile(values, table[base + 8]), tile(values, table[base + 9])]
                block = jnp.concatenate(
                    [jnp.concatenate(upper, axis=1), jnp.concatenate(lower, axis=1)], axis=0
                )
                total = total + dot(part[b], block)
        emit(q, total)


def backward_own_kernel(table, values, p0, p1, p2, p3, out, term):
    def emit(q, total):
        out[q] = total

    backward_tiles(1, table, values, (p0, p1, p2, p3), emit)
    term[...] = ring_sum(p0, p1, p2, p3, 4)


def backward_other_kernel(table, values, p0, p1, p2, p3, partial, term, own, own_term, s1, s2, s3):
    sends = (s1, s2, s3)

    def emit(q, total):
        total = total + partial[q]
        if q == 0:
            own[...] = total
        else:
            sends[q - 1][0] = total.astype(BF)

    backward_tiles(0, table, values, (p0, p1, p2, p3), emit)
    high, low = split(term[...] + ring_sum(p0, p1, p2, p3, 4))
    own_term[0] = high
    own_term[1] = low
    for out in sends:
        out[1] = high
        out[2] = low


BACK_COST = pl.CostEstimate(
    flops=2 * 4096 * 1024 * 128, bytes_accessed=6 << 20, transcendentals=0
)


def backward_own(table, values, parts):
    return pl.pallas_call(
        backward_own_kernel,
        out_shape=(sds((4, 128, 256), F32), sds((128, 256), F32)),
        in_specs=[SM] + [VM] * 5,
        out_specs=(VM,) * 2,
        name="backward_own",
        cost_estimate=BACK_COST,
        compiler_params=PARAMS,
    )(table, values, *parts)


def backward_other(table, values, parts, partial, term):
    return pl.pallas_call(
        backward_other_kernel,
        out_shape=(sds((128, 256), F32), sds((2, 128, 256), BF)) + (sds((3, 128, 256), BF),) * 3,
        in_specs=[SM] + [VM] * 7,
        out_specs=(VM,) * 5,
        name="backward_other",
        cost_estimate=BACK_COST,
        compiler_params=PARAMS,
    )(table, values, *parts, partial, term)


def finish_kernel(scale, own, own_term, g1, g2, g3, grad_in, grad_weight):
    total = own[...] + g1[0].astype(F32) + g2[0].astype(F32) + g3[0].astype(F32)
    grad_in[...] = total.T.astype(BF)
    term = (joined(own_term, 0) + joined(g2, 1)) + (joined(g1, 1) + joined(g3, 1))
    grad_weight[...] = term * scale


def finish(scale, own, own_term, got):
    return pl.pallas_call(
        functools.partial(finish_kernel, scale),
        out_shape=(sds((256, 128), BF), sds((128, 256), F32)),
        in_specs=[VM] * 5,
        out_specs=(VM,) * 2,
        name="finish",
        compiler_params=PARAMS,
    )(own, own_term, *got)


def row_shift(value, k):
    return lax.ppermute(value, "row", [(i, (i + k) % 4) for i in range(4)])


def swap_cores(value):
    return lax.ppermute(value, "col", [(j, j ^ 1) for j in range(32)])


def chip_shift(value, k, x_core):
    pairs = []
    for z in range(4):
        for x in range(4):
            for core in range(2):
                if core == x_core:
                    to = (z, (x + k) % 4)
                else:
                    to = ((z + k) % 4, x)
                pairs.append(((z * 4 + x) * 2 + core, (to[0] * 4 + to[1]) * 2 + core))
    return lax.ppermute(value, "col", pairs)


def slot_table(slot_rows, slot_cols, live_count):
    row, col = lax.axis_index("row"), lax.axis_index("col")
    core, x, z = col & 1, (col >> 1) & 3, col >> 3
    block = slot_rows >> 1
    parity = block & 1
    dx = (((block >> 1) & 3) - x) & 3
    dz = ((block >> 3) - z) & 3
    even = parity == 0
    a = jnp.where(even, dx, dz)
    b = jnp.where(even, dz, dx)
    half = (parity == core).astype(jnp.int32)
    place = half * 32 + a * 8 + b * 2 + (slot_rows & 1)
    source = ((row - (slot_cols >> 1)) & 3) * 2 + (slot_cols & 1)
    slots = jnp.arange(slot_rows.shape[0], dtype=jnp.int32)
    key = jnp.where(slots < live_count, place * 8 + source, -1)
    hits = key[:, None] == jnp.arange(512, dtype=jnp.int32)[None, :]
    return jnp.max(jnp.where(hits, slots[:, None], -1), axis=0)


def local(features, weight, cotangent, tile_values, tile_rows, tile_cols, tile_counts):
    values = tile_values[0, 0]
    table = slot_table(tile_rows[0, 0], tile_cols[0, 0], tile_counts[0, 0])
    sources = [features] + [row_shift(features, k) for k in (1, 2, 3)]
    other = swap_cores(forward_half(0, BF, table, values, sources))
    kept = forward_half(1, F32, table, values, sources)
    own, *sends = first_sum(kept, other)
    got = [chip_shift(v, k, 0) for k, v in zip((1, 2, 3), sends)]
    own, *sends = second_sum(own, got)
    got = [chip_shift(v, k, 1) for k, v in zip((1, 2, 3), sends)]
    output, message = middle(own, got, weight, cotangent)
    got = [chip_shift(message, -k, 1) for k in (1, 2, 3)]
    message = gather_step(message, got)
    mine = [message] + [chip_shift(message, -k, 0) for k in (1, 2, 3)]
    others = [swap_cores(v) for v in mine]
    partial, term = backward_own(table, values, mine)
    own, own_term, *sends = backward_other(table, values, others, partial, term)
    got = [row_shift(v, -k) for k, v in zip((1, 2, 3), sends)]
    grad_in, grad_weight = finish(32768.0 ** -0.5, own, own_term, got)
    return output, grad_in, grad_weight


def solution(mesh):
    placed = (
        P(("row", "col"), None),
        P(),
        P(("row", "col"), None),
        P("row", "col", None, None, None),
        P("row", "col", None),
        P("row", "col", None),
        P("row", "col"),
    )
    return jax.shard_map(
        local,
        mesh=mesh,
        in_specs=placed,
        out_specs=(P(("row", "col"), None), P(("row", "col"), None), P()),
        check_vma=False,
    )
```

time: 747 us -> 90.7 us (0.12)
  waiting for transfers between devices: 516 us -> 27.3 us
  other arithmetic: 103 us -> 0.9 us
  matrix products: 61 us -> 0 us
  local copies, waits for them, and re-layouts: 49.7 us -> 4.85 us
  starting transfers between devices: 0.2 us -> 40.6 us
  Pallas kernels: 0 us -> 15.3 us
  between operations: 14.5 us -> 1.43 us
    psum x2 -> x0, waiting for transfers between devices: 353 us -> none  [the longest x1 210 us: local(): summed = lax.psum(partial_value, 'col')]
    reduce_scatter x1 -> x0, waiting for transfers between devices: 89.2 us -> none  [local(): lax.psum_scatter(grad_cols, 'row', scatter_dimension=0, tiled=True)]
    scatter-add x10 -> x0, other arithmetic: 83 us -> none  [add_group(): return running.at[group_rows].add(products)]
    all_gather x2 -> x0, waiting for transfers between devices: 73.3 us -> none  [the longest x1 49 us: local(): full_cot = lax.all_gather(cotangent, 'col', axis=0, tiled=True)]
    dot_general x13 -> x0, matrix products: 61 us -> none  [the longest x5 35.3 us: add_group(): jnp.einsum(pattern, group_values.astype(jnp.float32), picked, precision=l...]
    ppermute x0 -> x23, starting transfers between devices: none -> 40.6 us  [the longest x12 18.4 us: chip_shift(): return lax.ppermute(value, 'col', pairs)]
    gather x10 -> x0, local copies, waits for them, and re-layouts: 28.3 us -> none  [add_group(): picked = jnp.take(source, group_cols, axis=0)]
    ppermute x0 -> x23, waiting for transfers between devices: none -> 27.3 us  [the longest x6 13.8 us: row_shift(): return lax.ppermute(value, 'row', [(i, (i + k) % 4) for i in range(4)])]
  transfers between devices with their start and end apart: 5 -> 23, of which waited for: 5 -> 12; matrix products, arithmetic and copies ran while one was open for 3% -> 1% of each run, Pallas kernels for 0% -> 7%
where the time goes in v1:
time: 90.7 us; the launch traced here: 90.4 us
  starting transfers between devices  40.6 us (45%)
  waiting for transfers between devices  27.3 us (30%)
  Pallas kernels  15.3 us (17%)
  local copies, waits for them, and re-layouts  4.85 us (5%)
  between operations  1.43 us (2%)
    ppermute x12, starting transfers between devices, chip_shift(): return lax.ppermute(value, 'col', pairs)  18.4 us
    ppermute x5, starting transfers between devices, swap_cores(): return lax.ppermute(value, 'col', [(j, j ^ 1) for j in range(32)])  15.6 us
    ppermute x6, waiting for transfers between devices, row_shift(): return lax.ppermute(value, 'row', [(i, (i + k) % 4) for i in range(4)])  13.8 us
    ppermute x12, waiting for transfers between devices, chip_shift(): return lax.ppermute(value, 'col', pairs)  13.5 us
    pallas_call x2, Pallas kernels, forward_half(): pl.pallas_call(functools.partial(forward_kernel, half), out_shape=sds((40...  8.33 us
    ppermute x6, starting transfers between devices, row_shift(): return lax.ppermute(value, 'row', [(i, (i + k) % 4) for i in range(4)])  6.62 us
    unnamed x14, local copies, waits for them, and re-layouts  4.85 us
    pallas_call x1, Pallas kernels, backward_other(): pl.pallas_call(backward_other_kernel, out_shape=(sds((128, 256), F32), sd...  2.44 us
  transfers between devices with their start and end apart: 23, of which 12 were waited for; matrix products, arithmetic and copies ran while one was open for 1% of the time, Pallas kernels for 7%

profile of v1, /device:TPU:1, one launch (start us, length us, event | category | flops | bytes accessed | tf_op | source)
XLA Modules:
  0.0 90.4 jit_solution(10473130758338419545)
XLA Ops:
  0.6 3.6 %collective-permute-start.2 = (bf16[256,128]{1,0:T(8,128)(2,1)}, bf16[256,128]{1,0:T(8,128)(2,1)S(1)}, u32[]{:S(2)}, u32[]{:S(2)}) collective-permute-start(bf16[256,128]{1,0:T(8,128)(2,1)} %x0.3), channel_id=1, source_target_pairs={{0,96},{32,0},{64,32},{96,64},{1,97},{33,1},{65,33},{97,65},{2,98}... | collective-permute-start | bytes 196616 | tf_op jit(solution)/shard_map/ppermute | solution.py:252
  6.9 2.3 %collective-permute-done.1.x2 = bf16[256,128]{1,0:T(8,128)(2,1)S(1)} collective-permute-done((bf16[256,128]{1,0:T(8,128)(2,1)}, bf16[256,128]{1,0:T(8,128)(2,1)S(1)}, u32[]{:S(2)}, u32[]{:S(2)}) %collective-permute-start.1) | collective-permute-done | bytes 65568 | tf_op jit(solution)/shard_map/ppermute | solution.py:252
  9.8 4.0 %copy-done = bf16[1,1,320,128,128]{4,3,2,1,0:T(8,128)(2,1)S(1)} copy-done((bf16[1,1,320,128,128]{4,3,2,1,0:T(8,128)(2,1)S(1)}, bf16[1,1,320,128,128]{4,3,2,1,0:T(8,128)(2,1)}, u32[]{:S(2)}) %copy-start) | copy-done | bytes 10485784
  13.8 0.8 copy-done.1
  14.6 4.2 %forward_0.1 = bf16[4096,128]{1,0:T(8,128)(2,1)S(1)} custom-call(s32[512]{0:T(512)S(1)} %select_reduce_fusion.table, bf16[320,128,128]{2,1,0:T(8,128)(2,1)S(1)} %bitcast.3, bf16[256,128]{1,0:T(8,128)(2,1)S(1)} %copy-done.1, bf16[256,128]{1,0:T(8,128)(2,1)S(1)} %collective-permute-done.x1, bf16[256,128]{1,0:T(8,128)(2,1)S(1)} %collective-permute-done.1.x2, ...), custom_call_target="tpu_custom_call" | custom-call | flops 1073741824 | bytes 6291456 | tf_op jit(solution)/shard_map/forward_0/pallas_call | solution.py:64
  18.9 2.2 %collective-permute-start.3 = (bf16[4096,128]{1,0:T(8,128)(2,1)S(1)}, bf16[4096,128]{1,0:T(8,128)(2,1)S(1)}, u32[]{:S(2)}, u32[]{:S(2)}) collective-permute-start(bf16[4096,128]{1,0:T(8,128)(2,1)S(1)} %forward_0.1), channel_id=1, source_target_pairs={{0,1},{1,0},{2,3},{3,2},{4,5},{5,4},{6,7},{7,6},{8,9},{9,8},{10,11... | collective-permute-start | bytes 3145736 | tf_op jit(solution)/shard_map/ppermute | solution.py:256
  21.0 4.1 %forward_1.1.own = f32[4096,128]{1,0:T(8,128)S(1)} custom-call(s32[512]{0:T(512)S(1)} %select_reduce_fusion.table, bf16[320,128,128]{2,1,0:T(8,128)(2,1)S(1)} %bitcast.4, bf16[256,128]{1,0:T(8,128)(2,1)S(1)} %copy-done.1, bf16[256,128]{1,0:T(8,128)(2,1)S(1)} %collective-permute-done.x1, bf16[256,128]{1,0:T(8,128)(2,1)S(1)} %collective-permute-done.1.x2, ...), custom_call_target="tpu_custom_call" | custom-call | flops 1073741824 | bytes 6291456 | tf_op jit(solution)/shard_map/forward_1/pallas_call | solution.py:64
  25.3 1.7 %collective-permute-start.4 = (bf16[1024,128]{1,0:T(8,128)(2,1)S(1)}, bf16[1024,128]{1,0:T(8,128)(2,1)S(1)}, u32[]{:S(2)}, u32[]{:S(2)}) collective-permute-start(bf16[1024,128]{1,0:T(8,128)(2,1)S(1)} %get-tuple-element.23), channel_id=1, source_target_pairs={{0,2},{1,9},{2,4},{3,11},{4,6},{5,13},{6,0},{7,15},{8,10},{9,17},{... | collective-permute-start | bytes 786440 | tf_op jit(solution)/shard_map/ppermute | solution.py:269
  27.0 3.3 %collective-permute-start.5 = (bf16[1024,128]{1,0:T(8,128)(2,1)S(1)}, bf16[1024,128]{1,0:T(8,128)(2,1)S(1)}, u32[]{:S(2)}, u32[]{:S(2)}) collective-permute-start(bf16[1024,128]{1,0:T(8,128)(2,1)S(1)} %get-tuple-element.24), channel_id=1, source_target_pairs={{0,4},{1,17},{2,6},{3,19},{4,0},{5,21},{6,2},{7,23},{8,12},{9,25},... | collective-permute-start | bytes 786440 | tf_op jit(solution)/shard_map/ppermute | solution.py:269
  30.3 0.8 collective-permute-start.6
  31.1 1.8 %collective-permute-done.4.g1 = bf16[1024,128]{1,0:T(8,128)(2,1)S(1)} collective-permute-done((bf16[1024,128]{1,0:T(8,128)(2,1)S(1)}, bf16[1024,128]{1,0:T(8,128)(2,1)S(1)}, u32[]{:S(2)}, u32[]{:S(2)}) %collective-permute-start.4) | collective-permute-done | bytes 262176 | tf_op jit(solution)/shard_map/ppermute | solution.py:269
  32.9 4.0 %collective-permute-done.5.g2 = bf16[1024,128]{1,0:T(8,128)(2,1)S(1)} collective-permute-done((bf16[1024,128]{1,0:T(8,128)(2,1)S(1)}, bf16[1024,128]{1,0:T(8,128)(2,1)S(1)}, u32[]{:S(2)}, u32[]{:S(2)}) %collective-permute-start.5) | collective-permute-done | bytes 262176 | tf_op jit(solution)/shard_map/ppermute | solution.py:269
  37.0 1.3 %collective-permute-start.7 = (bf16[256,128]{1,0:T(8,128)(2,1)S(1)}, bf16[256,128]{1,0:T(8,128)(2,1)S(1)}, u32[]{:S(2)}, u32[]{:S(2)}) collective-permute-start(bf16[256,128]{1,0:T(8,128)(2,1)S(1)} %get-tuple-element.27), channel_id=1, source_target_pairs={{0,8},{1,3},{2,10},{3,5},{4,12},{5,7},{6,14},{7,1},{8,16},{9,11},{... | collective-permute-start | bytes 196616 | tf_op jit(solution)/shard_map/ppermute | solution.py:269
  38.3 2.5 %collective-permute-start.8 = (bf16[256,128]{1,0:T(8,128)(2,1)S(1)}, bf16[256,128]{1,0:T(8,128)(2,1)S(1)}, u32[]{:S(2)}, u32[]{:S(2)}) collective-permute-start(bf16[256,128]{1,0:T(8,128)(2,1)S(1)} %get-tuple-element.28), channel_id=1, source_target_pairs={{0,16},{1,5},{2,18},{3,7},{4,20},{5,1},{6,22},{7,3},{8,24},{9,13},... | collective-permute-start | bytes 196616 | tf_op jit(solution)/shard_map/ppermute | solution.py:269
  40.8 1.2 %collective-permute-start.9 = (bf16[256,128]{1,0:T(8,128)(2,1)S(1)}, bf16[256,128]{1,0:T(8,128)(2,1)S(1)}, u32[]{:S(2)}, u32[]{:S(2)}) collective-permute-start(bf16[256,128]{1,0:T(8,128)(2,1)S(1)} %get-tuple-element.29), channel_id=1, source_target_pairs={{0,24},{1,7},{2,26},{3,1},{4,28},{5,3},{6,30},{7,5},{8,0},{9,15},{... | collective-permute-start | bytes 196616 | tf_op jit(solution)/shard_map/ppermute | solution.py:269
  42.0 1.2 %collective-permute-done.8.g2 = bf16[256,128]{1,0:T(8,128)(2,1)S(1)} collective-permute-done((bf16[256,128]{1,0:T(8,128)(2,1)S(1)}, bf16[256,128]{1,0:T(8,128)(2,1)S(1)}, u32[]{:S(2)}, u32[]{:S(2)}) %collective-permute-start.8) | collective-permute-done | bytes 65568 | tf_op jit(solution)/shard_map/ppermute | solution.py:269
  43.2 1.1 %collective-permute-done.9.g3 = bf16[256,128]{1,0:T(8,128)(2,1)S(1)} collective-permute-done((bf16[256,128]{1,0:T(8,128)(2,1)S(1)}, bf16[256,128]{1,0:T(8,128)(2,1)S(1)}, u32[]{:S(2)}, u32[]{:S(2)}) %collective-permute-start.9) | collective-permute-done | bytes 65568 | tf_op jit(solution)/shard_map/ppermute | solution.py:269
  44.2 1.0 %middle.1 = (bf16[256,256]{1,0:T(8,128)(2,1)}, bf16[3,128,256]{2,1,0:T(8,128)(2,1)S(1)}) custom-call(f32[256,128]{1,0:T(8,128)S(1)} %get-tuple-element.26.own, bf16[256,128]{1,0:T(8,128)(2,1)S(1)} %collective-permute-done.7.g1, bf16[256,128]{1,0:T(8,128)(2,1)S(1)} %collective-permute-done.8.g2, bf16[256,128]{1,0:T(8,128)(2,1)S(1)} %collective-permute-done.9.g3, ...), custom_call_target="tpu_custom_call" | custom-call | tf_op jit(solution)/shard_map/middle/pallas_call | solution.py:131
  45.5 3.3 %collective-permute-start.11 = (bf16[3,128,256]{2,1,0:T(8,128)(2,1)S(1)}, bf16[3,128,256]{2,1,0:T(8,128)(2,1)S(1)}, u32[]{:S(2)}, u32[]{:S(2)}) collective-permute-start(bf16[3,128,256]{2,1,0:T(8,128)(2,1)S(1)} %get-tuple-element.31.own), channel_id=1, source_target_pairs={{0,16},{1,5},{2,18},{3,7},{4,20},{5,1},{6,22},{7,3},{8,24},{9,13},... | collective-permute-start | bytes 589832 | tf_op jit(solution)/shard_map/ppermute | solution.py:269
  48.8 2.2 %collective-permute-done.12.g3 = bf16[3,128,256]{2,1,0:T(8,128)(2,1)S(1)} collective-permute-done((bf16[3,128,256]{2,1,0:T(8,128)(2,1)S(1)}, bf16[3,128,256]{2,1,0:T(8,128)(2,1)S(1)}, u32[]{:S(2)}, u32[]{:S(2)}) %collective-permute-start.12) | collective-permute-done | bytes 196640 | tf_op jit(solution)/shard_map/ppermute | solution.py:269
  50.9 3.0 %collective-permute-done.11.g2 = bf16[3,128,256]{2,1,0:T(8,128)(2,1)S(1)} collective-permute-done((bf16[3,128,256]{2,1,0:T(8,128)(2,1)S(1)}, bf16[3,128,256]{2,1,0:T(8,128)(2,1)S(1)}, u32[]{:S(2)}, u32[]{:S(2)}) %collective-permute-start.11) | collective-permute-done | bytes 196640 | tf_op jit(solution)/shard_map/ppermute | solution.py:269
  54.0 1.0 %collective-permute-start.18 = (bf16[6,128,256]{2,1,0:T(8,128)(2,1)S(1)}, bf16[6,128,256]{2,1,0:T(8,128)(2,1)S(1)}, u32[]{:S(2)}, u32[]{:S(2)}) collective-permute-start(bf16[6,128,256]{2,1,0:T(8,128)(2,1)S(1)} %gather_step.1.p0), channel_id=1, source_target_pairs={{0,2},{1,9},{2,4},{3,11},{4,6},{5,13},{6,0},{7,15},{8,10},{9,17},{... | collective-permute-start | bytes 1179656 | tf_op jit(solution)/shard_map/ppermute | solution.py:269
  55.1 2.4 %collective-permute-start.16 = (bf16[6,128,256]{2,1,0:T(8,128)(2,1)S(1)}, bf16[6,128,256]{2,1,0:T(8,128)(2,1)S(1)}, u32[]{:S(2)}, u32[]{:S(2)}) collective-permute-start(bf16[6,128,256]{2,1,0:T(8,128)(2,1)S(1)} %gather_step.1.p0), channel_id=1, source_target_pairs={{0,4},{1,17},{2,6},{3,19},{4,0},{5,21},{6,2},{7,23},{8,12},{9,25},... | collective-permute-start | bytes 1179656 | tf_op jit(solution)/shard_map/ppermute | solution.py:269
  58.1 5.2 %collective-permute-start.13 = (bf16[6,128,256]{2,1,0:T(8,128)(2,1)S(1)}, bf16[6,128,256]{2,1,0:T(8,128)(2,1)S(1)}, u32[]{:S(2)}, u32[]{:S(2)}) collective-permute-start(bf16[6,128,256]{2,1,0:T(8,128)(2,1)S(1)} %gather_step.1.p0), channel_id=1, source_target_pairs={{0,1},{1,0},{2,3},{3,2},{4,5},{5,4},{6,7},{7,6},{8,9},{9,8},{10,11... | collective-permute-start | bytes 1179656 | tf_op jit(solution)/shard_map/ppermute | solution.py:256
  63.3 3.4 %collective-permute-start.19 = (bf16[6,128,256]{2,1,0:T(8,128)(2,1)S(1)}, bf16[6,128,256]{2,1,0:T(8,128)(2,1)S(1)}, u32[]{:S(2)}, u32[]{:S(2)}) collective-permute-start(bf16[6,128,256]{2,1,0:T(8,128)(2,1)S(1)} %collective-permute-done.18.p3), channel_id=1, source_target_pairs={{0,1},{1,0},{2,3},{3,2},{4,5},{5,4},{6,7},{7,6},{8,9},{9,8},{10,11... | collective-permute-start | bytes 1179656 | tf_op jit(solution)/shard_map/ppermute | solution.py:256
  67.1 4.6 %collective-permute-start.17 = (bf16[6,128,256]{2,1,0:T(8,128)(2,1)S(1)}, bf16[6,128,256]{2,1,0:T(8,128)(2,1)S(1)}, u32[]{:S(2)}, u32[]{:S(2)}) collective-permute-start(bf16[6,128,256]{2,1,0:T(8,128)(2,1)S(1)} %collective-permute-done.16.p2), channel_id=1, source_target_pairs={{0,1},{1,0},{2,3},{3,2},{4,5},{5,4},{6,7},{7,6},{8,9},{9,8},{10,11... | collective-permute-start | bytes 1179656 | tf_op jit(solution)/shard_map/ppermute | solution.py:256
  71.9 2.4 %backward_own.1 = (f32[4,128,256]{2,1,0:T(8,128)S(1)}, f32[128,256]{1,0:T(8,128)S(1)}) custom-call(s32[512]{0:T(512)S(1)} %select_reduce_fusion.table, bf16[320,128,128]{2,1,0:T(8,128)(2,1)S(1)} %bitcast.7, bf16[6,128,256]{2,1,0:T(8,128)(2,1)S(1)} %gather_step.1.p0, bf16[6,128,256]{2,1,0:T(8,128)(2,1)S(1)} %collective-permute-done.14.p1, ...), custom_call_target="tpu_custom_call" | custom-call | flops 1073741824 | bytes 6291456 | tf_op jit(solution)/shard_map/backward_own/pallas_call | solution.py:210
  74.3 2.4 %backward_other.1 = (f32[128,256]{1,0:T(8,128)S(1)}, bf16[2,128,256]{2,1,0:T(8,128)(2,1)S(1)}, bf16[3,128,256]{2,1,0:T(8,128)(2,1)S(1)}, bf16[3,128,256]{2,1,0:T(8,128)(2,1)S(1)}, bf16[3,128,256]{2,1,0:T(8,128)(2,1)S(1)}) custom-call(s32[512]{0:T(512)S(1)} %select_reduce_fusion.table, bf16[320,128,128]{2,1,0:T(8,128)(2,1)S(1)} %bitcast.8, ...), custom_call_target="tpu_custom_call" | custom-call | flops 1073741824 | bytes 6291456 | tf_op jit(solution)/shard_map/backward_other/pallas_call | solution.py:222
  77.1 0.9 collective-permute-start.21
  78.7 4.3 %collective-permute-done.20.g1 = bf16[3,128,256]{2,1,0:T(8,128)(2,1)S(1)} collective-permute-done((bf16[3,128,256]{2,1,0:T(8,128)(2,1)S(1)}, bf16[3,128,256]{2,1,0:T(8,128)(2,1)S(1)}, u32[]{:S(2)}, u32[]{:S(2)}) %collective-permute-start.20) | collective-permute-done | bytes 196640 | tf_op jit(solution)/shard_map/ppermute | solution.py:252
  83.0 1.4 %collective-permute-done.21.g2 = bf16[3,128,256]{2,1,0:T(8,128)(2,1)S(1)} collective-permute-done((bf16[3,128,256]{2,1,0:T(8,128)(2,1)S(1)}, bf16[3,128,256]{2,1,0:T(8,128)(2,1)S(1)}, u32[]{:S(2)}, u32[]{:S(2)}) %collective-permute-start.21) | collective-permute-done | bytes 196640 | tf_op jit(solution)/shard_map/ppermute | solution.py:252
  84.4 5.2 %collective-permute-done.22.g3 = bf16[3,128,256]{2,1,0:T(8,128)(2,1)S(1)} collective-permute-done((bf16[3,128,256]{2,1,0:T(8,128)(2,1)S(1)}, bf16[3,128,256]{2,1,0:T(8,128)(2,1)S(1)}, u32[]{:S(2)}, u32[]{:S(2)}) %collective-permute-start.22) | collective-permute-done | bytes 196640 | tf_op jit(solution)/shard_map/ppermute | solution.py:252
  (41 shorter events, 6.4 us)
Async XLA Ops:
  0.6 6.2 %collective-permute-start.2 = (bf16[256,128]{1,0:T(8,128)(2,1)}, bf16[256,128]{1,0:T(8,128)(2,1)S(1)}, u32[]{:S(2)}, u32[]{:S(2)}) collective-permute-start(bf16[256,128]{1,0:T(8,128)(2,1)} %x0.3), channel_id=1, source_target_pairs={{0,96},{32,0},{64,32},{96,64},{1,97},{33,1},{65,33},{97,65},{2,98}... | collective-permute-start | bytes 196616 | tf_op jit(solution)/shard_map/ppermute | solution.py:252
  4.3 4.9 %collective-permute-start.1 = (bf16[256,128]{1,0:T(8,128)(2,1)}, bf16[256,128]{1,0:T(8,128)(2,1)S(1)}, u32[]{:S(2)}, u32[]{:S(2)}) collective-permute-start(bf16[256,128]{1,0:T(8,128)(2,1)} %x0.3), channel_id=1, source_target_pairs={{0,64},{32,96},{64,0},{96,32},{1,65},{33,97},{65,1},{97,33},{2,66}... | collective-permute-start | bytes 196616 | tf_op jit(solution)/shard_map/ppermute | solution.py:252
  4.6 5.2 %collective-permute-start = (bf16[256,128]{1,0:T(8,128)(2,1)}, bf16[256,128]{1,0:T(8,128)(2,1)S(1)}, u32[]{:S(2)}, u32[]{:S(2)}) collective-permute-start(bf16[256,128]{1,0:T(8,128)(2,1)} %x0.3), channel_id=1, source_target_pairs={{0,32},{32,64},{64,96},{96,0},{1,33},{33,65},{65,97},{97,1},{2,34}... | collective-permute-start | bytes 196616 | tf_op jit(solution)/shard_map/ppermute | solution.py:252
  9.8 4.0 %copy-start = (bf16[1,1,320,128,128]{4,3,2,1,0:T(8,128)(2,1)S(1)}, bf16[1,1,320,128,128]{4,3,2,1,0:T(8,128)(2,1)}, u32[]{:S(2)}) copy-start(bf16[1,1,320,128,128]{4,3,2,1,0:T(8,128)(2,1)} %param.10) | copy-start | bytes 31457284
  13.8 0.8 copy-start.1
  14.6 57.3 %slice-start = ((s8[10485760]{0:T(1024)(128)(4,1)}), s8[4194304]{0:T(1024)(128)(4,1)S(1)}, s32[]{:S(2)}) async-start(s8[10485760]{0:T(1024)(128)(4,1)} %bitcast.5), calls=%async_computation | async-start | bytes 8388608
  14.6 57.3 %slice-start.1 = ((s8[10485760]{0:T(1024)(128)(4,1)}), s8[4194304]{0:T(1024)(128)(4,1)S(1)}, s32[]{:S(2)}) async-start(s8[10485760]{0:T(1024)(128)(4,1)} %bitcast.5), calls=%async_computation.1 | async-start | bytes 8388608
  18.8 25.4 %copy-start.2 = (bf16[256,256]{1,0:T(8,128)(2,1)S(1)}, bf16[256,256]{1,0:T(8,128)(2,1)}, u32[]{:S(2)}) copy-start(bf16[256,256]{1,0:T(8,128)(2,1)} %cotangent.1) | copy-start | bytes 393220
  18.8 25.4 %copy-start.3 = (bf16[128,256]{1,0:T(8,128)(2,1)S(1)}, bf16[128,256]{1,0:T(8,128)(2,1)}, u32[]{:S(2)}) copy-start(bf16[128,256]{1,0:T(8,128)(2,1)} %weight.1) | copy-start | bytes 196612
  18.8 53.1 %slice-start.2 = ((s8[10485760]{0:T(1024)(128)(4,1)}), s8[2097152]{0:T(1024)(128)(4,1)S(1)}, s32[]{:S(2)}) async-start(s8[10485760]{0:T(1024)(128)(4,1)} %bitcast.5), calls=%async_computation.2 | async-start | bytes 4194304
  18.9 6.3 %collective-permute-start.3 = (bf16[4096,128]{1,0:T(8,128)(2,1)S(1)}, bf16[4096,128]{1,0:T(8,128)(2,1)S(1)}, u32[]{:S(2)}, u32[]{:S(2)}) collective-permute-start(bf16[4096,128]{1,0:T(8,128)(2,1)S(1)} %forward_0.1), channel_id=1, source_target_pairs={{0,1},{1,0},{2,3},{3,2},{4,5},{5,4},{6,7},{7,6},{8,9},{9,8},{10,11... | collective-permute-start | bytes 3145736 | tf_op jit(solution)/shard_map/ppermute | solution.py:256
  25.3 7.6 %collective-permute-start.4 = (bf16[1024,128]{1,0:T(8,128)(2,1)S(1)}, bf16[1024,128]{1,0:T(8,128)(2,1)S(1)}, u32[]{:S(2)}, u32[]{:S(2)}) collective-permute-start(bf16[1024,128]{1,0:T(8,128)(2,1)S(1)} %get-tuple-element.23), channel_id=1, source_target_pairs={{0,2},{1,9},{2,4},{3,11},{4,6},{5,13},{6,0},{7,15},{8,10},{9,17},{... | collective-permute-start | bytes 786440 | tf_op jit(solution)/shard_map/ppermute | solution.py:269
  27.0 9.9 %collective-permute-start.5 = (bf16[1024,128]{1,0:T(8,128)(2,1)S(1)}, bf16[1024,128]{1,0:T(8,128)(2,1)S(1)}, u32[]{:S(2)}, u32[]{:S(2)}) collective-permute-start(bf16[1024,128]{1,0:T(8,128)(2,1)S(1)} %get-tuple-element.24), channel_id=1, source_target_pairs={{0,4},{1,17},{2,6},{3,19},{4,0},{5,21},{6,2},{7,23},{8,12},{9,25},... | collective-permute-start | bytes 786440 | tf_op jit(solution)/shard_map/ppermute | solution.py:269
  30.3 6.6 %collective-permute-start.6 = (bf16[1024,128]{1,0:T(8,128)(2,1)S(1)}, bf16[1024,128]{1,0:T(8,128)(2,1)S(1)}, u32[]{:S(2)}, u32[]{:S(2)}) collective-permute-start(bf16[1024,128]{1,0:T(8,128)(2,1)S(1)} %get-tuple-element.25), channel_id=1, source_target_pairs={{0,6},{1,25},{2,0},{3,27},{4,2},{5,29},{6,4},{7,31},{8,14},{9,1},{... | collective-permute-start | bytes 786440 | tf_op jit(solution)/shard_map/ppermute | solution.py:269
  37.0 5.0 %collective-permute-start.7 = (bf16[256,128]{1,0:T(8,128)(2,1)S(1)}, bf16[256,128]{1,0:T(8,128)(2,1)S(1)}, u32[]{:S(2)}, u32[]{:S(2)}) collective-permute-start(bf16[256,128]{1,0:T(8,128)(2,1)S(1)} %get-tuple-element.27), channel_id=1, source_target_pairs={{0,8},{1,3},{2,10},{3,5},{4,12},{5,7},{6,14},{7,1},{8,16},{9,11},{... | collective-permute-start | bytes 196616 | tf_op jit(solution)/shard_map/ppermute | solution.py:269
  38.3 4.8 %collective-permute-start.8 = (bf16[256,128]{1,0:T(8,128)(2,1)S(1)}, bf16[256,128]{1,0:T(8,128)(2,1)S(1)}, u32[]{:S(2)}, u32[]{:S(2)}) collective-permute-start(bf16[256,128]{1,0:T(8,128)(2,1)S(1)} %get-tuple-element.28), channel_id=1, source_target_pairs={{0,16},{1,5},{2,18},{3,7},{4,20},{5,1},{6,22},{7,3},{8,24},{9,13},... | collective-permute-start | bytes 196616 | tf_op jit(solution)/shard_map/ppermute | solution.py:269
  40.8 3.4 %collective-permute-start.9 = (bf16[256,128]{1,0:T(8,128)(2,1)S(1)}, bf16[256,128]{1,0:T(8,128)(2,1)S(1)}, u32[]{:S(2)}, u32[]{:S(2)}) collective-permute-start(bf16[256,128]{1,0:T(8,128)(2,1)S(1)} %get-tuple-element.29), channel_id=1, source_target_pairs={{0,24},{1,7},{2,26},{3,1},{4,28},{5,3},{6,30},{7,5},{8,0},{9,15},{... | collective-permute-start | bytes 196616 | tf_op jit(solution)/shard_map/ppermute | solution.py:269
  45.2 5.7 %collective-permute-start.12 = (bf16[3,128,256]{2,1,0:T(8,128)(2,1)S(1)}, bf16[3,128,256]{2,1,0:T(8,128)(2,1)S(1)}, u32[]{:S(2)}, u32[]{:S(2)}) collective-permute-start(bf16[3,128,256]{2,1,0:T(8,128)(2,1)S(1)} %get-tuple-element.31.own), channel_id=1, source_target_pairs={{0,8},{1,3},{2,10},{3,5},{4,12},{5,7},{6,14},{7,1},{8,16},{9,11},{... | collective-permute-start | bytes 589832 | tf_op jit(solution)/shard_map/ppermute | solution.py:269
  45.5 8.5 %collective-permute-start.11 = (bf16[3,128,256]{2,1,0:T(8,128)(2,1)S(1)}, bf16[3,128,256]{2,1,0:T(8,128)(2,1)S(1)}, u32[]{:S(2)}, u32[]{:S(2)}) collective-permute-start(bf16[3,128,256]{2,1,0:T(8,128)(2,1)S(1)} %get-tuple-element.31.own), channel_id=1, source_target_pairs={{0,16},{1,5},{2,18},{3,7},{4,20},{5,1},{6,22},{7,3},{8,24},{9,13},... | collective-permute-start | bytes 589832 | tf_op jit(solution)/shard_map/ppermute | solution.py:269
  48.8 5.2 %collective-permute-start.10 = (bf16[3,128,256]{2,1,0:T(8,128)(2,1)S(1)}, bf16[3,128,256]{2,1,0:T(8,128)(2,1)S(1)}, u32[]{:S(2)}, u32[]{:S(2)}) collective-permute-start(bf16[3,128,256]{2,1,0:T(8,128)(2,1)S(1)} %get-tuple-element.31.own), channel_id=1, source_target_pairs={{0,24},{1,7},{2,26},{3,1},{4,28},{5,3},{6,30},{7,5},{8,0},{9,15},{... | collective-permute-start | bytes 589832 | tf_op jit(solution)/shard_map/ppermute | solution.py:269
  54.0 9.3 %collective-permute-start.18 = (bf16[6,128,256]{2,1,0:T(8,128)(2,1)S(1)}, bf16[6,128,256]{2,1,0:T(8,128)(2,1)S(1)}, u32[]{:S(2)}, u32[]{:S(2)}) collective-permute-start(bf16[6,128,256]{2,1,0:T(8,128)(2,1)S(1)} %gather_step.1.p0), channel_id=1, source_target_pairs={{0,2},{1,9},{2,4},{3,11},{4,6},{5,13},{6,0},{7,15},{8,10},{9,17},{... | collective-permute-start | bytes 1179656 | tf_op jit(solution)/shard_map/ppermute | solution.py:269
  55.1 12.1 %collective-permute-start.16 = (bf16[6,128,256]{2,1,0:T(8,128)(2,1)S(1)}, bf16[6,128,256]{2,1,0:T(8,128)(2,1)S(1)}, u32[]{:S(2)}, u32[]{:S(2)}) collective-permute-start(bf16[6,128,256]{2,1,0:T(8,128)(2,1)S(1)} %gather_step.1.p0), channel_id=1, source_target_pairs={{0,4},{1,17},{2,6},{3,19},{4,0},{5,21},{6,2},{7,23},{8,12},{9,25},... | collective-permute-start | bytes 1179656 | tf_op jit(solution)/shard_map/ppermute | solution.py:269
  57.5 14.3 %collective-permute-start.14 = (bf16[6,128,256]{2,1,0:T(8,128)(2,1)S(1)}, bf16[6,128,256]{2,1,0:T(8,128)(2,1)S(1)}, u32[]{:S(2)}, u32[]{:S(2)}) collective-permute-start(bf16[6,128,256]{2,1,0:T(8,128)(2,1)S(1)} %gather_step.1.p0), channel_id=1, source_target_pairs={{0,6},{1,25},{2,0},{3,27},{4,2},{5,29},{6,4},{7,31},{8,14},{9,1},{... | collective-permute-start | bytes 1179656 | tf_op jit(solution)/shard_map/ppermute | solution.py:269
  58.1 16.2 %collective-permute-start.13 = (bf16[6,128,256]{2,1,0:T(8,128)(2,1)S(1)}, bf16[6,128,256]{2,1,0:T(8,128)(2,1)S(1)}, u32[]{:S(2)}, u32[]{:S(2)}) collective-permute-start(bf16[6,128,256]{2,1,0:T(8,128)(2,1)S(1)} %gather_step.1.p0), channel_id=1, source_target_pairs={{0,1},{1,0},{2,3},{3,2},{4,5},{5,4},{6,7},{7,6},{8,9},{9,8},{10,11... | collective-permute-start | bytes 1179656 | tf_op jit(solution)/shard_map/ppermute | solution.py:256
  63.3 11.0 %collective-permute-start.19 = (bf16[6,128,256]{2,1,0:T(8,128)(2,1)S(1)}, bf16[6,128,256]{2,1,0:T(8,128)(2,1)S(1)}, u32[]{:S(2)}, u32[]{:S(2)}) collective-permute-start(bf16[6,128,256]{2,1,0:T(8,128)(2,1)S(1)} %collective-permute-done.18.p3), channel_id=1, source_target_pairs={{0,1},{1,0},{2,3},{3,2},{4,5},{5,4},{6,7},{7,6},{8,9},{9,8},{10,11... | collective-permute-start | bytes 1179656 | tf_op jit(solution)/shard_map/ppermute | solution.py:256
  67.1 7.2 %collective-permute-start.17 = (bf16[6,128,256]{2,1,0:T(8,128)(2,1)S(1)}, bf16[6,128,256]{2,1,0:T(8,128)(2,1)S(1)}, u32[]{:S(2)}, u32[]{:S(2)}) collective-permute-start(bf16[6,128,256]{2,1,0:T(8,128)(2,1)S(1)} %collective-permute-done.16.p2), channel_id=1, source_target_pairs={{0,1},{1,0},{2,3},{3,2},{4,5},{5,4},{6,7},{7,6},{8,9},{9,8},{10,11... | collective-permute-start | bytes 1179656 | tf_op jit(solution)/shard_map/ppermute | solution.py:256
  71.7 2.6 %collective-permute-start.15 = (bf16[6,128,256]{2,1,0:T(8,128)(2,1)S(1)}, bf16[6,128,256]{2,1,0:T(8,128)(2,1)S(1)}, u32[]{:S(2)}, u32[]{:S(2)}) collective-permute-start(bf16[6,128,256]{2,1,0:T(8,128)(2,1)S(1)} %collective-permute-done.14.p1), channel_id=1, source_target_pairs={{0,1},{1,0},{2,3},{3,2},{4,5},{5,4},{6,7},{7,6},{8,9},{9,8},{10,11... | collective-permute-start | bytes 1179656 | tf_op jit(solution)/shard_map/ppermute | solution.py:256
  76.8 6.2 %collective-permute-start.20 = (bf16[3,128,256]{2,1,0:T(8,128)(2,1)S(1)}, bf16[3,128,256]{2,1,0:T(8,128)(2,1)S(1)}, u32[]{:S(2)}, u32[]{:S(2)}) collective-permute-start(bf16[3,128,256]{2,1,0:T(8,128)(2,1)S(1)} %get-tuple-element.36), channel_id=1, source_target_pairs={{0,96},{32,0},{64,32},{96,64},{1,97},{33,1},{65,33},{97,65},{2,98}... | collective-permute-start | bytes 589832 | tf_op jit(solution)/shard_map/ppermute | solution.py:252
  77.1 7.3 %collective-permute-start.21 = (bf16[3,128,256]{2,1,0:T(8,128)(2,1)S(1)}, bf16[3,128,256]{2,1,0:T(8,128)(2,1)S(1)}, u32[]{:S(2)}, u32[]{:S(2)}) collective-permute-start(bf16[3,128,256]{2,1,0:T(8,128)(2,1)S(1)} %get-tuple-element.37), channel_id=1, source_target_pairs={{0,64},{32,96},{64,0},{96,32},{1,65},{33,97},{65,1},{97,33},{2,66}... | collective-permute-start | bytes 589832 | tf_op jit(solution)/shard_map/ppermute | solution.py:252
  78.0 11.7 %collective-permute-start.22 = (bf16[3,128,256]{2,1,0:T(8,128)(2,1)S(1)}, bf16[3,128,256]{2,1,0:T(8,128)(2,1)S(1)}, u32[]{:S(2)}, u32[]{:S(2)}) collective-permute-start(bf16[3,128,256]{2,1,0:T(8,128)(2,1)S(1)} %get-tuple-element.38), channel_id=1, source_target_pairs={{0,32},{32,64},{64,96},{96,0},{1,33},{33,65},{65,97},{97,1},{2,34}... | collective-permute-start | bytes 589832 | tf_op jit(solution)/shard_map/ppermute | solution.py:252

commit v2 on v1

v2 whole, which is shorter than its diff:
```python
import functools

import jax
import jax.numpy as jnp
from jax import lax
from jax.experimental import pallas as pl
from jax.experimental.pallas import tpu as pltpu
from jax.sharding import PartitionSpec as P

BF = jnp.bfloat16
F32 = jnp.float32
VM = pl.BlockSpec(memory_space=pltpu.VMEM)
SM = pl.BlockSpec(memory_space=pltpu.SMEM)
HB = pl.BlockSpec(memory_space=pltpu.HBM)
AN = pl.BlockSpec(memory_space=pl.ANY)
PARAMS = pltpu.CompilerParams(vmem_limit_bytes=24 << 20)

FWD_TILES = 4
COL_TERMS = 2
ROW_TERMS = 2


def sds(shape, dtype):
    return jax.ShapeDtypeStruct(shape, dtype)


def dot(a, b):
    return jnp.dot(a, b, preferred_element_type=F32)


def split(v, terms=2):
    high = v.astype(BF)
    if terms == 1:
        return (high,)
    return high, (v - high.astype(F32)).astype(BF)


def joined(ref, at, terms=2):
    high = ref[at].astype(F32)
    return high if terms == 1 else high + ref[at + 1].astype(F32)


def tile(values, slot):
    found = values[jnp.maximum(slot, 0)]
    return jnp.where(slot >= 0, found, jnp.zeros_like(found))


def load_kernel(values, features, rows_in, cols_in, live, held, own, table, slot_rows, slot_cols, sem):
    pairs = ((rows_in, slot_rows), (cols_in, slot_cols))
    small = [pltpu.make_async_copy(*pair, sem.at[2 + n]) for n, pair in enumerate(pairs)]
    copies = [
        pltpu.make_async_copy(values, held, sem.at[0]),
        pltpu.make_async_copy(features, own, sem.at[1]),
    ]
    for copy in small + copies:
        copy.start()
    row, col = lax.axis_index("row"), lax.axis_index("col")
    core, x, z = col & 1, (col >> 1) & 3, col >> 3

    def clear(step, carry):
        for u in range(16):
            table[step * 16 + u] = -1
        return carry

    lax.fori_loop(0, 32, clear, 0)
    for copy in small:
        copy.wait()

    def place(slot):
        tile_row, tile_col = slot_rows[0, 0, slot], slot_cols[0, 0, slot]
        parity = (tile_row >> 1) & 1
        dx = ((tile_row >> 2) - x) & 3
        dz = ((tile_row >> 4) - z) & 3
        a = jnp.where(parity == 0, dx, dz)
        b = jnp.where(parity == 0, dz, dx)
        half = 1 - (parity ^ core)
        source = ((row - (tile_col >> 1)) & 3) * 2 + (tile_col & 1)
        table[(half * 32 + a * 8 + b * 2 + (tile_row & 1)) * 8 + source] = slot

    count = live[0, 0]

    def place_four(step, carry):
        for u in range(4):
            place(step * 4 + u)
        return carry

    def place_one(slot, carry):
        place(slot)
        return carry

    lax.fori_loop(0, count >> 2, place_four, 0)
    lax.fori_loop((count >> 2) << 2, count, place_one, 0)
    for copy in copies:
        copy.wait()


def load(values, features, slot_rows, slot_cols, live):
    given = (values, features, slot_rows, slot_cols)
    given = [pltpu.with_memory_space_constraint(value, pltpu.HBM) for value in given]
    slots = values.shape[0]
    return pl.pallas_call(
        load_kernel,
        out_shape=(sds(values.shape, BF), sds(features.shape, BF), pltpu.SMEM((512,), jnp.int32)),
        in_specs=[HB] * 4 + [SM],
        out_specs=(VM, VM, SM),
        scratch_shapes=[
            pltpu.SMEM((1, 1, slots), jnp.int32),
            pltpu.SMEM((1, 1, slots), jnp.int32),
            pltpu.SemaphoreType.DMA((4,)),
        ],
        name="load",
        cost_estimate=pl.CostEstimate(flops=0, bytes_accessed=11 << 20, transcendentals=0),
        compiler_params=PARAMS,
    )(*given, live)


def forward_kernel(start, steps, table, values, x0, x1, x2, x3, out):
    sources = (x0, x1, x2, x3)
    rows = FWD_TILES * 128
    for step in range(steps):
        total = None
        for k in range(4):
            left = []
            for r in range(FWD_TILES):
                base = (start + step * FWD_TILES + r) * 8 + 2 * k
                left.append(
                    jnp.concatenate(
                        [tile(values, table[base]), tile(values, table[base + 1])], axis=1
                    )
                )
            term = dot(jnp.concatenate(left, axis=0), sources[k][...])
            total = term if total is None else total + term
        out[step * rows : (step + 1) * rows, :] = total.astype(out.dtype)


def forward(name, start, count, dtype, table, values, sources):
    return pl.pallas_call(
        functools.partial(forward_kernel, start, count // FWD_TILES),
        out_shape=sds((count * 128, 128), dtype),
        in_specs=[SM] + [VM] * 5,
        out_specs=VM,
        name=name,
        cost_estimate=pl.CostEstimate(
            flops=2 * count * 128 * 1024 * 128, bytes_accessed=count << 15, transcendentals=0
        ),
        compiler_params=PARAMS,
    )(table, values, *sources)


def first_sum_kernel(kept, got, s1, s2, s3):
    for a, out in enumerate((s1, s2, s3)):
        total = kept[a * 1024 : a * 1024 + 1024, :] + got[a * 1024 + 1024 : a * 1024 + 2048, :].astype(F32)
        out[...] = total.astype(BF)


def first_sum(kept, got):
    return pl.pallas_call(
        first_sum_kernel,
        out_shape=(sds((1024, 128), BF),) * 3,
        in_specs=[VM] * 2,
        out_specs=(VM,) * 3,
        name="first_sum",
        compiler_params=PARAMS,
    )(kept, got)


def second_sum_kernel(own, other, g1, g2, g3, mine, s1, s2, s3):
    for b, out in enumerate((mine, s1, s2, s3)):
        part = pl.ds(b * 256, 256)
        total = own[part, :] + other[part, :].astype(F32) + g1[part, :].astype(F32)
        total = total + g2[part, :].astype(F32) + g3[part, :].astype(F32)
        out[...] = total.astype(out.dtype)


def second_sum(own, other, got):
    return pl.pallas_call(
        second_sum_kernel,
        out_shape=(sds((256, 128), F32),) + (sds((256, 128), BF),) * 3,
        in_specs=[VM] * 5,
        out_specs=(VM,) * 4,
        name="second_sum",
        compiler_params=PARAMS,
    )(own, other, *got)


def middle_kernel(own, g1, g2, g3, weight, cotangent, out, message):
    mixed = own[...] + g1[...].astype(F32) + g2[...].astype(F32) + g3[...].astype(F32)
    high, low = split(mixed)
    w = weight[...]
    summed = dot(high, w) + dot(low, w)
    gate = 1.0 / (1.0 + jnp.exp(-summed))
    out[...] = (summed * gate).astype(BF)
    slope = gate * (1.0 + summed * (1.0 - gate))
    grad = (cotangent[...].astype(F32) * slope).astype(BF)
    back = lax.dot_general(w, grad, (((1,), (1,)), ((), ())), preferred_element_type=F32)
    message[0] = back.astype(BF)
    over_rows = (((0,), (0,)), ((), ()))
    term = lax.dot_general(high, grad, over_rows, preferred_element_type=F32)
    term = term + lax.dot_general(low, grad, over_rows, preferred_element_type=F32)
    message[1], message[2] = split(term)


def middle(own, got, weight, cotangent):
    return pl.pallas_call(
        middle_kernel,
        out_shape=(sds((256, 256), BF), sds((3, 128, 256), BF)),
        in_specs=[VM] * 6,
        out_specs=(VM,) * 2,
        name="middle",
        compiler_params=PARAMS,
    )(own, *got, weight, cotangent)


def ring_sum(own, g1, g2, g3, at, terms=2):
    own, g1, g2, g3 = [joined(ref, at, terms) for ref in (own, g1, g2, g3)]
    return (own + g2) + (g1 + g3)


def gather_kernel(own, g1, g2, g3, message):
    for b, ref in enumerate((own, g1, g2, g3)):
        message[b] = ref[0]
    for n, term in enumerate(split(ring_sum(own, g1, g2, g3, 1), COL_TERMS)):
        message[4 + n] = term


def gather_step(own, got):
    return pl.pallas_call(
        gather_kernel,
        out_shape=sds((4 + COL_TERMS, 128, 256), BF),
        in_specs=[VM] * 4,
        out_specs=VM,
        name="gather_step",
        compiler_params=PARAMS,
    )(own, *got)


def backward_tiles(half, a, q, table, values, part, total):
    for b in range(4):
        base = (half * 32 + a * 8 + b * 2) * 8 + 2 * q
        upper = [tile(values, table[base]), tile(values, table[base + 1])]
        lower = [tile(values, table[base + 8]), tile(values, table[base + 9])]
        block = jnp.concatenate(
            [jnp.concatenate(upper, axis=1), jnp.concatenate(lower, axis=1)], axis=0
        )
        term = dot(part[b], block)
        total = term if total is None else total + term
    return total


def backward_kernel(half, offsets, first, table, values, *refs):
    parts, out = refs[: len(offsets)], refs[-1]
    for q in range(4):
        total = None if first else refs[len(offsets)][q]
        for a, part in zip(offsets, parts):
            total = backward_tiles(half, a, q, table, values, part, total)
        out[q] = total


BACK_COST = pl.CostEstimate(flops=1, bytes_accessed=1, transcendentals=0)


def backward(half, offsets, table, values, parts, partial):
    given = () if partial is None else (partial,)
    return pl.pallas_call(
        functools.partial(backward_kernel, half, offsets, partial is None),
        out_shape=sds((4, 128, 256), F32),
        in_specs=[SM] + [VM] * (1 + len(parts) + len(given)),
        out_specs=VM,
        name=f"backward_{half}_{offsets[0]}",
        cost_estimate=BACK_COST,
        compiler_params=PARAMS,
    )(table, values, *parts, *given)


def tie_kernel(*refs):
    del refs


def tie(values, after):
    return pl.pallas_call(
        tie_kernel,
        out_shape=[sds(value.shape, value.dtype) for value in values],
        in_specs=[AN] * (len(values) + 1),
        out_specs=[AN] * len(values),
        input_output_aliases={n: n for n in range(len(values))},
        name="tie",
        compiler_params=PARAMS,
    )(*values, after)


def last_kernel(half, offsets, table, values, p0, p1, p2, p3, o0, o1, o2, o3, partial, own, own_term, s1, s2, s3):
    sends = (s1, s2, s3)
    parts = [(o0, o1, o2, o3)[a] for a in offsets]
    term = ring_sum(p0, p1, p2, p3, 4, COL_TERMS) + ring_sum(o0, o1, o2, o3, 4, COL_TERMS)
    for n, term in enumerate(split(term, ROW_TERMS)):
        own_term[n] = term
        for out in sends:
            out[1 + n] = term
    for q in range(4):
        total = partial[q]
        for a, part in zip(offsets, parts):
            total = backward_tiles(half, a, q, table, values, part, total)
        if q == 0:
            own[...] = total
        else:
            sends[q - 1][0] = total.astype(BF)


def last(half, offsets, table, values, mine, others, partial):
    return pl.pallas_call(
        functools.partial(last_kernel, half, offsets),
        out_shape=(sds((128, 256), F32), sds((ROW_TERMS, 128, 256), BF))
        + (sds((1 + ROW_TERMS, 128, 256), BF),) * 3,
        in_specs=[SM] + [VM] * 10,
        out_specs=(VM,) * 5,
        name="backward_last",
        cost_estimate=BACK_COST,
        compiler_params=PARAMS,
    )(table, values, *mine, *others, partial)


def finish_kernel(scale, own, own_term, g1, g2, g3, grad_in, grad_weight):
    total = own[...] + g1[0].astype(F32) + g2[0].astype(F32) + g3[0].astype(F32)
    grad_in[...] = total.T.astype(BF)
    g1, g2, g3 = [joined(ref, 1, ROW_TERMS) for ref in (g1, g2, g3)]
    term = (joined(own_term, 0, ROW_TERMS) + g2) + (g1 + g3)
    grad_weight[...] = term * scale


def finish(scale, own, own_term, got):
    return pl.pallas_call(
        functools.partial(finish_kernel, scale),
        out_shape=(sds((256, 128), BF), sds((128, 256), F32)),
        in_specs=[VM] * 5,
        out_specs=(VM,) * 2,
        name="finish",
        compiler_params=PARAMS,
    )(own, own_term, *got)


def row_shift(value, k):
    return lax.ppermute(value, "row", [(i, (i + k) % 4) for i in range(4)])


def swap_cores(value):
    return lax.ppermute(value, "col", [(j, j ^ 1) for j in range(32)])


def chip_shift(value, k, x_core):
    pairs = []
    for z in range(4):
        for x in range(4):
            for core in range(2):
                if core == x_core:
                    to = (z, (x + k) % 4)
                else:
                    to = ((z + k) % 4, x)
                pairs.append(((z * 4 + x) * 2 + core, (to[0] * 4 + to[1]) * 2 + core))
    return lax.ppermute(value, "col", pairs)


def local(features, weight, cotangent, tile_values, tile_rows, tile_cols, tile_counts):
    shifted = [row_shift(features, k) for k in (1, 2, 3)]
    values, own_features, table = load(
        tile_values[0, 0], features, tile_rows, tile_cols, tile_counts
    )
    sources = [own_features] + shifted
    other = swap_cores(forward("forward_other", 0, 32, BF, table, values, sources))
    kept = forward("forward_sent", 40, 24, F32, table, values, sources)
    sends = first_sum(kept, other)
    got = [chip_shift(v, k, 0) for k, v in zip((1, 2, 3), sends)]
    kept = forward("forward_kept", 32, 8, F32, table, values, sources)
    own, *sends = second_sum(kept, other, got)
    got = [chip_shift(v, k, 1) for k, v in zip((1, 2, 3), sends)]
    output, message = middle(own, got, weight, cotangent)
    got = [chip_shift(message, -k, 1) for k in (1, 2, 3)]
    message = gather_step(message, got)
    p0, p1, p2, p3 = [message] + [chip_shift(message, -k, 0) for k in (1, 2, 3)]
    o0 = swap_cores(p0)
    partial = backward(1, (0,), table, values, (p0,), None)
    partial = backward(0, (0,), table, values, (o0,), partial)
    p1, p2, p3 = tie((p1, p2, p3), partial)
    o1, o2, o3 = [swap_cores(v) for v in (p1, p2, p3)]
    partial = backward(1, (1, 2, 3), table, values, (p1, p2, p3), partial)
    mine, others = (p0, p1, p2, p3), (o0, o1, o2, o3)
    own, own_term, *sends = last(0, (1, 2, 3), table, values, mine, others, partial)
    got = [row_shift(v, -k) for k, v in zip((1, 2, 3), sends)]
    grad_in, grad_weight = finish(32768.0 ** -0.5, own, own_term, got)
    return output, grad_in, grad_weight


def solution(mesh):
    placed = (
        P(("row", "col"), None),
        P(),
        P(("row", "col"), None),
        P("row", "col", None, None, None),
        P("row", "col", None),
        P("row", "col", None),
        P("row", "col"),
    )
    return jax.shard_map(
        local,
        mesh=mesh,
        in_specs=placed,
        out_specs=(P(("row", "col"), None), P(("row", "col"), None), P()),
        check_vma=False,
    )
```

time: 90.7 us -> 82.3 us (0.907)
  starting transfers between devices: 40.6 us -> 33.1 us
  waiting for transfers between devices: 27.3 us -> 32.6 us
  local copies, waits for them, and re-layouts: 4.85 us -> 0.01 us
    ppermute x5, starting transfers between devices: 15.6 us -> 7.49 us  [swap_cores(): return lax.ppermute(value, 'col', [(j, j ^ 1) for j in range(32)])]
    ppermute x12, waiting for transfers between devices: 13.5 us -> 20.4 us  [chip_shift(): return lax.ppermute(value, 'col', pairs)]
    unnamed x14 -> x4, local copies, waits for them, and re-layouts: 4.85 us -> 0.01 us
    ppermute x6, waiting for transfers between devices: 13.8 us -> 11.2 us  [row_shift(): return lax.ppermute(value, 'row', [(i, (i + k) % 4) for i in range(4)])]
    ppermute x5, waiting for transfers between devices: 0.01 us -> 1.07 us  [swap_cores(): return lax.ppermute(value, 'col', [(j, j ^ 1) for j in range(32)])]
    ppermute x6, starting transfers between devices: 6.62 us -> 7.53 us  [row_shift(): return lax.ppermute(value, 'row', [(i, (i + k) % 4) for i in range(4)])]
    pallas_call x6 -> x11, Pallas kernels: 13.4 us -> 13.1 us  [the longest x3 4.81 us: forward(): pl.pallas_call(functools.partial(forward_kernel, start, count // FWD_TILE...]
  transfers between devices with their start and end apart: 23 -> 23, of which waited for: 12 -> 13; matrix products, arithmetic and copies ran while one was open for 1% -> 0% of each run, Pallas kernels for 7% -> 11%
where the time goes in v2:
time: 82.3 us; the launch traced here: 82.2 us
  starting transfers between devices  33.1 us (40%)
  waiting for transfers between devices  32.6 us (40%)
  Pallas kernels  15 us (18%)
  between operations  1.43 us (2%)
    ppermute x12, waiting for transfers between devices, chip_shift(): return lax.ppermute(value, 'col', pairs)  20.4 us
    ppermute x12, starting transfers between devices, chip_shift(): return lax.ppermute(value, 'col', pairs)  18.1 us
    ppermute x6, waiting for transfers between devices, row_shift(): return lax.ppermute(value, 'row', [(i, (i + k) % 4) for i in range(4)])  11.2 us
    ppermute x6, starting transfers between devices, row_shift(): return lax.ppermute(value, 'row', [(i, (i + k) % 4) for i in range(4)])  7.53 us
    ppermute x5, starting transfers between devices, swap_cores(): return lax.ppermute(value, 'col', [(j, j ^ 1) for j in range(32)])  7.49 us
    pallas_call x3, Pallas kernels, forward(): pl.pallas_call(functools.partial(forward_kernel, start, count // FWD_TILE...  4.81 us
    pallas_call x1, Pallas kernels, load(): pl.pallas_call(load_kernel, out_shape=(sds(values.shape, BF), sds(feature...  4.02 us
    pallas_call x3, Pallas kernels, backward(): pl.pallas_call(functools.partial(backward_kernel, half, offsets, partial...  2.48 us
  transfers between devices with their start and end apart: 23, of which 13 were waited for; matrix products, arithmetic and copies ran while one was open for 0% of the time, Pallas kernels for 11%

profile of v2, /device:TPU:1, one launch (start us, length us, event | category | flops | bytes accessed | tf_op | source)
XLA Modules:
  0.0 82.2 jit_solution(12076929850756510435)
XLA Ops:
  0.6 2.2 %collective-permute-start = (bf16[256,128]{1,0:T(8,128)(2,1)}, bf16[256,128]{1,0:T(8,128)(2,1)S(1)}, u32[]{:S(2)}, u32[]{:S(2)}) collective-permute-start(bf16[256,128]{1,0:T(8,128)(2,1)} %features.1), channel_id=1, source_target_pairs={{0,32},{32,64},{64,96},{96,0},{1,33},{33,65},{65,97},{97,1},{2,34}... | collective-permute-start | bytes 196616 | tf_op jit(solution)/shard_map/ppermute | solution.py:342
  2.8 1.5 %collective-permute-start.2 = (bf16[256,128]{1,0:T(8,128)(2,1)}, bf16[256,128]{1,0:T(8,128)(2,1)S(1)}, u32[]{:S(2)}, u32[]{:S(2)}) collective-permute-start(bf16[256,128]{1,0:T(8,128)(2,1)} %features.1), channel_id=1, source_target_pairs={{0,96},{32,0},{64,32},{96,64},{1,97},{33,1},{65,33},{97,65},{2,98}... | collective-permute-start | bytes 196616 | tf_op jit(solution)/shard_map/ppermute | solution.py:342
  4.3 1.6 %collective-permute-start.1 = (bf16[256,128]{1,0:T(8,128)(2,1)}, bf16[256,128]{1,0:T(8,128)(2,1)S(1)}, u32[]{:S(2)}, u32[]{:S(2)}) collective-permute-start(bf16[256,128]{1,0:T(8,128)(2,1)} %features.1), channel_id=1, source_target_pairs={{0,64},{32,96},{64,0},{96,32},{1,65},{33,97},{65,1},{97,33},{2,66}... | collective-permute-start | bytes 196616 | tf_op jit(solution)/shard_map/ppermute | solution.py:342
  6.6 4.0 %load.1 = (bf16[320,128,128]{2,1,0:T(8,128)(2,1)S(1)}, bf16[256,128]{1,0:T(8,128)(2,1)S(1)}, s32[512]{0:T(512)S(4)}) custom-call(bf16[320,128,128]{2,1,0:T(8,128)(2,1)} %bitcast.1, bf16[256,128]{1,0:T(8,128)(2,1)} %features.1, s32[1,1,320]{2,1,0:T(1,128)} %rows_in.1, s32[1,1,320]{2,1,0:T(1,128)} %cols_in.1, s32[1,1]{1,0:T(1,128)S(6)} %copy.16.live), custom_call_target="tpu_custom_call" | custom-call | bytes 11534336 | tf_op jit(solution)/shard_map/load/pallas_call | solution.py:101
  10.6 2.3 %forward_other.1 = bf16[4096,128]{1,0:T(8,128)(2,1)S(1)} custom-call(s32[512]{0:T(512)S(4)} %get-tuple-element.25.table, bf16[320,128,128]{2,1,0:T(8,128)(2,1)S(1)} %get-tuple-element.26.values, bf16[256,128]{1,0:T(8,128)(2,1)S(1)} %get-tuple-element.27.x0, bf16[256,128]{1,0:T(8,128)(2,1)S(1)} %collective-permute-done.x1, ...), custom_call_target="tpu_custom_call" | custom-call | flops 1073741824 | bytes 1048576 | tf_op jit(solution)/shard_map/forward_other/pallas_call | solution.py:137
  13.0 1.6 %collective-permute-start.3 = (bf16[4096,128]{1,0:T(8,128)(2,1)S(1)}, bf16[4096,128]{1,0:T(8,128)(2,1)S(1)}, u32[]{:S(2)}, u32[]{:S(2)}) collective-permute-start(bf16[4096,128]{1,0:T(8,128)(2,1)S(1)} %forward_other.1), channel_id=1, source_target_pairs={{0,1},{1,0},{2,3},{3,2},{4,5},{5,4},{6,7},{7,6},{8,9},{9,8},{10,11... | collective-permute-start | bytes 3145736 | tf_op jit(solution)/shard_map/ppermute | solution.py:346
  14.6 1.8 %forward_sent.1.kept = f32[3072,128]{1,0:T(8,128)S(1)} custom-call(s32[512]{0:T(512)S(4)} %get-tuple-element.25.table, bf16[320,128,128]{2,1,0:T(8,128)(2,1)S(1)} %get-tuple-element.26.values, bf16[256,128]{1,0:T(8,128)(2,1)S(1)} %get-tuple-element.27.x0, bf16[256,128]{1,0:T(8,128)(2,1)S(1)} %collective-permute-done.x1, ...), custom_call_target="tpu_custom_call" | custom-call | flops 805306368 | bytes 786432 | tf_op jit(solution)/shard_map/forward_sent/pallas_call | solution.py:137
  17.0 1.7 %collective-permute-start.4 = (bf16[1024,128]{1,0:T(8,128)(2,1)S(1)}, bf16[1024,128]{1,0:T(8,128)(2,1)S(1)}, u32[]{:S(2)}, u32[]{:S(2)}) collective-permute-start(bf16[1024,128]{1,0:T(8,128)(2,1)S(1)} %get-tuple-element.28), channel_id=1, source_target_pairs={{0,2},{1,9},{2,4},{3,11},{4,6},{5,13},{6,0},{7,15},{8,10},{9,17},{... | collective-permute-start | bytes 786440 | tf_op jit(solution)/shard_map/ppermute | solution.py:359
  18.7 3.3 %collective-permute-start.5 = (bf16[1024,128]{1,0:T(8,128)(2,1)S(1)}, bf16[1024,128]{1,0:T(8,128)(2,1)S(1)}, u32[]{:S(2)}, u32[]{:S(2)}) collective-permute-start(bf16[1024,128]{1,0:T(8,128)(2,1)S(1)} %get-tuple-element.29), channel_id=1, source_target_pairs={{0,4},{1,17},{2,6},{3,19},{4,0},{5,21},{6,2},{7,23},{8,12},{9,25},... | collective-permute-start | bytes 786440 | tf_op jit(solution)/shard_map/ppermute | solution.py:359
  23.4 1.2 %collective-permute-done.4.g1 = bf16[1024,128]{1,0:T(8,128)(2,1)S(1)} collective-permute-done((bf16[1024,128]{1,0:T(8,128)(2,1)S(1)}, bf16[1024,128]{1,0:T(8,128)(2,1)S(1)}, u32[]{:S(2)}, u32[]{:S(2)}) %collective-permute-start.4) | collective-permute-done | bytes 262176 | tf_op jit(solution)/shard_map/ppermute | solution.py:359
  24.6 3.9 %collective-permute-done.5.g2 = bf16[1024,128]{1,0:T(8,128)(2,1)S(1)} collective-permute-done((bf16[1024,128]{1,0:T(8,128)(2,1)S(1)}, bf16[1024,128]{1,0:T(8,128)(2,1)S(1)}, u32[]{:S(2)}, u32[]{:S(2)}) %collective-permute-start.5) | collective-permute-done | bytes 262176 | tf_op jit(solution)/shard_map/ppermute | solution.py:359
  28.7 1.3 %collective-permute-start.7 = (bf16[256,128]{1,0:T(8,128)(2,1)S(1)}, bf16[256,128]{1,0:T(8,128)(2,1)S(1)}, u32[]{:S(2)}, u32[]{:S(2)}) collective-permute-start(bf16[256,128]{1,0:T(8,128)(2,1)S(1)} %get-tuple-element.32), channel_id=1, source_target_pairs={{0,8},{1,3},{2,10},{3,5},{4,12},{5,7},{6,14},{7,1},{8,16},{9,11},{... | collective-permute-start | bytes 196616 | tf_op jit(solution)/shard_map/ppermute | solution.py:359
  30.0 2.4 %collective-permute-start.8 = (bf16[256,128]{1,0:T(8,128)(2,1)S(1)}, bf16[256,128]{1,0:T(8,128)(2,1)S(1)}, u32[]{:S(2)}, u32[]{:S(2)}) collective-permute-start(bf16[256,128]{1,0:T(8,128)(2,1)S(1)} %get-tuple-element.33), channel_id=1, source_target_pairs={{0,16},{1,5},{2,18},{3,7},{4,20},{5,1},{6,22},{7,3},{8,24},{9,13},... | collective-permute-start | bytes 196616 | tf_op jit(solution)/shard_map/ppermute | solution.py:359
  32.4 1.1 %collective-permute-start.9 = (bf16[256,128]{1,0:T(8,128)(2,1)S(1)}, bf16[256,128]{1,0:T(8,128)(2,1)S(1)}, u32[]{:S(2)}, u32[]{:S(2)}) collective-permute-start(bf16[256,128]{1,0:T(8,128)(2,1)S(1)} %get-tuple-element.34), channel_id=1, source_target_pairs={{0,24},{1,7},{2,26},{3,1},{4,28},{5,3},{6,30},{7,5},{8,0},{9,15},{... | collective-permute-start | bytes 196616 | tf_op jit(solution)/shard_map/ppermute | solution.py:359
  33.6 1.2 %collective-permute-done.8.g2 = bf16[256,128]{1,0:T(8,128)(2,1)S(1)} collective-permute-done((bf16[256,128]{1,0:T(8,128)(2,1)S(1)}, bf16[256,128]{1,0:T(8,128)(2,1)S(1)}, u32[]{:S(2)}, u32[]{:S(2)}) %collective-permute-start.8) | collective-permute-done | bytes 65568 | tf_op jit(solution)/shard_map/ppermute | solution.py:359
  35.6 1.0 %middle.1 = (bf16[256,256]{1,0:T(8,128)(2,1)}, bf16[3,128,256]{2,1,0:T(8,128)(2,1)S(1)}) custom-call(f32[256,128]{1,0:T(8,128)S(1)} %get-tuple-element.31.own, bf16[256,128]{1,0:T(8,128)(2,1)S(1)} %collective-permute-done.7.g1, bf16[256,128]{1,0:T(8,128)(2,1)S(1)} %collective-permute-done.8.g2, bf16[256,128]{1,0:T(8,128)(2,1)S(1)} %collective-permute-done.9.g3, ...), custom_call_target="tpu_custom_call" | custom-call | tf_op jit(solution)/shard_map/middle/pallas_call | solution.py:204
  37.1 3.0 %collective-permute-start.11 = (bf16[3,128,256]{2,1,0:T(8,128)(2,1)S(1)}, bf16[3,128,256]{2,1,0:T(8,128)(2,1)S(1)}, u32[]{:S(2)}, u32[]{:S(2)}) collective-permute-start(bf16[3,128,256]{2,1,0:T(8,128)(2,1)S(1)} %get-tuple-element.36.own), channel_id=1, source_target_pairs={{0,16},{1,5},{2,18},{3,7},{4,20},{5,1},{6,22},{7,3},{8,24},{9,13},... | collective-permute-start | bytes 589832 | tf_op jit(solution)/shard_map/ppermute | solution.py:359
  40.5 1.8 %collective-permute-done.12.g3 = bf16[3,128,256]{2,1,0:T(8,128)(2,1)S(1)} collective-permute-done((bf16[3,128,256]{2,1,0:T(8,128)(2,1)S(1)}, bf16[3,128,256]{2,1,0:T(8,128)(2,1)S(1)}, u32[]{:S(2)}, u32[]{:S(2)}) %collective-permute-start.12) | collective-permute-done | bytes 196640 | tf_op jit(solution)/shard_map/ppermute | solution.py:359
  42.3 3.0 %collective-permute-done.11.g2 = bf16[3,128,256]{2,1,0:T(8,128)(2,1)S(1)} collective-permute-done((bf16[3,128,256]{2,1,0:T(8,128)(2,1)S(1)}, bf16[3,128,256]{2,1,0:T(8,128)(2,1)S(1)}, u32[]{:S(2)}, u32[]{:S(2)}) %collective-permute-start.11) | collective-permute-done | bytes 196640 | tf_op jit(solution)/shard_map/ppermute | solution.py:359
  45.4 4.4 %collective-permute-start.16 = (bf16[6,128,256]{2,1,0:T(8,128)(2,1)S(1)}, bf16[6,128,256]{2,1,0:T(8,128)(2,1)S(1)}, u32[]{:S(2)}, u32[]{:S(2)}) collective-permute-start(bf16[6,128,256]{2,1,0:T(8,128)(2,1)S(1)} %gather_step.1.refs_0_.p0), channel_id=1, source_target_pairs={{0,1},{1,0},{2,3},{3,2},{4,5},{5,4},{6,7},{7,6},{8,9},{9,8},{10,11... | collective-permute-start | bytes 1179656 | tf_op jit(solution)/shard_map/ppermute | solution.py:346
  50.4 3.0 %collective-permute-start.14 = (bf16[6,128,256]{2,1,0:T(8,128)(2,1)S(1)}, bf16[6,128,256]{2,1,0:T(8,128)(2,1)S(1)}, u32[]{:S(2)}, u32[]{:S(2)}) collective-permute-start(bf16[6,128,256]{2,1,0:T(8,128)(2,1)S(1)} %gather_step.1.refs_0_.p0), channel_id=1, source_target_pairs={{0,4},{1,17},{2,6},{3,19},{4,0},{5,21},{6,2},{7,23},{8,12},{9,25},... | collective-permute-start | bytes 1179656 | tf_op jit(solution)/shard_map/ppermute | solution.py:359
  54.5 3.4 %collective-permute-done.15.refs_2_ = bf16[6,128,256]{2,1,0:T(8,128)(2,1)S(1)} collective-permute-done((bf16[6,128,256]{2,1,0:T(8,128)(2,1)S(1)}, bf16[6,128,256]{2,1,0:T(8,128)(2,1)S(1)}, u32[]{:S(2)}, u32[]{:S(2)}) %collective-permute-start.15) | collective-permute-done | bytes 393248 | tf_op jit(solution)/shard_map/ppermute | solution.py:359
  57.9 5.1 %collective-permute-done.14.refs_1_ = bf16[6,128,256]{2,1,0:T(8,128)(2,1)S(1)} collective-permute-done((bf16[6,128,256]{2,1,0:T(8,128)(2,1)S(1)}, bf16[6,128,256]{2,1,0:T(8,128)(2,1)S(1)}, u32[]{:S(2)}, u32[]{:S(2)}) %collective-permute-start.14) | collective-permute-done | bytes 393248 | tf_op jit(solution)/shard_map/ppermute | solution.py:359
  63.0 0.9 %collective-permute-start.17 = (bf16[6,128,256]{2,1,0:T(8,128)(2,1)S(1)}, bf16[6,128,256]{2,1,0:T(8,128)(2,1)S(1)}, u32[]{:S(2)}, u32[]{:S(2)}) collective-permute-start(bf16[6,128,256]{2,1,0:T(8,128)(2,1)S(1)} %get-tuple-element.37.refs_0_.p1), channel_id=1, source_target_pairs={{0,1},{1,0},{2,3},{3,2},{4,5},{5,4},{6,7},{7,6},{8,9},{9,8},{10,11... | collective-permute-start | bytes 1179656 | tf_op jit(solution)/shard_map/ppermute | solution.py:346
  64.5 1.4 %backward_1_1.1.partial = f32[4,128,256]{2,1,0:T(8,128)S(1)} custom-call(s32[512]{0:T(512)S(4)} %get-tuple-element.25.table, bf16[320,128,128]{2,1,0:T(8,128)(2,1)S(1)} %get-tuple-element.26.values, bf16[6,128,256]{2,1,0:T(8,128)(2,1)S(1)} %get-tuple-element.37.refs_0_.p1, bf16[6,128,256]{2,1,0:T(8,128)(2,1)S(1)} %get-tuple-element.38.refs_1_.p2, ...), custom_call_target="tpu_custom_call" | custom-call | flops 1 | bytes 1 | tf_op jit(solution)/shard_map/backward_1_1/pallas_call | solution.py:264
  66.5 1.5 %backward_last.1 = (f32[128,256]{1,0:T(8,128)S(1)}, bf16[2,128,256]{2,1,0:T(8,128)(2,1)S(1)}, bf16[3,128,256]{2,1,0:T(8,128)(2,1)S(1)}, bf16[3,128,256]{2,1,0:T(8,128)(2,1)S(1)}, bf16[3,128,256]{2,1,0:T(8,128)(2,1)S(1)}) custom-call(s32[512]{0:T(512)S(4)} %get-tuple-element.25.table, bf16[320,128,128]{2,1,0:T(8,128)(2,1)S(1)} %get-tuple-element.26.values, ...), custom_call_target="tpu_custom_call" | custom-call | flops 1 | bytes 1 | tf_op jit(solution)/shard_map/backward_last/pallas_call | solution.py:310
  68.0 0.9 %collective-permute-start.20 = (bf16[3,128,256]{2,1,0:T(8,128)(2,1)S(1)}, bf16[3,128,256]{2,1,0:T(8,128)(2,1)S(1)}, u32[]{:S(2)}, u32[]{:S(2)}) collective-permute-start(bf16[3,128,256]{2,1,0:T(8,128)(2,1)S(1)} %get-tuple-element.42), channel_id=1, source_target_pairs={{0,96},{32,0},{64,32},{96,64},{1,97},{33,1},{65,33},{97,65},{2,98}... | collective-permute-start | bytes 589832 | tf_op jit(solution)/shard_map/ppermute | solution.py:342
  68.8 1.4 %collective-permute-start.21 = (bf16[3,128,256]{2,1,0:T(8,128)(2,1)S(1)}, bf16[3,128,256]{2,1,0:T(8,128)(2,1)S(1)}, u32[]{:S(2)}, u32[]{:S(2)}) collective-permute-start(bf16[3,128,256]{2,1,0:T(8,128)(2,1)S(1)} %get-tuple-element.43), channel_id=1, source_target_pairs={{0,64},{32,96},{64,0},{96,32},{1,65},{33,97},{65,1},{97,33},{2,66}... | collective-permute-start | bytes 589832 | tf_op jit(solution)/shard_map/ppermute | solution.py:342
  70.2 3.9 %collective-permute-done.20.g1 = bf16[3,128,256]{2,1,0:T(8,128)(2,1)S(1)} collective-permute-done((bf16[3,128,256]{2,1,0:T(8,128)(2,1)S(1)}, bf16[3,128,256]{2,1,0:T(8,128)(2,1)S(1)}, u32[]{:S(2)}, u32[]{:S(2)}) %collective-permute-start.20) | collective-permute-done | bytes 196640 | tf_op jit(solution)/shard_map/ppermute | solution.py:342
  74.2 2.0 %collective-permute-done.21.g2 = bf16[3,128,256]{2,1,0:T(8,128)(2,1)S(1)} collective-permute-done((bf16[3,128,256]{2,1,0:T(8,128)(2,1)S(1)}, bf16[3,128,256]{2,1,0:T(8,128)(2,1)S(1)}, u32[]{:S(2)}, u32[]{:S(2)}) %collective-permute-start.21) | collective-permute-done | bytes 196640 | tf_op jit(solution)/shard_map/ppermute | solution.py:342
  76.2 5.2 %collective-permute-done.22.g3 = bf16[3,128,256]{2,1,0:T(8,128)(2,1)S(1)} collective-permute-done((bf16[3,128,256]{2,1,0:T(8,128)(2,1)S(1)}, bf16[3,128,256]{2,1,0:T(8,128)(2,1)S(1)}, u32[]{:S(2)}, u32[]{:S(2)}) %collective-permute-start.22) | collective-permute-done | bytes 196640 | tf_op jit(solution)/shard_map/ppermute | solution.py:342
  81.4 0.8 finish.1
  (32 shorter events, 6.9 us)
Async XLA Ops:
  0.6 10.0 %collective-permute-start = (bf16[256,128]{1,0:T(8,128)(2,1)}, bf16[256,128]{1,0:T(8,128)(2,1)S(1)}, u32[]{:S(2)}, u32[]{:S(2)}) collective-permute-start(bf16[256,128]{1,0:T(8,128)(2,1)} %features.1), channel_id=1, source_target_pairs={{0,32},{32,64},{64,96},{96,0},{1,33},{33,65},{65,97},{97,1},{2,34}... | collective-permute-start | bytes 196616 | tf_op jit(solution)/shard_map/ppermute | solution.py:342
  2.8 7.8 %collective-permute-start.2 = (bf16[256,128]{1,0:T(8,128)(2,1)}, bf16[256,128]{1,0:T(8,128)(2,1)S(1)}, u32[]{:S(2)}, u32[]{:S(2)}) collective-permute-start(bf16[256,128]{1,0:T(8,128)(2,1)} %features.1), channel_id=1, source_target_pairs={{0,96},{32,0},{64,32},{96,64},{1,97},{33,1},{65,33},{97,65},{2,98}... | collective-permute-start | bytes 196616 | tf_op jit(solution)/shard_map/ppermute | solution.py:342
  4.3 6.3 %collective-permute-start.1 = (bf16[256,128]{1,0:T(8,128)(2,1)}, bf16[256,128]{1,0:T(8,128)(2,1)S(1)}, u32[]{:S(2)}, u32[]{:S(2)}) collective-permute-start(bf16[256,128]{1,0:T(8,128)(2,1)} %features.1), channel_id=1, source_target_pairs={{0,64},{32,96},{64,0},{96,32},{1,65},{33,97},{65,1},{97,33},{2,66}... | collective-permute-start | bytes 196616 | tf_op jit(solution)/shard_map/ppermute | solution.py:342
  13.0 3.9 %collective-permute-start.3 = (bf16[4096,128]{1,0:T(8,128)(2,1)S(1)}, bf16[4096,128]{1,0:T(8,128)(2,1)S(1)}, u32[]{:S(2)}, u32[]{:S(2)}) collective-permute-start(bf16[4096,128]{1,0:T(8,128)(2,1)S(1)} %forward_other.1), channel_id=1, source_target_pairs={{0,1},{1,0},{2,3},{3,2},{4,5},{5,4},{6,7},{7,6},{8,9},{9,8},{10,11... | collective-permute-start | bytes 3145736 | tf_op jit(solution)/shard_map/ppermute | solution.py:346
  16.3 19.2 %copy-start = (bf16[256,256]{1,0:T(8,128)(2,1)S(1)}, bf16[256,256]{1,0:T(8,128)(2,1)}, u32[]{:S(2)}) copy-start(bf16[256,256]{1,0:T(8,128)(2,1)} %cotangent.1) | copy-start | bytes 393220
  16.4 19.2 %copy-start.1 = (bf16[128,256]{1,0:T(8,128)(2,1)S(1)}, bf16[128,256]{1,0:T(8,128)(2,1)}, u32[]{:S(2)}) copy-start(bf16[128,256]{1,0:T(8,128)(2,1)} %weight.1) | copy-start | bytes 196612
  17.0 7.6 %collective-permute-start.4 = (bf16[1024,128]{1,0:T(8,128)(2,1)S(1)}, bf16[1024,128]{1,0:T(8,128)(2,1)S(1)}, u32[]{:S(2)}, u32[]{:S(2)}) collective-permute-start(bf16[1024,128]{1,0:T(8,128)(2,1)S(1)} %get-tuple-element.28), channel_id=1, source_target_pairs={{0,2},{1,9},{2,4},{3,11},{4,6},{5,13},{6,0},{7,15},{8,10},{9,17},{... | collective-permute-start | bytes 786440 | tf_op jit(solution)/shard_map/ppermute | solution.py:359
  18.7 9.9 %collective-permute-start.5 = (bf16[1024,128]{1,0:T(8,128)(2,1)S(1)}, bf16[1024,128]{1,0:T(8,128)(2,1)S(1)}, u32[]{:S(2)}, u32[]{:S(2)}) collective-permute-start(bf16[1024,128]{1,0:T(8,128)(2,1)S(1)} %get-tuple-element.29), channel_id=1, source_target_pairs={{0,4},{1,17},{2,6},{3,19},{4,0},{5,21},{6,2},{7,23},{8,12},{9,25},... | collective-permute-start | bytes 786440 | tf_op jit(solution)/shard_map/ppermute | solution.py:359
  22.0 6.6 %collective-permute-start.6 = (bf16[1024,128]{1,0:T(8,128)(2,1)S(1)}, bf16[1024,128]{1,0:T(8,128)(2,1)S(1)}, u32[]{:S(2)}, u32[]{:S(2)}) collective-permute-start(bf16[1024,128]{1,0:T(8,128)(2,1)S(1)} %get-tuple-element.30), channel_id=1, source_target_pairs={{0,6},{1,25},{2,0},{3,27},{4,2},{5,29},{6,4},{7,31},{8,14},{9,1},{... | collective-permute-start | bytes 786440 | tf_op jit(solution)/shard_map/ppermute | solution.py:359
  28.7 4.9 %collective-permute-start.7 = (bf16[256,128]{1,0:T(8,128)(2,1)S(1)}, bf16[256,128]{1,0:T(8,128)(2,1)S(1)}, u32[]{:S(2)}, u32[]{:S(2)}) collective-permute-start(bf16[256,128]{1,0:T(8,128)(2,1)S(1)} %get-tuple-element.32), channel_id=1, source_target_pairs={{0,8},{1,3},{2,10},{3,5},{4,12},{5,7},{6,14},{7,1},{8,16},{9,11},{... | collective-permute-start | bytes 196616 | tf_op jit(solution)/shard_map/ppermute | solution.py:359
  30.0 4.8 %collective-permute-start.8 = (bf16[256,128]{1,0:T(8,128)(2,1)S(1)}, bf16[256,128]{1,0:T(8,128)(2,1)S(1)}, u32[]{:S(2)}, u32[]{:S(2)}) collective-permute-start(bf16[256,128]{1,0:T(8,128)(2,1)S(1)} %get-tuple-element.33), channel_id=1, source_target_pairs={{0,16},{1,5},{2,18},{3,7},{4,20},{5,1},{6,22},{7,3},{8,24},{9,13},... | collective-permute-start | bytes 196616 | tf_op jit(solution)/shard_map/ppermute | solution.py:359
  32.4 3.1 %collective-permute-start.9 = (bf16[256,128]{1,0:T(8,128)(2,1)S(1)}, bf16[256,128]{1,0:T(8,128)(2,1)S(1)}, u32[]{:S(2)}, u32[]{:S(2)}) collective-permute-start(bf16[256,128]{1,0:T(8,128)(2,1)S(1)} %get-tuple-element.34), channel_id=1, source_target_pairs={{0,24},{1,7},{2,26},{3,1},{4,28},{5,3},{6,30},{7,5},{8,0},{9,15},{... | collective-permute-start | bytes 196616 | tf_op jit(solution)/shard_map/ppermute | solution.py:359
  36.5 5.7 %collective-permute-start.12 = (bf16[3,128,256]{2,1,0:T(8,128)(2,1)S(1)}, bf16[3,128,256]{2,1,0:T(8,128)(2,1)S(1)}, u32[]{:S(2)}, u32[]{:S(2)}) collective-permute-start(bf16[3,128,256]{2,1,0:T(8,128)(2,1)S(1)} %get-tuple-element.36.own), channel_id=1, source_target_pairs={{0,8},{1,3},{2,10},{3,5},{4,12},{5,7},{6,14},{7,1},{8,16},{9,11},{... | collective-permute-start | bytes 589832 | tf_op jit(solution)/shard_map/ppermute | solution.py:359
  37.1 8.1 %collective-permute-start.11 = (bf16[3,128,256]{2,1,0:T(8,128)(2,1)S(1)}, bf16[3,128,256]{2,1,0:T(8,128)(2,1)S(1)}, u32[]{:S(2)}, u32[]{:S(2)}) collective-permute-start(bf16[3,128,256]{2,1,0:T(8,128)(2,1)S(1)} %get-tuple-element.36.own), channel_id=1, source_target_pairs={{0,16},{1,5},{2,18},{3,7},{4,20},{5,1},{6,22},{7,3},{8,24},{9,13},... | collective-permute-start | bytes 589832 | tf_op jit(solution)/shard_map/ppermute | solution.py:359
  40.1 5.2 %collective-permute-start.10 = (bf16[3,128,256]{2,1,0:T(8,128)(2,1)S(1)}, bf16[3,128,256]{2,1,0:T(8,128)(2,1)S(1)}, u32[]{:S(2)}, u32[]{:S(2)}) collective-permute-start(bf16[3,128,256]{2,1,0:T(8,128)(2,1)S(1)} %get-tuple-element.36.own), channel_id=1, source_target_pairs={{0,24},{1,7},{2,26},{3,1},{4,28},{5,3},{6,30},{7,5},{8,0},{9,15},{... | collective-permute-start | bytes 589832 | tf_op jit(solution)/shard_map/ppermute | solution.py:359
  45.4 8.6 %collective-permute-start.16 = (bf16[6,128,256]{2,1,0:T(8,128)(2,1)S(1)}, bf16[6,128,256]{2,1,0:T(8,128)(2,1)S(1)}, u32[]{:S(2)}, u32[]{:S(2)}) collective-permute-start(bf16[6,128,256]{2,1,0:T(8,128)(2,1)S(1)} %gather_step.1.refs_0_.p0), channel_id=1, source_target_pairs={{0,1},{1,0},{2,3},{3,2},{4,5},{5,4},{6,7},{7,6},{8,9},{9,8},{10,11... | collective-permute-start | bytes 1179656 | tf_op jit(solution)/shard_map/ppermute | solution.py:346
  49.8 8.1 %collective-permute-start.15 = (bf16[6,128,256]{2,1,0:T(8,128)(2,1)S(1)}, bf16[6,128,256]{2,1,0:T(8,128)(2,1)S(1)}, u32[]{:S(2)}, u32[]{:S(2)}) collective-permute-start(bf16[6,128,256]{2,1,0:T(8,128)(2,1)S(1)} %gather_step.1.refs_0_.p0), channel_id=1, source_target_pairs={{0,2},{1,9},{2,4},{3,11},{4,6},{5,13},{6,0},{7,15},{8,10},{9,17},{... | collective-permute-start | bytes 1179656 | tf_op jit(solution)/shard_map/ppermute | solution.py:359
  50.4 12.6 %collective-permute-start.14 = (bf16[6,128,256]{2,1,0:T(8,128)(2,1)S(1)}, bf16[6,128,256]{2,1,0:T(8,128)(2,1)S(1)}, u32[]{:S(2)}, u32[]{:S(2)}) collective-permute-start(bf16[6,128,256]{2,1,0:T(8,128)(2,1)S(1)} %gather_step.1.refs_0_.p0), channel_id=1, source_target_pairs={{0,4},{1,17},{2,6},{3,19},{4,0},{5,21},{6,2},{7,23},{8,12},{9,25},... | collective-permute-start | bytes 1179656 | tf_op jit(solution)/shard_map/ppermute | solution.py:359
  53.4 9.7 %collective-permute-start.13 = (bf16[6,128,256]{2,1,0:T(8,128)(2,1)S(1)}, bf16[6,128,256]{2,1,0:T(8,128)(2,1)S(1)}, u32[]{:S(2)}, u32[]{:S(2)}) collective-permute-start(bf16[6,128,256]{2,1,0:T(8,128)(2,1)S(1)} %gather_step.1.refs_0_.p0), channel_id=1, source_target_pairs={{0,6},{1,25},{2,0},{3,27},{4,2},{5,29},{6,4},{7,31},{8,14},{9,1},{... | collective-permute-start | bytes 1179656 | tf_op jit(solution)/shard_map/ppermute | solution.py:359
  63.0 2.8 %collective-permute-start.17 = (bf16[6,128,256]{2,1,0:T(8,128)(2,1)S(1)}, bf16[6,128,256]{2,1,0:T(8,128)(2,1)S(1)}, u32[]{:S(2)}, u32[]{:S(2)}) collective-permute-start(bf16[6,128,256]{2,1,0:T(8,128)(2,1)S(1)} %get-tuple-element.37.refs_0_.p1), channel_id=1, source_target_pairs={{0,1},{1,0},{2,3},{3,2},{4,5},{5,4},{6,7},{7,6},{8,9},{9,8},{10,11... | collective-permute-start | bytes 1179656 | tf_op jit(solution)/shard_map/ppermute | solution.py:346
  64.0 1.9 %collective-permute-start.18 = (bf16[6,128,256]{2,1,0:T(8,128)(2,1)S(1)}, bf16[6,128,256]{2,1,0:T(8,128)(2,1)S(1)}, u32[]{:S(2)}, u32[]{:S(2)}) collective-permute-start(bf16[6,128,256]{2,1,0:T(8,128)(2,1)S(1)} %get-tuple-element.38.refs_1_.p2), channel_id=1, source_target_pairs={{0,1},{1,0},{2,3},{3,2},{4,5},{5,4},{6,7},{7,6},{8,9},{9,8},{10,11... | collective-permute-start | bytes 1179656 | tf_op jit(solution)/shard_map/ppermute | solution.py:346
  64.1 2.4 %collective-permute-start.19 = (bf16[6,128,256]{2,1,0:T(8,128)(2,1)S(1)}, bf16[6,128,256]{2,1,0:T(8,128)(2,1)S(1)}, u32[]{:S(2)}, u32[]{:S(2)}) collective-permute-start(bf16[6,128,256]{2,1,0:T(8,128)(2,1)S(1)} %get-tuple-element.39.refs_2_.p3), channel_id=1, source_target_pairs={{0,1},{1,0},{2,3},{3,2},{4,5},{5,4},{6,7},{7,6},{8,9},{9,8},{10,11... | collective-permute-start | bytes 1179656 | tf_op jit(solution)/shard_map/ppermute | solution.py:346
  68.0 6.2 %collective-permute-start.20 = (bf16[3,128,256]{2,1,0:T(8,128)(2,1)S(1)}, bf16[3,128,256]{2,1,0:T(8,128)(2,1)S(1)}, u32[]{:S(2)}, u32[]{:S(2)}) collective-permute-start(bf16[3,128,256]{2,1,0:T(8,128)(2,1)S(1)} %get-tuple-element.42), channel_id=1, source_target_pairs={{0,96},{32,0},{64,32},{96,64},{1,97},{33,1},{65,33},{97,65},{2,98}... | collective-permute-start | bytes 589832 | tf_op jit(solution)/shard_map/ppermute | solution.py:342
  68.8 7.3 %collective-permute-start.21 = (bf16[3,128,256]{2,1,0:T(8,128)(2,1)S(1)}, bf16[3,128,256]{2,1,0:T(8,128)(2,1)S(1)}, u32[]{:S(2)}, u32[]{:S(2)}) collective-permute-start(bf16[3,128,256]{2,1,0:T(8,128)(2,1)S(1)} %get-tuple-element.43), channel_id=1, source_target_pairs={{0,64},{32,96},{64,0},{96,32},{1,65},{33,97},{65,1},{97,33},{2,66}... | collective-permute-start | bytes 589832 | tf_op jit(solution)/shard_map/ppermute | solution.py:342
  70.2 11.2 %collective-permute-start.22 = (bf16[3,128,256]{2,1,0:T(8,128)(2,1)S(1)}, bf16[3,128,256]{2,1,0:T(8,128)(2,1)S(1)}, u32[]{:S(2)}, u32[]{:S(2)}) collective-permute-start(bf16[3,128,256]{2,1,0:T(8,128)(2,1)S(1)} %get-tuple-element.44), channel_id=1, source_target_pairs={{0,32},{32,64},{64,96},{96,0},{1,33},{33,65},{65,97},{97,1},{2,34}... | collective-permute-start | bytes 589832 | tf_op jit(solution)/shard_map/ppermute | solution.py:342

commit v3 on v2

--- a/solution.py
+++ b/solution.py
@@ -16,8 +16,8 @@
 PARAMS = pltpu.CompilerParams(vmem_limit_bytes=24 << 20)
 
 FWD_TILES = 4
-COL_TERMS = 2
-ROW_TERMS = 2
+COL_TERMS = 1
+ROW_TERMS = 1
 
 
 def sds(shape, dtype):
@@ -114,7 +114,7 @@
     )(*given, live)
 
 
-def forward_kernel(start, steps, table, values, x0, x1, x2, x3, out):
+def forward_kernel(start, steps, table, values, x0, x1, x3, x2, out):
     sources = (x0, x1, x2, x3)
     rows = FWD_TILES * 128
     for step in range(steps):
@@ -147,7 +147,7 @@
     )(table, values, *sources)
 
 
-def first_sum_kernel(kept, got, s1, s2, s3):
+def first_sum_kernel(kept, got, s1, s3, s2):
     for a, out in enumerate((s1, s2, s3)):
         total = kept[a * 1024 : a * 1024 + 1024, :] + got[a * 1024 + 1024 : a * 1024 + 2048, :].astype(F32)
         out[...] = total.astype(BF)
@@ -164,7 +164,7 @@
     )(kept, got)
 
 
-def second_sum_kernel(own, other, g1, g2, g3, mine, s1, s2, s3):
+def second_sum_kernel(own, other, g1, g3, g2, mine, s1, s3, s2):
     for b, out in enumerate((mine, s1, s2, s3)):
         part = pl.ds(b * 256, 256)
         total = own[part, :] + other[part, :].astype(F32) + g1[part, :].astype(F32)
@@ -183,7 +183,7 @@
     )(own, other, *got)
 
 
-def middle_kernel(own, g1, g2, g3, weight, cotangent, out, message):
+def middle_kernel(own, g1, g3, g2, weight, cotangent, out, message):
     mixed = own[...] + g1[...].astype(F32) + g2[...].astype(F32) + g3[...].astype(F32)
     high, low = split(mixed)
     w = weight[...]
@@ -216,7 +216,7 @@
     return (own + g2) + (g1 + g3)
 
 
-def gather_kernel(own, g1, g2, g3, message):
+def gather_kernel(own, g3, g1, g2, message):
     for b, ref in enumerate((own, g1, g2, g3)):
         message[b] = ref[0]
     for n, term in enumerate(split(ring_sum(own, g1, g2, g3, 1), COL_TERMS)):
@@ -288,7 +288,7 @@
     )(*values, after)
 
 
-def last_kernel(half, offsets, table, values, p0, p1, p2, p3, o0, o1, o2, o3, partial, own, own_term, s1, s2, s3):
+def last_kernel(half, offsets, table, values, p0, p3, p1, p2, o0, o3, o1, o2, partial, own, own_term, s3, s1, s2):
     sends = (s1, s2, s3)
     parts = [(o0, o1, o2, o3)[a] for a in offsets]
     term = ring_sum(p0, p1, p2, p3, 4, COL_TERMS) + ring_sum(o0, o1, o2, o3, 4, COL_TERMS)
@@ -319,7 +319,7 @@
     )(table, values, *mine, *others, partial)
 
 
-def finish_kernel(scale, own, own_term, g1, g2, g3, grad_in, grad_weight):
+def finish_kernel(scale, own, own_term, g3, g1, g2, grad_in, grad_weight):
     total = own[...] + g1[0].astype(F32) + g2[0].astype(F32) + g3[0].astype(F32)
     grad_in[...] = total.T.astype(BF)
     g1, g2, g3 = [joined(ref, 1, ROW_TERMS) for ref in (g1, g2, g3)]
@@ -359,32 +359,39 @@
     return lax.ppermute(value, "col", pairs)
 
 
+ORDER = {1: (1, 3, 2), -1: (3, 1, 2)}
+
+
+def shift_each(shift, values, sign, *args):
+    return [shift(v, sign * k, *args) for k, v in zip(ORDER[sign], values)]
+
+
 def local(features, weight, cotangent, tile_values, tile_rows, tile_cols, tile_counts):
-    shifted = [row_shift(features, k) for k in (1, 2, 3)]
+    shifted = shift_each(row_shift, [features] * 3, 1)
     values, own_features, table = load(
         tile_values[0, 0], features, tile_rows, tile_cols, tile_counts
     )
     sources = [own_features] + shifted
     other = swap_cores(forward("forward_other", 0, 32, BF, table, values, sources))
     kept = forward("forward_sent", 40, 24, F32, table, values, sources)
-    sends = first_sum(kept, other)
-    got = [chip_shift(v, k, 0) for k, v in zip((1, 2, 3), sends)]
+    got = shift_each(chip_shift, first_sum(kept, other), 1, 0)
     kept = forward("forward_kept", 32, 8, F32, table, values, sources)
     own, *sends = second_sum(kept, other, got)
-    got = [chip_shift(v, k, 1) for k, v in zip((1, 2, 3), sends)]
+    got = shift_each(chip_shift, sends, 1, 1)
     output, message = middle(own, got, weight, cotangent)
-    got = [chip_shift(message, -k, 1) for k in (1, 2, 3)]
+    got = shift_each(chip_shift, [message] * 3, -1, 1)
     message = gather_step(message, got)
-    p0, p1, p2, p3 = [message] + [chip_shift(message, -k, 0) for k in (1, 2, 3)]
-    o0 = swap_cores(p0)
-    partial = backward(1, (0,), table, values, (p0,), None)
-    partial = backward(0, (0,), table, values, (o0,), partial)
-    p1, p2, p3 = tie((p1, p2, p3), partial)
-    o1, o2, o3 = [swap_cores(v) for v in (p1, p2, p3)]
-    partial = backward(1, (1, 2, 3), table, values, (p1, p2, p3), partial)
-    mine, others = (p0, p1, p2, p3), (o0, o1, o2, o3)
-    own, own_term, *sends = last(0, (1, 2, 3), table, values, mine, others, partial)
-    got = [row_shift(v, -k) for k, v in zip((1, 2, 3), sends)]
+    first = message
+    rest = shift_each(chip_shift, [message] * 3, -1, 0)
+    other_first = swap_cores(first)
+    partial = backward(1, (0,), table, values, (first,), None)
+    partial = backward(0, (0,), table, values, (other_first,), partial)
+    rest = tie(rest, partial)
+    other_rest = [swap_cores(v) for v in rest]
+    partial = backward(1, ORDER[-1], table, values, rest, partial)
+    mine, others = (first, *rest), (other_first, *other_rest)
+    own, own_term, *sends = last(0, ORDER[-1], table, values, mine, others, partial)
+    got = shift_each(row_shift, sends, -1)
     grad_in, grad_weight = finish(32768.0 ** -0.5, own, own_term, got)
     return output, grad_in, grad_weight
 

time: 82.3 us -> 76.2 us (0.926)
  waiting for transfers between devices: 32.6 us -> 28.1 us
  starting transfers between devices: 33.1 us -> 30.9 us
    ppermute x6, waiting for transfers between devices: 11.2 us -> 4.87 us  [row_shift(): return lax.ppermute(value, 'row', [(i, (i + k) % 4) for i in range(4)])]
    ppermute x12, starting transfers between devices: 18.1 us -> 14.6 us  [chip_shift(): return lax.ppermute(value, 'col', pairs)]
    ppermute x12, waiting for transfers between devices: 20.4 us -> 22.4 us  [chip_shift(): return lax.ppermute(value, 'col', pairs)]
    ppermute x6, starting transfers between devices: 7.53 us -> 8.48 us  [row_shift(): return lax.ppermute(value, 'row', [(i, (i + k) % 4) for i in range(4)])]
  transfers between devices with their start and end apart: 23 -> 23, of which waited for: 13 -> 16; matrix products, arithmetic and copies ran while one was open for 0% -> 0% of each run, Pallas kernels for 11% -> 12%
where the time goes in v3:
time: 76.2 us; the launch traced here: 75.3 us
  starting transfers between devices  30.9 us (41%)
  waiting for transfers between devices  28.1 us (37%)
  Pallas kernels  14.9 us (20%)
  between operations  1.44 us (2%)
    ppermute x12, waiting for transfers between devices, chip_shift(): return lax.ppermute(value, 'col', pairs)  22.4 us
    ppermute x12, starting transfers between devices, chip_shift(): return lax.ppermute(value, 'col', pairs)  14.6 us
    ppermute x6, starting transfers between devices, row_shift(): return lax.ppermute(value, 'row', [(i, (i + k) % 4) for i in range(4)])  8.48 us
    ppermute x5, starting transfers between devices, swap_cores(): return lax.ppermute(value, 'col', [(j, j ^ 1) for j in range(32)])  7.85 us
    ppermute x6, waiting for transfers between devices, row_shift(): return lax.ppermute(value, 'row', [(i, (i + k) % 4) for i in range(4)])  4.87 us
    pallas_call x3, Pallas kernels, forward(): pl.pallas_call(functools.partial(forward_kernel, start, count // FWD_TILE...  4.82 us
    pallas_call x1, Pallas kernels, load(): pl.pallas_call(load_kernel, out_shape=(sds(values.shape, BF), sds(feature...  4.02 us
    pallas_call x3, Pallas kernels, backward(): pl.pallas_call(functools.partial(backward_kernel, half, offsets, partial...  2.47 us
  transfers between devices with their start and end apart: 23, of which 16 were waited for; matrix products, arithmetic and copies ran while one was open for 0% of the time, Pallas kernels for 12%

profile of v3, /device:TPU:1, one launch (start us, length us, event | category | flops | bytes accessed | tf_op | source)
XLA Modules:
  0.0 75.3 jit_solution(11786906965180741613)
XLA Ops:
  0.6 2.2 %collective-permute-start = (bf16[256,128]{1,0:T(8,128)(2,1)}, bf16[256,128]{1,0:T(8,128)(2,1)S(1)}, u32[]{:S(2)}, u32[]{:S(2)}) collective-permute-start(bf16[256,128]{1,0:T(8,128)(2,1)} %features.1), channel_id=1, source_target_pairs={{0,32},{32,64},{64,96},{96,0},{1,33},{33,65},{65,97},{97,1},{2,34}... | collective-permute-start | bytes 196616 | tf_op jit(solution)/shard_map/ppermute | solution.py:342
  2.8 1.5 %collective-permute-start.1 = (bf16[256,128]{1,0:T(8,128)(2,1)}, bf16[256,128]{1,0:T(8,128)(2,1)S(1)}, u32[]{:S(2)}, u32[]{:S(2)}) collective-permute-start(bf16[256,128]{1,0:T(8,128)(2,1)} %features.1), channel_id=1, source_target_pairs={{0,96},{32,0},{64,32},{96,64},{1,97},{33,1},{65,33},{97,65},{2,98}... | collective-permute-start | bytes 196616 | tf_op jit(solution)/shard_map/ppermute | solution.py:342
  4.3 1.6 %collective-permute-start.2 = (bf16[256,128]{1,0:T(8,128)(2,1)}, bf16[256,128]{1,0:T(8,128)(2,1)S(1)}, u32[]{:S(2)}, u32[]{:S(2)}) collective-permute-start(bf16[256,128]{1,0:T(8,128)(2,1)} %features.1), channel_id=1, source_target_pairs={{0,64},{32,96},{64,0},{96,32},{1,65},{33,97},{65,1},{97,33},{2,66}... | collective-permute-start | bytes 196616 | tf_op jit(solution)/shard_map/ppermute | solution.py:342
  6.6 4.0 %load.1 = (bf16[320,128,128]{2,1,0:T(8,128)(2,1)S(1)}, bf16[256,128]{1,0:T(8,128)(2,1)S(1)}, s32[512]{0:T(512)S(4)}) custom-call(bf16[320,128,128]{2,1,0:T(8,128)(2,1)} %bitcast.1, bf16[256,128]{1,0:T(8,128)(2,1)} %features.1, s32[1,1,320]{2,1,0:T(1,128)} %rows_in.1, s32[1,1,320]{2,1,0:T(1,128)} %cols_in.1, s32[1,1]{1,0:T(1,128)S(6)} %copy.16.live), custom_call_target="tpu_custom_call" | custom-call | bytes 11534336 | tf_op jit(solution)/shard_map/load/pallas_call | solution.py:101
  10.6 2.3 %forward_other.1 = bf16[4096,128]{1,0:T(8,128)(2,1)S(1)} custom-call(s32[512]{0:T(512)S(4)} %get-tuple-element.25.table, bf16[320,128,128]{2,1,0:T(8,128)(2,1)S(1)} %get-tuple-element.26.values, bf16[256,128]{1,0:T(8,128)(2,1)S(1)} %get-tuple-element.27.x0, bf16[256,128]{1,0:T(8,128)(2,1)S(1)} %collective-permute-done.x1, ...), custom_call_target="tpu_custom_call" | custom-call | flops 1073741824 | bytes 1048576 | tf_op jit(solution)/shard_map/forward_other/pallas_call | solution.py:137
  13.0 1.6 %collective-permute-start.3 = (bf16[4096,128]{1,0:T(8,128)(2,1)S(1)}, bf16[4096,128]{1,0:T(8,128)(2,1)S(1)}, u32[]{:S(2)}, u32[]{:S(2)}) collective-permute-start(bf16[4096,128]{1,0:T(8,128)(2,1)S(1)} %forward_other.1), channel_id=1, source_target_pairs={{0,1},{1,0},{2,3},{3,2},{4,5},{5,4},{6,7},{7,6},{8,9},{9,8},{10,11... | collective-permute-start | bytes 3145736 | tf_op jit(solution)/shard_map/ppermute | solution.py:346
  14.6 1.8 %forward_sent.1.kept = f32[3072,128]{1,0:T(8,128)S(1)} custom-call(s32[512]{0:T(512)S(4)} %get-tuple-element.25.table, bf16[320,128,128]{2,1,0:T(8,128)(2,1)S(1)} %get-tuple-element.26.values, bf16[256,128]{1,0:T(8,128)(2,1)S(1)} %get-tuple-element.27.x0, bf16[256,128]{1,0:T(8,128)(2,1)S(1)} %collective-permute-done.x1, ...), custom_call_target="tpu_custom_call" | custom-call | flops 805306368 | bytes 786432 | tf_op jit(solution)/shard_map/forward_sent/pallas_call | solution.py:137
  17.0 1.7 %collective-permute-start.4 = (bf16[1024,128]{1,0:T(8,128)(2,1)S(1)}, bf16[1024,128]{1,0:T(8,128)(2,1)S(1)}, u32[]{:S(2)}, u32[]{:S(2)}) collective-permute-start(bf16[1024,128]{1,0:T(8,128)(2,1)S(1)} %get-tuple-element.28), channel_id=1, source_target_pairs={{0,2},{1,9},{2,4},{3,11},{4,6},{5,13},{6,0},{7,15},{8,10},{9,17},{... | collective-permute-start | bytes 786440 | tf_op jit(solution)/shard_map/ppermute | solution.py:359
  18.7 2.2 %collective-permute-start.5 = (bf16[1024,128]{1,0:T(8,128)(2,1)S(1)}, bf16[1024,128]{1,0:T(8,128)(2,1)S(1)}, u32[]{:S(2)}, u32[]{:S(2)}) collective-permute-start(bf16[1024,128]{1,0:T(8,128)(2,1)S(1)} %get-tuple-element.29), channel_id=1, source_target_pairs={{0,6},{1,25},{2,0},{3,27},{4,2},{5,29},{6,4},{7,31},{8,14},{9,1},{... | collective-permute-start | bytes 786440 | tf_op jit(solution)/shard_map/ppermute | solution.py:359
  20.9 1.2 %collective-permute-start.6 = (bf16[1024,128]{1,0:T(8,128)(2,1)S(1)}, bf16[1024,128]{1,0:T(8,128)(2,1)S(1)}, u32[]{:S(2)}, u32[]{:S(2)}) collective-permute-start(bf16[1024,128]{1,0:T(8,128)(2,1)S(1)} %get-tuple-element.30), channel_id=1, source_target_pairs={{0,4},{1,17},{2,6},{3,19},{4,0},{5,21},{6,2},{7,23},{8,12},{9,25},... | collective-permute-start | bytes 786440 | tf_op jit(solution)/shard_map/ppermute | solution.py:359
  22.8 1.8 %collective-permute-done.4.g1 = bf16[1024,128]{1,0:T(8,128)(2,1)S(1)} collective-permute-done((bf16[1024,128]{1,0:T(8,128)(2,1)S(1)}, bf16[1024,128]{1,0:T(8,128)(2,1)S(1)}, u32[]{:S(2)}, u32[]{:S(2)}) %collective-permute-start.4) | collective-permute-done | bytes 262176 | tf_op jit(solution)/shard_map/ppermute | solution.py:359
  24.6 2.4 %collective-permute-done.5.g3 = bf16[1024,128]{1,0:T(8,128)(2,1)S(1)} collective-permute-done((bf16[1024,128]{1,0:T(8,128)(2,1)S(1)}, bf16[1024,128]{1,0:T(8,128)(2,1)S(1)}, u32[]{:S(2)}, u32[]{:S(2)}) %collective-permute-start.5) | collective-permute-done | bytes 262176 | tf_op jit(solution)/shard_map/ppermute | solution.py:359
  27.0 1.8 %collective-permute-done.6.g2 = bf16[1024,128]{1,0:T(8,128)(2,1)S(1)} collective-permute-done((bf16[1024,128]{1,0:T(8,128)(2,1)S(1)}, bf16[1024,128]{1,0:T(8,128)(2,1)S(1)}, u32[]{:S(2)}, u32[]{:S(2)}) %collective-permute-start.6) | collective-permute-done | bytes 262176 | tf_op jit(solution)/shard_map/ppermute | solution.py:359
  29.0 1.0 %collective-permute-start.7 = (bf16[256,128]{1,0:T(8,128)(2,1)S(1)}, bf16[256,128]{1,0:T(8,128)(2,1)S(1)}, u32[]{:S(2)}, u32[]{:S(2)}) collective-permute-start(bf16[256,128]{1,0:T(8,128)(2,1)S(1)} %get-tuple-element.32), channel_id=1, source_target_pairs={{0,8},{1,3},{2,10},{3,5},{4,12},{5,7},{6,14},{7,1},{8,16},{9,11},{... | collective-permute-start | bytes 196616 | tf_op jit(solution)/shard_map/ppermute | solution.py:359
  30.0 1.7 %collective-permute-start.8 = (bf16[256,128]{1,0:T(8,128)(2,1)S(1)}, bf16[256,128]{1,0:T(8,128)(2,1)S(1)}, u32[]{:S(2)}, u32[]{:S(2)}) collective-permute-start(bf16[256,128]{1,0:T(8,128)(2,1)S(1)} %get-tuple-element.33), channel_id=1, source_target_pairs={{0,24},{1,7},{2,26},{3,1},{4,28},{5,3},{6,30},{7,5},{8,0},{9,15},{... | collective-permute-start | bytes 196616 | tf_op jit(solution)/shard_map/ppermute | solution.py:359
  31.7 1.3 %collective-permute-start.9 = (bf16[256,128]{1,0:T(8,128)(2,1)S(1)}, bf16[256,128]{1,0:T(8,128)(2,1)S(1)}, u32[]{:S(2)}, u32[]{:S(2)}) collective-permute-start(bf16[256,128]{1,0:T(8,128)(2,1)S(1)} %get-tuple-element.34), channel_id=1, source_target_pairs={{0,16},{1,5},{2,18},{3,7},{4,20},{5,1},{6,22},{7,3},{8,24},{9,13},... | collective-permute-start | bytes 196616 | tf_op jit(solution)/shard_map/ppermute | solution.py:359
  33.4 3.0 %collective-permute-done.9.g2 = bf16[256,128]{1,0:T(8,128)(2,1)S(1)} collective-permute-done((bf16[256,128]{1,0:T(8,128)(2,1)S(1)}, bf16[256,128]{1,0:T(8,128)(2,1)S(1)}, u32[]{:S(2)}, u32[]{:S(2)}) %collective-permute-start.9) | collective-permute-done | bytes 65568 | tf_op jit(solution)/shard_map/ppermute | solution.py:359
  36.3 1.0 %middle.1 = (bf16[256,256]{1,0:T(8,128)(2,1)}, bf16[3,128,256]{2,1,0:T(8,128)(2,1)S(1)}) custom-call(f32[256,128]{1,0:T(8,128)S(1)} %get-tuple-element.31.own, bf16[256,128]{1,0:T(8,128)(2,1)S(1)} %collective-permute-done.7.g1, bf16[256,128]{1,0:T(8,128)(2,1)S(1)} %collective-permute-done.8.g3, bf16[256,128]{1,0:T(8,128)(2,1)S(1)} %collective-permute-done.9.g2, ...), custom_call_target="tpu_custom_call" | custom-call | tf_op jit(solution)/shard_map/middle/pallas_call | solution.py:204
  37.3 2.7 %collective-permute-start.11 = (bf16[3,128,256]{2,1,0:T(8,128)(2,1)S(1)}, bf16[3,128,256]{2,1,0:T(8,128)(2,1)S(1)}, u32[]{:S(2)}, u32[]{:S(2)}) collective-permute-start(bf16[3,128,256]{2,1,0:T(8,128)(2,1)S(1)} %get-tuple-element.36.own), channel_id=1, source_target_pairs={{0,24},{1,7},{2,26},{3,1},{4,28},{5,3},{6,30},{7,5},{8,0},{9,15},{... | collective-permute-start | bytes 589832 | tf_op jit(solution)/shard_map/ppermute | solution.py:359
  40.0 3.0 %collective-permute-done.10.g3 = bf16[3,128,256]{2,1,0:T(8,128)(2,1)S(1)} collective-permute-done((bf16[3,128,256]{2,1,0:T(8,128)(2,1)S(1)}, bf16[3,128,256]{2,1,0:T(8,128)(2,1)S(1)}, u32[]{:S(2)}, u32[]{:S(2)}) %collective-permute-start.10) | collective-permute-done | bytes 196640 | tf_op jit(solution)/shard_map/ppermute | solution.py:359
  43.0 1.7 %collective-permute-done.11.g1 = bf16[3,128,256]{2,1,0:T(8,128)(2,1)S(1)} collective-permute-done((bf16[3,128,256]{2,1,0:T(8,128)(2,1)S(1)}, bf16[3,128,256]{2,1,0:T(8,128)(2,1)S(1)}, u32[]{:S(2)}, u32[]{:S(2)}) %collective-permute-start.11) | collective-permute-done | bytes 196640 | tf_op jit(solution)/shard_map/ppermute | solution.py:359
  44.7 1.3 %collective-permute-done.12.g2 = bf16[3,128,256]{2,1,0:T(8,128)(2,1)S(1)} collective-permute-done((bf16[3,128,256]{2,1,0:T(8,128)(2,1)S(1)}, bf16[3,128,256]{2,1,0:T(8,128)(2,1)S(1)}, u32[]{:S(2)}, u32[]{:S(2)}) %collective-permute-start.12) | collective-permute-done | bytes 196640 | tf_op jit(solution)/shard_map/ppermute | solution.py:359
  46.1 4.4 %collective-permute-start.16 = (bf16[5,128,256]{2,1,0:T(8,128)(2,1)S(1)}, bf16[5,128,256]{2,1,0:T(8,128)(2,1)S(1)}, u32[]{:S(2)}, u32[]{:S(2)}) collective-permute-start(bf16[5,128,256]{2,1,0:T(8,128)(2,1)S(1)} %gather_step.1.refs_0_.p0), channel_id=1, source_target_pairs={{0,1},{1,0},{2,3},{3,2},{4,5},{5,4},{6,7},{7,6},{8,9},{9,8},{10,11... | collective-permute-start | bytes 983048 | tf_op jit(solution)/shard_map/ppermute | solution.py:346
  50.5 2.7 %collective-permute-start.14 = (bf16[5,128,256]{2,1,0:T(8,128)(2,1)S(1)}, bf16[5,128,256]{2,1,0:T(8,128)(2,1)S(1)}, u32[]{:S(2)}, u32[]{:S(2)}) collective-permute-start(bf16[5,128,256]{2,1,0:T(8,128)(2,1)S(1)} %gather_step.1.refs_0_.p0), channel_id=1, source_target_pairs={{0,6},{1,25},{2,0},{3,27},{4,2},{5,29},{6,4},{7,31},{8,14},{9,1},{... | collective-permute-start | bytes 983048 | tf_op jit(solution)/shard_map/ppermute | solution.py:359
  54.3 3.6 %collective-permute-done.13.refs_0_ = bf16[5,128,256]{2,1,0:T(8,128)(2,1)S(1)} collective-permute-done((bf16[5,128,256]{2,1,0:T(8,128)(2,1)S(1)}, bf16[5,128,256]{2,1,0:T(8,128)(2,1)S(1)}, u32[]{:S(2)}, u32[]{:S(2)}) %collective-permute-start.13) | collective-permute-done | bytes 327712 | tf_op jit(solution)/shard_map/ppermute | solution.py:359
  57.9 2.8 %collective-permute-done.14.refs_1_ = bf16[5,128,256]{2,1,0:T(8,128)(2,1)S(1)} collective-permute-done((bf16[5,128,256]{2,1,0:T(8,128)(2,1)S(1)}, bf16[5,128,256]{2,1,0:T(8,128)(2,1)S(1)}, u32[]{:S(2)}, u32[]{:S(2)}) %collective-permute-start.14) | collective-permute-done | bytes 327712 | tf_op jit(solution)/shard_map/ppermute | solution.py:359
  61.5 1.4 %collective-permute-start.17 = (bf16[5,128,256]{2,1,0:T(8,128)(2,1)S(1)}, bf16[5,128,256]{2,1,0:T(8,128)(2,1)S(1)}, u32[]{:S(2)}, u32[]{:S(2)}) collective-permute-start(bf16[5,128,256]{2,1,0:T(8,128)(2,1)S(1)} %get-tuple-element.37.refs_0_.p3), channel_id=1, source_target_pairs={{0,1},{1,0},{2,3},{3,2},{4,5},{5,4},{6,7},{7,6},{8,9},{9,8},{10,11... | collective-permute-start | bytes 983048 | tf_op jit(solution)/shard_map/ppermute | solution.py:346
  63.3 1.4 %backward_1_3.1.partial = f32[4,128,256]{2,1,0:T(8,128)S(1)} custom-call(s32[512]{0:T(512)S(4)} %get-tuple-element.25.table, bf16[320,128,128]{2,1,0:T(8,128)(2,1)S(1)} %get-tuple-element.26.values, bf16[5,128,256]{2,1,0:T(8,128)(2,1)S(1)} %get-tuple-element.37.refs_0_.p3, bf16[5,128,256]{2,1,0:T(8,128)(2,1)S(1)} %get-tuple-element.38.refs_1_.p1, ...), custom_call_target="tpu_custom_call" | custom-call | flops 1 | bytes 1 | tf_op jit(solution)/shard_map/backward_1_3/pallas_call | solution.py:264
  65.0 1.5 %backward_last.1 = (f32[128,256]{1,0:T(8,128)S(1)}, bf16[1,128,256]{2,1,0:T(8,128)(2,1)S(1)}, bf16[2,128,256]{2,1,0:T(8,128)(2,1)S(1)}, bf16[2,128,256]{2,1,0:T(8,128)(2,1)S(1)}, bf16[2,128,256]{2,1,0:T(8,128)(2,1)S(1)}) custom-call(s32[512]{0:T(512)S(4)} %get-tuple-element.25.table, bf16[320,128,128]{2,1,0:T(8,128)(2,1)S(1)} %get-tuple-element.26.values, ...), custom_call_target="tpu_custom_call" | custom-call | flops 1 | bytes 1 | tf_op jit(solution)/shard_map/backward_last/pallas_call | solution.py:310
  66.9 2.3 %collective-permute-start.21 = (bf16[2,128,256]{2,1,0:T(8,128)(2,1)S(1)}, bf16[2,128,256]{2,1,0:T(8,128)(2,1)S(1)}, u32[]{:S(2)}, u32[]{:S(2)}) collective-permute-start(bf16[2,128,256]{2,1,0:T(8,128)(2,1)S(1)} %get-tuple-element.43), channel_id=1, source_target_pairs={{0,96},{32,0},{64,32},{96,64},{1,97},{33,1},{65,33},{97,65},{2,98}... | collective-permute-start | bytes 393224 | tf_op jit(solution)/shard_map/ppermute | solution.py:342
  69.7 2.8 %collective-permute-done.20.g3 = bf16[2,128,256]{2,1,0:T(8,128)(2,1)S(1)} collective-permute-done((bf16[2,128,256]{2,1,0:T(8,128)(2,1)S(1)}, bf16[2,128,256]{2,1,0:T(8,128)(2,1)S(1)}, u32[]{:S(2)}, u32[]{:S(2)}) %collective-permute-start.20) | collective-permute-done | bytes 131104 | tf_op jit(solution)/shard_map/ppermute | solution.py:342
  72.5 2.0 %collective-permute-done.22.g2 = bf16[2,128,256]{2,1,0:T(8,128)(2,1)S(1)} collective-permute-done((bf16[2,128,256]{2,1,0:T(8,128)(2,1)S(1)}, bf16[2,128,256]{2,1,0:T(8,128)(2,1)S(1)}, u32[]{:S(2)}, u32[]{:S(2)}) %collective-permute-start.22) | collective-permute-done | bytes 131104 | tf_op jit(solution)/shard_map/ppermute | solution.py:342
  (32 shorter events, 6.5 us)
Async XLA Ops:
  0.6 10.0 %collective-permute-start = (bf16[256,128]{1,0:T(8,128)(2,1)}, bf16[256,128]{1,0:T(8,128)(2,1)S(1)}, u32[]{:S(2)}, u32[]{:S(2)}) collective-permute-start(bf16[256,128]{1,0:T(8,128)(2,1)} %features.1), channel_id=1, source_target_pairs={{0,32},{32,64},{64,96},{96,0},{1,33},{33,65},{65,97},{97,1},{2,34}... | collective-permute-start | bytes 196616 | tf_op jit(solution)/shard_map/ppermute | solution.py:342
  2.8 7.8 %collective-permute-start.1 = (bf16[256,128]{1,0:T(8,128)(2,1)}, bf16[256,128]{1,0:T(8,128)(2,1)S(1)}, u32[]{:S(2)}, u32[]{:S(2)}) collective-permute-start(bf16[256,128]{1,0:T(8,128)(2,1)} %features.1), channel_id=1, source_target_pairs={{0,96},{32,0},{64,32},{96,64},{1,97},{33,1},{65,33},{97,65},{2,98}... | collective-permute-start | bytes 196616 | tf_op jit(solution)/shard_map/ppermute | solution.py:342
  4.3 6.3 %collective-permute-start.2 = (bf16[256,128]{1,0:T(8,128)(2,1)}, bf16[256,128]{1,0:T(8,128)(2,1)S(1)}, u32[]{:S(2)}, u32[]{:S(2)}) collective-permute-start(bf16[256,128]{1,0:T(8,128)(2,1)} %features.1), channel_id=1, source_target_pairs={{0,64},{32,96},{64,0},{96,32},{1,65},{33,97},{65,1},{97,33},{2,66}... | collective-permute-start | bytes 196616 | tf_op jit(solution)/shard_map/ppermute | solution.py:342
  13.0 3.9 %collective-permute-start.3 = (bf16[4096,128]{1,0:T(8,128)(2,1)S(1)}, bf16[4096,128]{1,0:T(8,128)(2,1)S(1)}, u32[]{:S(2)}, u32[]{:S(2)}) collective-permute-start(bf16[4096,128]{1,0:T(8,128)(2,1)S(1)} %forward_other.1), channel_id=1, source_target_pairs={{0,1},{1,0},{2,3},{3,2},{4,5},{5,4},{6,7},{7,6},{8,9},{9,8},{10,11... | collective-permute-start | bytes 3145736 | tf_op jit(solution)/shard_map/ppermute | solution.py:346
  16.3 20.0 %copy-start = (bf16[256,256]{1,0:T(8,128)(2,1)S(1)}, bf16[256,256]{1,0:T(8,128)(2,1)}, u32[]{:S(2)}) copy-start(bf16[256,256]{1,0:T(8,128)(2,1)} %cotangent.1) | copy-start | bytes 393220
  16.4 20.0 %copy-start.1 = (bf16[128,256]{1,0:T(8,128)(2,1)S(1)}, bf16[128,256]{1,0:T(8,128)(2,1)}, u32[]{:S(2)}) copy-start(bf16[128,256]{1,0:T(8,128)(2,1)} %weight.1) | copy-start | bytes 196612
  17.0 7.6 %collective-permute-start.4 = (bf16[1024,128]{1,0:T(8,128)(2,1)S(1)}, bf16[1024,128]{1,0:T(8,128)(2,1)S(1)}, u32[]{:S(2)}, u32[]{:S(2)}) collective-permute-start(bf16[1024,128]{1,0:T(8,128)(2,1)S(1)} %get-tuple-element.28), channel_id=1, source_target_pairs={{0,2},{1,9},{2,4},{3,11},{4,6},{5,13},{6,0},{7,15},{8,10},{9,17},{... | collective-permute-start | bytes 786440 | tf_op jit(solution)/shard_map/ppermute | solution.py:359
  18.7 8.3 %collective-permute-start.5 = (bf16[1024,128]{1,0:T(8,128)(2,1)S(1)}, bf16[1024,128]{1,0:T(8,128)(2,1)S(1)}, u32[]{:S(2)}, u32[]{:S(2)}) collective-permute-start(bf16[1024,128]{1,0:T(8,128)(2,1)S(1)} %get-tuple-element.29), channel_id=1, source_target_pairs={{0,6},{1,25},{2,0},{3,27},{4,2},{5,29},{6,4},{7,31},{8,14},{9,1},{... | collective-permute-start | bytes 786440 | tf_op jit(solution)/shard_map/ppermute | solution.py:359
  20.9 7.9 %collective-permute-start.6 = (bf16[1024,128]{1,0:T(8,128)(2,1)S(1)}, bf16[1024,128]{1,0:T(8,128)(2,1)S(1)}, u32[]{:S(2)}, u32[]{:S(2)}) collective-permute-start(bf16[1024,128]{1,0:T(8,128)(2,1)S(1)} %get-tuple-element.30), channel_id=1, source_target_pairs={{0,4},{1,17},{2,6},{3,19},{4,0},{5,21},{6,2},{7,23},{8,12},{9,25},... | collective-permute-start | bytes 786440 | tf_op jit(solution)/shard_map/ppermute | solution.py:359
  29.0 4.4 %collective-permute-start.7 = (bf16[256,128]{1,0:T(8,128)(2,1)S(1)}, bf16[256,128]{1,0:T(8,128)(2,1)S(1)}, u32[]{:S(2)}, u32[]{:S(2)}) collective-permute-start(bf16[256,128]{1,0:T(8,128)(2,1)S(1)} %get-tuple-element.32), channel_id=1, source_target_pairs={{0,8},{1,3},{2,10},{3,5},{4,12},{5,7},{6,14},{7,1},{8,16},{9,11},{... | collective-permute-start | bytes 196616 | tf_op jit(solution)/shard_map/ppermute | solution.py:359
  30.0 3.4 %collective-permute-start.8 = (bf16[256,128]{1,0:T(8,128)(2,1)S(1)}, bf16[256,128]{1,0:T(8,128)(2,1)S(1)}, u32[]{:S(2)}, u32[]{:S(2)}) collective-permute-start(bf16[256,128]{1,0:T(8,128)(2,1)S(1)} %get-tuple-element.33), channel_id=1, source_target_pairs={{0,24},{1,7},{2,26},{3,1},{4,28},{5,3},{6,30},{7,5},{8,0},{9,15},{... | collective-permute-start | bytes 196616 | tf_op jit(solution)/shard_map/ppermute | solution.py:359
  31.7 4.6 %collective-permute-start.9 = (bf16[256,128]{1,0:T(8,128)(2,1)S(1)}, bf16[256,128]{1,0:T(8,128)(2,1)S(1)}, u32[]{:S(2)}, u32[]{:S(2)}) collective-permute-start(bf16[256,128]{1,0:T(8,128)(2,1)S(1)} %get-tuple-element.34), channel_id=1, source_target_pairs={{0,16},{1,5},{2,18},{3,7},{4,20},{5,1},{6,22},{7,3},{8,24},{9,13},... | collective-permute-start | bytes 196616 | tf_op jit(solution)/shard_map/ppermute | solution.py:359
  37.3 5.7 %collective-permute-start.10 = (bf16[3,128,256]{2,1,0:T(8,128)(2,1)S(1)}, bf16[3,128,256]{2,1,0:T(8,128)(2,1)S(1)}, u32[]{:S(2)}, u32[]{:S(2)}) collective-permute-start(bf16[3,128,256]{2,1,0:T(8,128)(2,1)S(1)} %get-tuple-element.36.own), channel_id=1, source_target_pairs={{0,8},{1,3},{2,10},{3,5},{4,12},{5,7},{6,14},{7,1},{8,16},{9,11},{... | collective-permute-start | bytes 589832 | tf_op jit(solution)/shard_map/ppermute | solution.py:359
  37.3 7.4 %collective-permute-start.11 = (bf16[3,128,256]{2,1,0:T(8,128)(2,1)S(1)}, bf16[3,128,256]{2,1,0:T(8,128)(2,1)S(1)}, u32[]{:S(2)}, u32[]{:S(2)}) collective-permute-start(bf16[3,128,256]{2,1,0:T(8,128)(2,1)S(1)} %get-tuple-element.36.own), channel_id=1, source_target_pairs={{0,24},{1,7},{2,26},{3,1},{4,28},{5,3},{6,30},{7,5},{8,0},{9,15},{... | collective-permute-start | bytes 589832 | tf_op jit(solution)/shard_map/ppermute | solution.py:359
  40.0 6.0 %collective-permute-start.12 = (bf16[3,128,256]{2,1,0:T(8,128)(2,1)S(1)}, bf16[3,128,256]{2,1,0:T(8,128)(2,1)S(1)}, u32[]{:S(2)}, u32[]{:S(2)}) collective-permute-start(bf16[3,128,256]{2,1,0:T(8,128)(2,1)S(1)} %get-tuple-element.36.own), channel_id=1, source_target_pairs={{0,16},{1,5},{2,18},{3,7},{4,20},{5,1},{6,22},{7,3},{8,24},{9,13},... | collective-permute-start | bytes 589832 | tf_op jit(solution)/shard_map/ppermute | solution.py:359
  46.1 7.7 %collective-permute-start.16 = (bf16[5,128,256]{2,1,0:T(8,128)(2,1)S(1)}, bf16[5,128,256]{2,1,0:T(8,128)(2,1)S(1)}, u32[]{:S(2)}, u32[]{:S(2)}) collective-permute-start(bf16[5,128,256]{2,1,0:T(8,128)(2,1)S(1)} %gather_step.1.refs_0_.p0), channel_id=1, source_target_pairs={{0,1},{1,0},{2,3},{3,2},{4,5},{5,4},{6,7},{7,6},{8,9},{9,8},{10,11... | collective-permute-start | bytes 983048 | tf_op jit(solution)/shard_map/ppermute | solution.py:346
  50.5 7.4 %collective-permute-start.13 = (bf16[5,128,256]{2,1,0:T(8,128)(2,1)S(1)}, bf16[5,128,256]{2,1,0:T(8,128)(2,1)S(1)}, u32[]{:S(2)}, u32[]{:S(2)}) collective-permute-start(bf16[5,128,256]{2,1,0:T(8,128)(2,1)S(1)} %gather_step.1.refs_0_.p0), channel_id=1, source_target_pairs={{0,2},{1,9},{2,4},{3,11},{4,6},{5,13},{6,0},{7,15},{8,10},{9,17},{... | collective-permute-start | bytes 983048 | tf_op jit(solution)/shard_map/ppermute | solution.py:359
  50.5 10.2 %collective-permute-start.14 = (bf16[5,128,256]{2,1,0:T(8,128)(2,1)S(1)}, bf16[5,128,256]{2,1,0:T(8,128)(2,1)S(1)}, u32[]{:S(2)}, u32[]{:S(2)}) collective-permute-start(bf16[5,128,256]{2,1,0:T(8,128)(2,1)S(1)} %gather_step.1.refs_0_.p0), channel_id=1, source_target_pairs={{0,6},{1,25},{2,0},{3,27},{4,2},{5,29},{6,4},{7,31},{8,14},{9,1},{... | collective-permute-start | bytes 983048 | tf_op jit(solution)/shard_map/ppermute | solution.py:359
  53.1 8.3 %collective-permute-start.15 = (bf16[5,128,256]{2,1,0:T(8,128)(2,1)S(1)}, bf16[5,128,256]{2,1,0:T(8,128)(2,1)S(1)}, u32[]{:S(2)}, u32[]{:S(2)}) collective-permute-start(bf16[5,128,256]{2,1,0:T(8,128)(2,1)S(1)} %gather_step.1.refs_0_.p0), channel_id=1, source_target_pairs={{0,4},{1,17},{2,6},{3,19},{4,0},{5,21},{6,2},{7,23},{8,12},{9,25},... | collective-permute-start | bytes 983048 | tf_op jit(solution)/shard_map/ppermute | solution.py:359
  61.5 3.3 %collective-permute-start.17 = (bf16[5,128,256]{2,1,0:T(8,128)(2,1)S(1)}, bf16[5,128,256]{2,1,0:T(8,128)(2,1)S(1)}, u32[]{:S(2)}, u32[]{:S(2)}) collective-permute-start(bf16[5,128,256]{2,1,0:T(8,128)(2,1)S(1)} %get-tuple-element.37.refs_0_.p3), channel_id=1, source_target_pairs={{0,1},{1,0},{2,3},{3,2},{4,5},{5,4},{6,7},{7,6},{8,9},{9,8},{10,11... | collective-permute-start | bytes 983048 | tf_op jit(solution)/shard_map/ppermute | solution.py:346
  62.8 1.9 %collective-permute-start.18 = (bf16[5,128,256]{2,1,0:T(8,128)(2,1)S(1)}, bf16[5,128,256]{2,1,0:T(8,128)(2,1)S(1)}, u32[]{:S(2)}, u32[]{:S(2)}) collective-permute-start(bf16[5,128,256]{2,1,0:T(8,128)(2,1)S(1)} %get-tuple-element.38.refs_1_.p1), channel_id=1, source_target_pairs={{0,1},{1,0},{2,3},{3,2},{4,5},{5,4},{6,7},{7,6},{8,9},{9,8},{10,11... | collective-permute-start | bytes 983048 | tf_op jit(solution)/shard_map/ppermute | solution.py:346
  62.8 2.2 %collective-permute-start.19 = (bf16[5,128,256]{2,1,0:T(8,128)(2,1)S(1)}, bf16[5,128,256]{2,1,0:T(8,128)(2,1)S(1)}, u32[]{:S(2)}, u32[]{:S(2)}) collective-permute-start(bf16[5,128,256]{2,1,0:T(8,128)(2,1)S(1)} %get-tuple-element.39.refs_2_.p2), channel_id=1, source_target_pairs={{0,1},{1,0},{2,3},{3,2},{4,5},{5,4},{6,7},{7,6},{8,9},{9,8},{10,11... | collective-permute-start | bytes 983048 | tf_op jit(solution)/shard_map/ppermute | solution.py:346
  66.5 6.0 %collective-permute-start.20 = (bf16[2,128,256]{2,1,0:T(8,128)(2,1)S(1)}, bf16[2,128,256]{2,1,0:T(8,128)(2,1)S(1)}, u32[]{:S(2)}, u32[]{:S(2)}) collective-permute-start(bf16[2,128,256]{2,1,0:T(8,128)(2,1)S(1)} %get-tuple-element.42), channel_id=1, source_target_pairs={{0,32},{32,64},{64,96},{96,0},{1,33},{33,65},{65,97},{97,1},{2,34}... | collective-permute-start | bytes 393224 | tf_op jit(solution)/shard_map/ppermute | solution.py:342
  66.9 5.6 %collective-permute-start.21 = (bf16[2,128,256]{2,1,0:T(8,128)(2,1)S(1)}, bf16[2,128,256]{2,1,0:T(8,128)(2,1)S(1)}, u32[]{:S(2)}, u32[]{:S(2)}) collective-permute-start(bf16[2,128,256]{2,1,0:T(8,128)(2,1)S(1)} %get-tuple-element.43), channel_id=1, source_target_pairs={{0,96},{32,0},{64,32},{96,64},{1,97},{33,1},{65,33},{97,65},{2,98}... | collective-permute-start | bytes 393224 | tf_op jit(solution)/shard_map/ppermute | solution.py:342
  69.2 5.3 %collective-permute-start.22 = (bf16[2,128,256]{2,1,0:T(8,128)(2,1)S(1)}, bf16[2,128,256]{2,1,0:T(8,128)(2,1)S(1)}, u32[]{:S(2)}, u32[]{:S(2)}) collective-permute-start(bf16[2,128,256]{2,1,0:T(8,128)(2,1)S(1)} %get-tuple-element.44), channel_id=1, source_target_pairs={{0,64},{32,96},{64,0},{96,32},{1,65},{33,97},{65,1},{97,33},{2,66}... | collective-permute-start | bytes 393224 | tf_op jit(solution)/shard_map/ppermute | solution.py:342

commit v4 on v3

--- a/solution.py
+++ b/solution.py
@@ -114,7 +114,8 @@
     )(*given, live)
 
 
-def forward_kernel(start, steps, table, values, x0, x1, x3, x2, out):
+def forward_kernel(start, steps, table, values, x0, x1, x3, x2, *refs):
+    out = refs[-1]
     sources = (x0, x1, x2, x3)
     rows = FWD_TILES * 128
     for step in range(steps):
@@ -133,23 +134,23 @@
         out[step * rows : (step + 1) * rows, :] = total.astype(out.dtype)
 
 
-def forward(name, start, count, dtype, table, values, sources):
+def forward(name, start, count, dtype, table, values, sources, *after):
     return pl.pallas_call(
         functools.partial(forward_kernel, start, count // FWD_TILES),
         out_shape=sds((count * 128, 128), dtype),
-        in_specs=[SM] + [VM] * 5,
+        in_specs=[SM] + [VM] * 5 + [AN] * len(after),
         out_specs=VM,
         name=name,
         cost_estimate=pl.CostEstimate(
             flops=2 * count * 128 * 1024 * 128, bytes_accessed=count << 15, transcendentals=0
         ),
         compiler_params=PARAMS,
-    )(table, values, *sources)
+    )(table, values, *sources, *after)
 
 
 def first_sum_kernel(kept, got, s1, s3, s2):
     for a, out in enumerate((s1, s2, s3)):
-        total = kept[a * 1024 : a * 1024 + 1024, :] + got[a * 1024 + 1024 : a * 1024 + 2048, :].astype(F32)
+        total = kept[a * 1024 : a * 1024 + 1024, :] + got[a * 1024 : a * 1024 + 1024, :].astype(F32)
         out[...] = total.astype(BF)
 
 
@@ -372,9 +373,10 @@
         tile_values[0, 0], features, tile_rows, tile_cols, tile_counts
     )
     sources = [own_features] + shifted
-    other = swap_cores(forward("forward_other", 0, 32, BF, table, values, sources))
-    kept = forward("forward_sent", 40, 24, F32, table, values, sources)
-    got = shift_each(chip_shift, first_sum(kept, other), 1, 0)
+    other = swap_cores(forward("forward_other", 8, 24, BF, table, values, sources))
+    sent = forward("forward_sent", 40, 24, F32, table, values, sources)
+    got = shift_each(chip_shift, first_sum(sent, other), 1, 0)
+    other = swap_cores(forward("forward_rest", 0, 8, BF, table, values, sources, sent))
     kept = forward("forward_kept", 32, 8, F32, table, values, sources)
     own, *sends = second_sum(kept, other, got)
     got = shift_each(chip_shift, sends, 1, 1)

time: 76.2 us -> 75.7 us (level)
  waiting for transfers between devices: 28.1 us -> 25.2 us
  starting transfers between devices: 30.9 us -> 33 us
    ppermute x12, waiting for transfers between devices: 22.4 us -> 19.6 us  [chip_shift(): return lax.ppermute(value, 'col', pairs)]
    ppermute x12, starting transfers between devices: 14.6 us -> 17.4 us  [chip_shift(): return lax.ppermute(value, 'col', pairs)]
    ppermute x5 -> x6, starting transfers between devices: 7.85 us -> 7.56 us  [swap_cores(): return lax.ppermute(value, 'col', [(j, j ^ 1) for j in range(32)])]
    pallas_call x3 -> x4, Pallas kernels: 4.82 us -> 4.99 us  [forward(): pl.pallas_call(functools.partial(forward_kernel, start, count // FWD_TILE...]
  transfers between devices with their start and end apart: 23 -> 24, of which waited for: 16 -> 13; matrix products, arithmetic and copies ran while one was open for 0% -> 0% of each run, Pallas kernels for 12% -> 13%
where the time goes in v4:
time: 75.7 us; the launch traced here: 74.7 us
  starting transfers between devices  33 us (44%)
  waiting for transfers between devices  25.2 us (33%)
  Pallas kernels  15 us (20%)
  between operations  1.47 us (2%)
    ppermute x12, waiting for transfers between devices, chip_shift(): return lax.ppermute(value, 'col', pairs)  19.6 us
    ppermute x12, starting transfers between devices, chip_shift(): return lax.ppermute(value, 'col', pairs)  17.4 us
    ppermute x6, starting transfers between devices, row_shift(): return lax.ppermute(value, 'row', [(i, (i + k) % 4) for i in range(4)])  8.08 us
    ppermute x6, starting transfers between devices, swap_cores(): return lax.ppermute(value, 'col', [(j, j ^ 1) for j in range(32)])  7.56 us
    ppermute x6, waiting for transfers between devices, row_shift(): return lax.ppermute(value, 'row', [(i, (i + k) % 4) for i in range(4)])  5.27 us
    pallas_call x4, Pallas kernels, forward(): pl.pallas_call(functools.partial(forward_kernel, start, count // FWD_TILE...  4.99 us
    pallas_call x1, Pallas kernels, load(): pl.pallas_call(load_kernel, out_shape=(sds(values.shape, BF), sds(feature...  4.02 us
    pallas_call x3, Pallas kernels, backward(): pl.pallas_call(functools.partial(backward_kernel, half, offsets, partial...  2.49 us
  transfers between devices with their start and end apart: 24, of which 13 were waited for; matrix products, arithmetic and copies ran while one was open for 0% of the time, Pallas kernels for 13%

profile of v4, /device:TPU:1, one launch (start us, length us, event | category | flops | bytes accessed | tf_op | source)
XLA Modules:
  0.0 74.7 jit_solution(16494303340144050126)
XLA Ops:
  0.6 2.2 %collective-permute-start = (bf16[256,128]{1,0:T(8,128)(2,1)}, bf16[256,128]{1,0:T(8,128)(2,1)S(1)}, u32[]{:S(2)}, u32[]{:S(2)}) collective-permute-start(bf16[256,128]{1,0:T(8,128)(2,1)} %features.1), channel_id=1, source_target_pairs={{0,32},{32,64},{64,96},{96,0},{1,33},{33,65},{65,97},{97,1},{2,34}... | collective-permute-start | bytes 196616 | tf_op jit(solution)/shard_map/ppermute | solution.py:343
  2.8 1.5 %collective-permute-start.1 = (bf16[256,128]{1,0:T(8,128)(2,1)}, bf16[256,128]{1,0:T(8,128)(2,1)S(1)}, u32[]{:S(2)}, u32[]{:S(2)}) collective-permute-start(bf16[256,128]{1,0:T(8,128)(2,1)} %features.1), channel_id=1, source_target_pairs={{0,96},{32,0},{64,32},{96,64},{1,97},{33,1},{65,33},{97,65},{2,98}... | collective-permute-start | bytes 196616 | tf_op jit(solution)/shard_map/ppermute | solution.py:343
  4.3 1.6 %collective-permute-start.2 = (bf16[256,128]{1,0:T(8,128)(2,1)}, bf16[256,128]{1,0:T(8,128)(2,1)S(1)}, u32[]{:S(2)}, u32[]{:S(2)}) collective-permute-start(bf16[256,128]{1,0:T(8,128)(2,1)} %features.1), channel_id=1, source_target_pairs={{0,64},{32,96},{64,0},{96,32},{1,65},{33,97},{65,1},{97,33},{2,66}... | collective-permute-start | bytes 196616 | tf_op jit(solution)/shard_map/ppermute | solution.py:343
  6.6 4.0 %load.1 = (bf16[320,128,128]{2,1,0:T(8,128)(2,1)S(1)}, bf16[256,128]{1,0:T(8,128)(2,1)S(1)}, s32[512]{0:T(512)S(4)}) custom-call(bf16[320,128,128]{2,1,0:T(8,128)(2,1)} %bitcast.1, bf16[256,128]{1,0:T(8,128)(2,1)} %features.1, s32[1,1,320]{2,1,0:T(1,128)} %rows_in.1, s32[1,1,320]{2,1,0:T(1,128)} %cols_in.1, s32[1,1]{1,0:T(1,128)S(6)} %copy.16.live), custom_call_target="tpu_custom_call" | custom-call | bytes 11534336 | tf_op jit(solution)/shard_map/load/pallas_call | solution.py:101
  10.6 1.8 %forward_other.1 = bf16[3072,128]{1,0:T(8,128)(2,1)S(1)} custom-call(s32[512]{0:T(512)S(4)} %get-tuple-element.25.table, bf16[320,128,128]{2,1,0:T(8,128)(2,1)S(1)} %get-tuple-element.26.values, bf16[256,128]{1,0:T(8,128)(2,1)S(1)} %get-tuple-element.27.x0, bf16[256,128]{1,0:T(8,128)(2,1)S(1)} %collective-permute-done.x1, ...), custom_call_target="tpu_custom_call" | custom-call | flops 805306368 | bytes 786432 | tf_op jit(solution)/shard_map/forward_other/pallas_call | solution.py:138
  12.4 1.6 %collective-permute-start.4 = (bf16[3072,128]{1,0:T(8,128)(2,1)S(1)}, bf16[3072,128]{1,0:T(8,128)(2,1)S(1)}, u32[]{:S(2)}, u32[]{:S(2)}) collective-permute-start(bf16[3072,128]{1,0:T(8,128)(2,1)S(1)} %forward_other.1), channel_id=1, source_target_pairs={{0,1},{1,0},{2,3},{3,2},{4,5},{5,4},{6,7},{7,6},{8,9},{9,8},{10,11... | collective-permute-start | bytes 2359304 | tf_op jit(solution)/shard_map/ppermute | solution.py:347
  14.0 1.8 %forward_sent.1.refs_0_.kept = f32[3072,128]{1,0:T(8,128)S(1)} custom-call(s32[512]{0:T(512)S(4)} %get-tuple-element.25.table, bf16[320,128,128]{2,1,0:T(8,128)(2,1)S(1)} %get-tuple-element.26.values, bf16[256,128]{1,0:T(8,128)(2,1)S(1)} %get-tuple-element.27.x0, bf16[256,128]{1,0:T(8,128)(2,1)S(1)} %collective-permute-done.x1, ...), custom_call_target="tpu_custom_call" | custom-call | flops 805306368 | bytes 786432 | tf_op jit(solution)/shard_map/forward_sent/pallas_call | solution.py:138
  16.8 1.7 %collective-permute-start.5 = (bf16[1024,128]{1,0:T(8,128)(2,1)S(1)}, bf16[1024,128]{1,0:T(8,128)(2,1)S(1)}, u32[]{:S(2)}, u32[]{:S(2)}) collective-permute-start(bf16[1024,128]{1,0:T(8,128)(2,1)S(1)} %get-tuple-element.28), channel_id=1, source_target_pairs={{0,2},{1,9},{2,4},{3,11},{4,6},{5,13},{6,0},{7,15},{8,10},{9,17},{... | collective-permute-start | bytes 786440 | tf_op jit(solution)/shard_map/ppermute | solution.py:360
  18.5 2.2 %collective-permute-start.6 = (bf16[1024,128]{1,0:T(8,128)(2,1)S(1)}, bf16[1024,128]{1,0:T(8,128)(2,1)S(1)}, u32[]{:S(2)}, u32[]{:S(2)}) collective-permute-start(bf16[1024,128]{1,0:T(8,128)(2,1)S(1)} %get-tuple-element.29), channel_id=1, source_target_pairs={{0,6},{1,25},{2,0},{3,27},{4,2},{5,29},{6,4},{7,31},{8,14},{9,1},{... | collective-permute-start | bytes 786440 | tf_op jit(solution)/shard_map/ppermute | solution.py:360
  20.7 1.2 %collective-permute-start.7 = (bf16[1024,128]{1,0:T(8,128)(2,1)S(1)}, bf16[1024,128]{1,0:T(8,128)(2,1)S(1)}, u32[]{:S(2)}, u32[]{:S(2)}) collective-permute-start(bf16[1024,128]{1,0:T(8,128)(2,1)S(1)} %get-tuple-element.30), channel_id=1, source_target_pairs={{0,4},{1,17},{2,6},{3,19},{4,0},{5,21},{6,2},{7,23},{8,12},{9,25},... | collective-permute-start | bytes 786440 | tf_op jit(solution)/shard_map/ppermute | solution.py:360
  22.6 1.9 %collective-permute-done.5.g1 = bf16[1024,128]{1,0:T(8,128)(2,1)S(1)} collective-permute-done((bf16[1024,128]{1,0:T(8,128)(2,1)S(1)}, bf16[1024,128]{1,0:T(8,128)(2,1)S(1)}, u32[]{:S(2)}, u32[]{:S(2)}) %collective-permute-start.5) | collective-permute-done | bytes 262176 | tf_op jit(solution)/shard_map/ppermute | solution.py:360
  24.5 2.3 %collective-permute-done.6.g3 = bf16[1024,128]{1,0:T(8,128)(2,1)S(1)} collective-permute-done((bf16[1024,128]{1,0:T(8,128)(2,1)S(1)}, bf16[1024,128]{1,0:T(8,128)(2,1)S(1)}, u32[]{:S(2)}, u32[]{:S(2)}) %collective-permute-start.6) | collective-permute-done | bytes 262176 | tf_op jit(solution)/shard_map/ppermute | solution.py:360
  26.8 1.5 %collective-permute-done.7.g2 = bf16[1024,128]{1,0:T(8,128)(2,1)S(1)} collective-permute-done((bf16[1024,128]{1,0:T(8,128)(2,1)S(1)}, bf16[1024,128]{1,0:T(8,128)(2,1)S(1)}, u32[]{:S(2)}, u32[]{:S(2)}) %collective-permute-start.7) | collective-permute-done | bytes 262176 | tf_op jit(solution)/shard_map/ppermute | solution.py:360
  28.5 2.8 %collective-permute-start.10 = (bf16[256,128]{1,0:T(8,128)(2,1)S(1)}, bf16[256,128]{1,0:T(8,128)(2,1)S(1)}, u32[]{:S(2)}, u32[]{:S(2)}) collective-permute-start(bf16[256,128]{1,0:T(8,128)(2,1)S(1)} %get-tuple-element.34), channel_id=1, source_target_pairs={{0,16},{1,5},{2,18},{3,7},{4,20},{5,1},{6,22},{7,3},{8,24},{9,13},... | collective-permute-start | bytes 196616 | tf_op jit(solution)/shard_map/ppermute | solution.py:360
  31.7 2.3 %collective-permute-start.9 = (bf16[256,128]{1,0:T(8,128)(2,1)S(1)}, bf16[256,128]{1,0:T(8,128)(2,1)S(1)}, u32[]{:S(2)}, u32[]{:S(2)}) collective-permute-start(bf16[256,128]{1,0:T(8,128)(2,1)S(1)} %get-tuple-element.33), channel_id=1, source_target_pairs={{0,24},{1,7},{2,26},{3,1},{4,28},{5,3},{6,30},{7,5},{8,0},{9,15},{... | collective-permute-start | bytes 196616 | tf_op jit(solution)/shard_map/ppermute | solution.py:360
  34.0 1.6 %collective-permute-done.8.g1 = bf16[256,128]{1,0:T(8,128)(2,1)S(1)} collective-permute-done((bf16[256,128]{1,0:T(8,128)(2,1)S(1)}, bf16[256,128]{1,0:T(8,128)(2,1)S(1)}, u32[]{:S(2)}, u32[]{:S(2)}) %collective-permute-start.8) | collective-permute-done | bytes 65568 | tf_op jit(solution)/shard_map/ppermute | solution.py:360
  36.6 2.7 %collective-permute-start.12 = (bf16[3,128,256]{2,1,0:T(8,128)(2,1)S(1)}, bf16[3,128,256]{2,1,0:T(8,128)(2,1)S(1)}, u32[]{:S(2)}, u32[]{:S(2)}) collective-permute-start(bf16[3,128,256]{2,1,0:T(8,128)(2,1)S(1)} %get-tuple-element.36.own), channel_id=1, source_target_pairs={{0,24},{1,7},{2,26},{3,1},{4,28},{5,3},{6,30},{7,5},{8,0},{9,15},{... | collective-permute-start | bytes 589832 | tf_op jit(solution)/shard_map/ppermute | solution.py:360
  39.3 1.2 %collective-permute-start.13 = (bf16[3,128,256]{2,1,0:T(8,128)(2,1)S(1)}, bf16[3,128,256]{2,1,0:T(8,128)(2,1)S(1)}, u32[]{:S(2)}, u32[]{:S(2)}) collective-permute-start(bf16[3,128,256]{2,1,0:T(8,128)(2,1)S(1)} %get-tuple-element.36.own), channel_id=1, source_target_pairs={{0,16},{1,5},{2,18},{3,7},{4,20},{5,1},{6,22},{7,3},{8,24},{9,13},... | collective-permute-start | bytes 589832 | tf_op jit(solution)/shard_map/ppermute | solution.py:360
  40.5 1.9 %collective-permute-done.11.g3 = bf16[3,128,256]{2,1,0:T(8,128)(2,1)S(1)} collective-permute-done((bf16[3,128,256]{2,1,0:T(8,128)(2,1)S(1)}, bf16[3,128,256]{2,1,0:T(8,128)(2,1)S(1)}, u32[]{:S(2)}, u32[]{:S(2)}) %collective-permute-start.11) | collective-permute-done | bytes 196640 | tf_op jit(solution)/shard_map/ppermute | solution.py:360
  42.4 1.7 %collective-permute-done.12.g1 = bf16[3,128,256]{2,1,0:T(8,128)(2,1)S(1)} collective-permute-done((bf16[3,128,256]{2,1,0:T(8,128)(2,1)S(1)}, bf16[3,128,256]{2,1,0:T(8,128)(2,1)S(1)}, u32[]{:S(2)}, u32[]{:S(2)}) %collective-permute-start.12) | collective-permute-done | bytes 196640 | tf_op jit(solution)/shard_map/ppermute | solution.py:360
  44.0 1.6 %collective-permute-done.13.g2 = bf16[3,128,256]{2,1,0:T(8,128)(2,1)S(1)} collective-permute-done((bf16[3,128,256]{2,1,0:T(8,128)(2,1)S(1)}, bf16[3,128,256]{2,1,0:T(8,128)(2,1)S(1)}, u32[]{:S(2)}, u32[]{:S(2)}) %collective-permute-start.13) | collective-permute-done | bytes 196640 | tf_op jit(solution)/shard_map/ppermute | solution.py:360
  45.7 4.1 %collective-permute-start.17 = (bf16[5,128,256]{2,1,0:T(8,128)(2,1)S(1)}, bf16[5,128,256]{2,1,0:T(8,128)(2,1)S(1)}, u32[]{:S(2)}, u32[]{:S(2)}) collective-permute-start(bf16[5,128,256]{2,1,0:T(8,128)(2,1)S(1)} %gather_step.1.refs_0_.p0), channel_id=1, source_target_pairs={{0,1},{1,0},{2,3},{3,2},{4,5},{5,4},{6,7},{7,6},{8,9},{9,8},{10,11... | collective-permute-start | bytes 983048 | tf_op jit(solution)/shard_map/ppermute | solution.py:347
  49.9 1.1 %collective-permute-start.14 = (bf16[5,128,256]{2,1,0:T(8,128)(2,1)S(1)}, bf16[5,128,256]{2,1,0:T(8,128)(2,1)S(1)}, u32[]{:S(2)}, u32[]{:S(2)}) collective-permute-start(bf16[5,128,256]{2,1,0:T(8,128)(2,1)S(1)} %gather_step.1.refs_0_.p0), channel_id=1, source_target_pairs={{0,2},{1,9},{2,4},{3,11},{4,6},{5,13},{6,0},{7,15},{8,10},{9,17},{... | collective-permute-start | bytes 983048 | tf_op jit(solution)/shard_map/ppermute | solution.py:360
  51.0 1.5 %collective-permute-start.15 = (bf16[5,128,256]{2,1,0:T(8,128)(2,1)S(1)}, bf16[5,128,256]{2,1,0:T(8,128)(2,1)S(1)}, u32[]{:S(2)}, u32[]{:S(2)}) collective-permute-start(bf16[5,128,256]{2,1,0:T(8,128)(2,1)S(1)} %gather_step.1.refs_0_.p0), channel_id=1, source_target_pairs={{0,6},{1,25},{2,0},{3,27},{4,2},{5,29},{6,4},{7,31},{8,14},{9,1},{... | collective-permute-start | bytes 983048 | tf_op jit(solution)/shard_map/ppermute | solution.py:360
  54.0 3.3 %collective-permute-done.14.refs_0_ = bf16[5,128,256]{2,1,0:T(8,128)(2,1)S(1)} collective-permute-done((bf16[5,128,256]{2,1,0:T(8,128)(2,1)S(1)}, bf16[5,128,256]{2,1,0:T(8,128)(2,1)S(1)}, u32[]{:S(2)}, u32[]{:S(2)}) %collective-permute-start.14) | collective-permute-done | bytes 327712 | tf_op jit(solution)/shard_map/ppermute | solution.py:360
  57.3 2.8 %collective-permute-done.15.refs_1_ = bf16[5,128,256]{2,1,0:T(8,128)(2,1)S(1)} collective-permute-done((bf16[5,128,256]{2,1,0:T(8,128)(2,1)S(1)}, bf16[5,128,256]{2,1,0:T(8,128)(2,1)S(1)}, u32[]{:S(2)}, u32[]{:S(2)}) %collective-permute-start.15) | collective-permute-done | bytes 327712 | tf_op jit(solution)/shard_map/ppermute | solution.py:360
  61.1 1.2 %collective-permute-start.18 = (bf16[5,128,256]{2,1,0:T(8,128)(2,1)S(1)}, bf16[5,128,256]{2,1,0:T(8,128)(2,1)S(1)}, u32[]{:S(2)}, u32[]{:S(2)}) collective-permute-start(bf16[5,128,256]{2,1,0:T(8,128)(2,1)S(1)} %get-tuple-element.37.refs_0_.p3), channel_id=1, source_target_pairs={{0,1},{1,0},{2,3},{3,2},{4,5},{5,4},{6,7},{7,6},{8,9},{9,8},{10,11... | collective-permute-start | bytes 983048 | tf_op jit(solution)/shard_map/ppermute | solution.py:347
  62.8 1.4 %backward_1_3.1.partial = f32[4,128,256]{2,1,0:T(8,128)S(1)} custom-call(s32[512]{0:T(512)S(4)} %get-tuple-element.25.table, bf16[320,128,128]{2,1,0:T(8,128)(2,1)S(1)} %get-tuple-element.26.values, bf16[5,128,256]{2,1,0:T(8,128)(2,1)S(1)} %get-tuple-element.37.refs_0_.p3, bf16[5,128,256]{2,1,0:T(8,128)(2,1)S(1)} %get-tuple-element.38.refs_1_.p1, ...), custom_call_target="tpu_custom_call" | custom-call | flops 1 | bytes 1 | tf_op jit(solution)/shard_map/backward_1_3/pallas_call | solution.py:265
  64.5 1.4 %backward_last.1 = (f32[128,256]{1,0:T(8,128)S(1)}, bf16[1,128,256]{2,1,0:T(8,128)(2,1)S(1)}, bf16[2,128,256]{2,1,0:T(8,128)(2,1)S(1)}, bf16[2,128,256]{2,1,0:T(8,128)(2,1)S(1)}, bf16[2,128,256]{2,1,0:T(8,128)(2,1)S(1)}) custom-call(s32[512]{0:T(512)S(4)} %get-tuple-element.25.table, bf16[320,128,128]{2,1,0:T(8,128)(2,1)S(1)} %get-tuple-element.26.values, ...), custom_call_target="tpu_custom_call" | custom-call | flops 1 | bytes 1 | tf_op jit(solution)/shard_map/backward_last/pallas_call | solution.py:311
  66.8 1.9 %collective-permute-start.22 = (bf16[2,128,256]{2,1,0:T(8,128)(2,1)S(1)}, bf16[2,128,256]{2,1,0:T(8,128)(2,1)S(1)}, u32[]{:S(2)}, u32[]{:S(2)}) collective-permute-start(bf16[2,128,256]{2,1,0:T(8,128)(2,1)S(1)} %get-tuple-element.43), channel_id=1, source_target_pairs={{0,96},{32,0},{64,32},{96,64},{1,97},{33,1},{65,33},{97,65},{2,98}... | collective-permute-start | bytes 393224 | tf_op jit(solution)/shard_map/ppermute | solution.py:343
  68.7 3.2 %collective-permute-done.21.g3 = bf16[2,128,256]{2,1,0:T(8,128)(2,1)S(1)} collective-permute-done((bf16[2,128,256]{2,1,0:T(8,128)(2,1)S(1)}, bf16[2,128,256]{2,1,0:T(8,128)(2,1)S(1)}, u32[]{:S(2)}, u32[]{:S(2)}) %collective-permute-start.21) | collective-permute-done | bytes 131104 | tf_op jit(solution)/shard_map/ppermute | solution.py:343
  71.9 2.1 %collective-permute-done.23.g2 = bf16[2,128,256]{2,1,0:T(8,128)(2,1)S(1)} collective-permute-done((bf16[2,128,256]{2,1,0:T(8,128)(2,1)S(1)}, bf16[2,128,256]{2,1,0:T(8,128)(2,1)S(1)}, u32[]{:S(2)}, u32[]{:S(2)}) %collective-permute-start.23) | collective-permute-done | bytes 131104 | tf_op jit(solution)/shard_map/ppermute | solution.py:343
  (35 shorter events, 8.0 us)
Async XLA Ops:
  0.6 10.0 %collective-permute-start = (bf16[256,128]{1,0:T(8,128)(2,1)}, bf16[256,128]{1,0:T(8,128)(2,1)S(1)}, u32[]{:S(2)}, u32[]{:S(2)}) collective-permute-start(bf16[256,128]{1,0:T(8,128)(2,1)} %features.1), channel_id=1, source_target_pairs={{0,32},{32,64},{64,96},{96,0},{1,33},{33,65},{65,97},{97,1},{2,34}... | collective-permute-start | bytes 196616 | tf_op jit(solution)/shard_map/ppermute | solution.py:343
  2.8 7.8 %collective-permute-start.1 = (bf16[256,128]{1,0:T(8,128)(2,1)}, bf16[256,128]{1,0:T(8,128)(2,1)S(1)}, u32[]{:S(2)}, u32[]{:S(2)}) collective-permute-start(bf16[256,128]{1,0:T(8,128)(2,1)} %features.1), channel_id=1, source_target_pairs={{0,96},{32,0},{64,32},{96,64},{1,97},{33,1},{65,33},{97,65},{2,98}... | collective-permute-start | bytes 196616 | tf_op jit(solution)/shard_map/ppermute | solution.py:343
  4.3 6.3 %collective-permute-start.2 = (bf16[256,128]{1,0:T(8,128)(2,1)}, bf16[256,128]{1,0:T(8,128)(2,1)S(1)}, u32[]{:S(2)}, u32[]{:S(2)}) collective-permute-start(bf16[256,128]{1,0:T(8,128)(2,1)} %features.1), channel_id=1, source_target_pairs={{0,64},{32,96},{64,0},{96,32},{1,65},{33,97},{65,1},{97,33},{2,66}... | collective-permute-start | bytes 196616 | tf_op jit(solution)/shard_map/ppermute | solution.py:343
  12.4 4.2 %collective-permute-start.4 = (bf16[3072,128]{1,0:T(8,128)(2,1)S(1)}, bf16[3072,128]{1,0:T(8,128)(2,1)S(1)}, u32[]{:S(2)}, u32[]{:S(2)}) collective-permute-start(bf16[3072,128]{1,0:T(8,128)(2,1)S(1)} %forward_other.1), channel_id=1, source_target_pairs={{0,1},{1,0},{2,3},{3,2},{4,5},{5,4},{6,7},{7,6},{8,9},{9,8},{10,11... | collective-permute-start | bytes 2359304 | tf_op jit(solution)/shard_map/ppermute | solution.py:347
  16.5 19.1 %copy-start = (bf16[256,256]{1,0:T(8,128)(2,1)S(1)}, bf16[256,256]{1,0:T(8,128)(2,1)}, u32[]{:S(2)}) copy-start(bf16[256,256]{1,0:T(8,128)(2,1)} %cotangent.1) | copy-start | bytes 393220
  16.5 19.1 %copy-start.1 = (bf16[128,256]{1,0:T(8,128)(2,1)S(1)}, bf16[128,256]{1,0:T(8,128)(2,1)}, u32[]{:S(2)}) copy-start(bf16[128,256]{1,0:T(8,128)(2,1)} %weight.1) | copy-start | bytes 196612
  16.6 6.1 %collective-permute-start.3 = (bf16[1024,128]{1,0:T(8,128)(2,1)S(1)}, bf16[1024,128]{1,0:T(8,128)(2,1)S(1)}, u32[]{:S(2)}, u32[]{:S(2)}) collective-permute-start(bf16[1024,128]{1,0:T(8,128)(2,1)S(1)} %forward_rest.1), channel_id=1, source_target_pairs={{0,1},{1,0},{2,3},{3,2},{4,5},{5,4},{6,7},{7,6},{8,9},{9,8},{10,11... | collective-permute-start | bytes 786440 | tf_op jit(solution)/shard_map/ppermute | solution.py:347
  16.8 7.7 %collective-permute-start.5 = (bf16[1024,128]{1,0:T(8,128)(2,1)S(1)}, bf16[1024,128]{1,0:T(8,128)(2,1)S(1)}, u32[]{:S(2)}, u32[]{:S(2)}) collective-permute-start(bf16[1024,128]{1,0:T(8,128)(2,1)S(1)} %get-tuple-element.28), channel_id=1, source_target_pairs={{0,2},{1,9},{2,4},{3,11},{4,6},{5,13},{6,0},{7,15},{8,10},{9,17},{... | collective-permute-start | bytes 786440 | tf_op jit(solution)/shard_map/ppermute | solution.py:360
  18.5 8.3 %collective-permute-start.6 = (bf16[1024,128]{1,0:T(8,128)(2,1)S(1)}, bf16[1024,128]{1,0:T(8,128)(2,1)S(1)}, u32[]{:S(2)}, u32[]{:S(2)}) collective-permute-start(bf16[1024,128]{1,0:T(8,128)(2,1)S(1)} %get-tuple-element.29), channel_id=1, source_target_pairs={{0,6},{1,25},{2,0},{3,27},{4,2},{5,29},{6,4},{7,31},{8,14},{9,1},{... | collective-permute-start | bytes 786440 | tf_op jit(solution)/shard_map/ppermute | solution.py:360
  20.7 7.7 %collective-permute-start.7 = (bf16[1024,128]{1,0:T(8,128)(2,1)S(1)}, bf16[1024,128]{1,0:T(8,128)(2,1)S(1)}, u32[]{:S(2)}, u32[]{:S(2)}) collective-permute-start(bf16[1024,128]{1,0:T(8,128)(2,1)S(1)} %get-tuple-element.30), channel_id=1, source_target_pairs={{0,4},{1,17},{2,6},{3,19},{4,0},{5,21},{6,2},{7,23},{8,12},{9,25},... | collective-permute-start | bytes 786440 | tf_op jit(solution)/shard_map/ppermute | solution.py:360
  28.5 5.5 %collective-permute-start.10 = (bf16[256,128]{1,0:T(8,128)(2,1)S(1)}, bf16[256,128]{1,0:T(8,128)(2,1)S(1)}, u32[]{:S(2)}, u32[]{:S(2)}) collective-permute-start(bf16[256,128]{1,0:T(8,128)(2,1)S(1)} %get-tuple-element.34), channel_id=1, source_target_pairs={{0,16},{1,5},{2,18},{3,7},{4,20},{5,1},{6,22},{7,3},{8,24},{9,13},... | collective-permute-start | bytes 196616 | tf_op jit(solution)/shard_map/ppermute | solution.py:360
  31.3 4.3 %collective-permute-start.8 = (bf16[256,128]{1,0:T(8,128)(2,1)S(1)}, bf16[256,128]{1,0:T(8,128)(2,1)S(1)}, u32[]{:S(2)}, u32[]{:S(2)}) collective-permute-start(bf16[256,128]{1,0:T(8,128)(2,1)S(1)} %get-tuple-element.32), channel_id=1, source_target_pairs={{0,8},{1,3},{2,10},{3,5},{4,12},{5,7},{6,14},{7,1},{8,16},{9,11},{... | collective-permute-start | bytes 196616 | tf_op jit(solution)/shard_map/ppermute | solution.py:360
  31.7 4.0 %collective-permute-start.9 = (bf16[256,128]{1,0:T(8,128)(2,1)S(1)}, bf16[256,128]{1,0:T(8,128)(2,1)S(1)}, u32[]{:S(2)}, u32[]{:S(2)}) collective-permute-start(bf16[256,128]{1,0:T(8,128)(2,1)S(1)} %get-tuple-element.33), channel_id=1, source_target_pairs={{0,24},{1,7},{2,26},{3,1},{4,28},{5,3},{6,30},{7,5},{8,0},{9,15},{... | collective-permute-start | bytes 196616 | tf_op jit(solution)/shard_map/ppermute | solution.py:360
  36.6 5.7 %collective-permute-start.11 = (bf16[3,128,256]{2,1,0:T(8,128)(2,1)S(1)}, bf16[3,128,256]{2,1,0:T(8,128)(2,1)S(1)}, u32[]{:S(2)}, u32[]{:S(2)}) collective-permute-start(bf16[3,128,256]{2,1,0:T(8,128)(2,1)S(1)} %get-tuple-element.36.own), channel_id=1, source_target_pairs={{0,8},{1,3},{2,10},{3,5},{4,12},{5,7},{6,14},{7,1},{8,16},{9,11},{... | collective-permute-start | bytes 589832 | tf_op jit(solution)/shard_map/ppermute | solution.py:360
  36.6 7.4 %collective-permute-start.12 = (bf16[3,128,256]{2,1,0:T(8,128)(2,1)S(1)}, bf16[3,128,256]{2,1,0:T(8,128)(2,1)S(1)}, u32[]{:S(2)}, u32[]{:S(2)}) collective-permute-start(bf16[3,128,256]{2,1,0:T(8,128)(2,1)S(1)} %get-tuple-element.36.own), channel_id=1, source_target_pairs={{0,24},{1,7},{2,26},{3,1},{4,28},{5,3},{6,30},{7,5},{8,0},{9,15},{... | collective-permute-start | bytes 589832 | tf_op jit(solution)/shard_map/ppermute | solution.py:360
  39.3 6.3 %collective-permute-start.13 = (bf16[3,128,256]{2,1,0:T(8,128)(2,1)S(1)}, bf16[3,128,256]{2,1,0:T(8,128)(2,1)S(1)}, u32[]{:S(2)}, u32[]{:S(2)}) collective-permute-start(bf16[3,128,256]{2,1,0:T(8,128)(2,1)S(1)} %get-tuple-element.36.own), channel_id=1, source_target_pairs={{0,16},{1,5},{2,18},{3,7},{4,20},{5,1},{6,22},{7,3},{8,24},{9,13},... | collective-permute-start | bytes 589832 | tf_op jit(solution)/shard_map/ppermute | solution.py:360
  45.7 7.7 %collective-permute-start.17 = (bf16[5,128,256]{2,1,0:T(8,128)(2,1)S(1)}, bf16[5,128,256]{2,1,0:T(8,128)(2,1)S(1)}, u32[]{:S(2)}, u32[]{:S(2)}) collective-permute-start(bf16[5,128,256]{2,1,0:T(8,128)(2,1)S(1)} %gather_step.1.refs_0_.p0), channel_id=1, source_target_pairs={{0,1},{1,0},{2,3},{3,2},{4,5},{5,4},{6,7},{7,6},{8,9},{9,8},{10,11... | collective-permute-start | bytes 983048 | tf_op jit(solution)/shard_map/ppermute | solution.py:347
  49.9 7.4 %collective-permute-start.14 = (bf16[5,128,256]{2,1,0:T(8,128)(2,1)S(1)}, bf16[5,128,256]{2,1,0:T(8,128)(2,1)S(1)}, u32[]{:S(2)}, u32[]{:S(2)}) collective-permute-start(bf16[5,128,256]{2,1,0:T(8,128)(2,1)S(1)} %gather_step.1.refs_0_.p0), channel_id=1, source_target_pairs={{0,2},{1,9},{2,4},{3,11},{4,6},{5,13},{6,0},{7,15},{8,10},{9,17},{... | collective-permute-start | bytes 983048 | tf_op jit(solution)/shard_map/ppermute | solution.py:360
  51.0 9.1 %collective-permute-start.15 = (bf16[5,128,256]{2,1,0:T(8,128)(2,1)S(1)}, bf16[5,128,256]{2,1,0:T(8,128)(2,1)S(1)}, u32[]{:S(2)}, u32[]{:S(2)}) collective-permute-start(bf16[5,128,256]{2,1,0:T(8,128)(2,1)S(1)} %gather_step.1.refs_0_.p0), channel_id=1, source_target_pairs={{0,6},{1,25},{2,0},{3,27},{4,2},{5,29},{6,4},{7,31},{8,14},{9,1},{... | collective-permute-start | bytes 983048 | tf_op jit(solution)/shard_map/ppermute | solution.py:360
  52.6 8.5 %collective-permute-start.16 = (bf16[5,128,256]{2,1,0:T(8,128)(2,1)S(1)}, bf16[5,128,256]{2,1,0:T(8,128)(2,1)S(1)}, u32[]{:S(2)}, u32[]{:S(2)}) collective-permute-start(bf16[5,128,256]{2,1,0:T(8,128)(2,1)S(1)} %gather_step.1.refs_0_.p0), channel_id=1, source_target_pairs={{0,4},{1,17},{2,6},{3,19},{4,0},{5,21},{6,2},{7,23},{8,12},{9,25},... | collective-permute-start | bytes 983048 | tf_op jit(solution)/shard_map/ppermute | solution.py:360
  61.1 3.1 %collective-permute-start.18 = (bf16[5,128,256]{2,1,0:T(8,128)(2,1)S(1)}, bf16[5,128,256]{2,1,0:T(8,128)(2,1)S(1)}, u32[]{:S(2)}, u32[]{:S(2)}) collective-permute-start(bf16[5,128,256]{2,1,0:T(8,128)(2,1)S(1)} %get-tuple-element.37.refs_0_.p3), channel_id=1, source_target_pairs={{0,1},{1,0},{2,3},{3,2},{4,5},{5,4},{6,7},{7,6},{8,9},{9,8},{10,11... | collective-permute-start | bytes 983048 | tf_op jit(solution)/shard_map/ppermute | solution.py:347
  62.3 1.9 %collective-permute-start.19 = (bf16[5,128,256]{2,1,0:T(8,128)(2,1)S(1)}, bf16[5,128,256]{2,1,0:T(8,128)(2,1)S(1)}, u32[]{:S(2)}, u32[]{:S(2)}) collective-permute-start(bf16[5,128,256]{2,1,0:T(8,128)(2,1)S(1)} %get-tuple-element.38.refs_1_.p1), channel_id=1, source_target_pairs={{0,1},{1,0},{2,3},{3,2},{4,5},{5,4},{6,7},{7,6},{8,9},{9,8},{10,11... | collective-permute-start | bytes 983048 | tf_op jit(solution)/shard_map/ppermute | solution.py:347
  62.3 2.2 %collective-permute-start.20 = (bf16[5,128,256]{2,1,0:T(8,128)(2,1)S(1)}, bf16[5,128,256]{2,1,0:T(8,128)(2,1)S(1)}, u32[]{:S(2)}, u32[]{:S(2)}) collective-permute-start(bf16[5,128,256]{2,1,0:T(8,128)(2,1)S(1)} %get-tuple-element.39.refs_2_.p2), channel_id=1, source_target_pairs={{0,1},{1,0},{2,3},{3,2},{4,5},{5,4},{6,7},{7,6},{8,9},{9,8},{10,11... | collective-permute-start | bytes 983048 | tf_op jit(solution)/shard_map/ppermute | solution.py:347
  65.9 6.0 %collective-permute-start.21 = (bf16[2,128,256]{2,1,0:T(8,128)(2,1)S(1)}, bf16[2,128,256]{2,1,0:T(8,128)(2,1)S(1)}, u32[]{:S(2)}, u32[]{:S(2)}) collective-permute-start(bf16[2,128,256]{2,1,0:T(8,128)(2,1)S(1)} %get-tuple-element.42), channel_id=1, source_target_pairs={{0,32},{32,64},{64,96},{96,0},{1,33},{33,65},{65,97},{97,1},{2,34}... | collective-permute-start | bytes 393224 | tf_op jit(solution)/shard_map/ppermute | solution.py:343
  66.8 5.1 %collective-permute-start.22 = (bf16[2,128,256]{2,1,0:T(8,128)(2,1)S(1)}, bf16[2,128,256]{2,1,0:T(8,128)(2,1)S(1)}, u32[]{:S(2)}, u32[]{:S(2)}) collective-permute-start(bf16[2,128,256]{2,1,0:T(8,128)(2,1)S(1)} %get-tuple-element.43), channel_id=1, source_target_pairs={{0,96},{32,0},{64,32},{96,64},{1,97},{33,1},{65,33},{97,65},{2,98}... | collective-permute-start | bytes 393224 | tf_op jit(solution)/shard_map/ppermute | solution.py:343
  68.7 5.3 %collective-permute-start.23 = (bf16[2,128,256]{2,1,0:T(8,128)(2,1)S(1)}, bf16[2,128,256]{2,1,0:T(8,128)(2,1)S(1)}, u32[]{:S(2)}, u32[]{:S(2)}) collective-permute-start(bf16[2,128,256]{2,1,0:T(8,128)(2,1)S(1)} %get-tuple-element.44), channel_id=1, source_target_pairs={{0,64},{32,96},{64,0},{96,32},{1,65},{33,97},{65,1},{97,33},{2,66}... | collective-permute-start | bytes 393224 | tf_op jit(solution)/shard_map/ppermute | solution.py:343

commit v5 on v4

--- a/solution.py
+++ b/solution.py
@@ -190,7 +190,7 @@
     w = weight[...]
     summed = dot(high, w) + dot(low, w)
     gate = 1.0 / (1.0 + jnp.exp(-summed))
-    out[...] = (summed * gate).astype(BF)
+    out[...] = summed * gate
     slope = gate * (1.0 + summed * (1.0 - gate))
     grad = (cotangent[...].astype(F32) * slope).astype(BF)
     back = lax.dot_general(w, grad, (((1,), (1,)), ((), ())), preferred_element_type=F32)
@@ -204,7 +204,7 @@
 def middle(own, got, weight, cotangent):
     return pl.pallas_call(
         middle_kernel,
-        out_shape=(sds((256, 256), BF), sds((3, 128, 256), BF)),
+        out_shape=(sds((256, 256), F32), sds((3, 128, 256), BF)),
         in_specs=[VM] * 6,
         out_specs=(VM,) * 2,
         name="middle",
@@ -273,6 +273,24 @@
     )(table, values, *parts, *given)
 
 
+def backward_first_kernel(table, values, part, active, out, output):
+    for q in range(4):
+        out[q] = backward_tiles(1, 0, q, table, values, part, None)
+    output[...] = active[...].astype(BF)
+
+
+def backward_first(table, values, part, active):
+    return pl.pallas_call(
+        backward_first_kernel,
+        out_shape=(sds((4, 128, 256), F32), sds(active.shape, BF)),
+        in_specs=[SM] + [VM] * 3,
+        out_specs=(VM,) * 2,
+        name="backward_first",
+        cost_estimate=BACK_COST,
+        compiler_params=PARAMS,
+    )(table, values, part, active)
+
+
 def tie_kernel(*refs):
     del refs
 
@@ -289,7 +307,7 @@
     )(*values, after)
 
 
-def last_kernel(half, offsets, table, values, p0, p3, p1, p2, o0, o3, o1, o2, partial, own, own_term, s3, s1, s2):
+def last_kernel(half, offsets, table, values, p0, p3, p1, p2, o0, o3, o1, o2, partial, own_term, s3, s1, s2):
     sends = (s1, s2, s3)
     parts = [(o0, o1, o2, o3)[a] for a in offsets]
     term = ring_sum(p0, p1, p2, p3, 4, COL_TERMS) + ring_sum(o0, o1, o2, o3, 4, COL_TERMS)
@@ -297,27 +315,43 @@
         own_term[n] = term
         for out in sends:
             out[1 + n] = term
-    for q in range(4):
+    for q in range(1, 4):
         total = partial[q]
         for a, part in zip(offsets, parts):
             total = backward_tiles(half, a, q, table, values, part, total)
-        if q == 0:
-            own[...] = total
-        else:
-            sends[q - 1][0] = total.astype(BF)
+        sends[q - 1][0] = total.astype(BF)
 
 
 def last(half, offsets, table, values, mine, others, partial):
     return pl.pallas_call(
         functools.partial(last_kernel, half, offsets),
-        out_shape=(sds((128, 256), F32), sds((ROW_TERMS, 128, 256), BF))
-        + (sds((1 + ROW_TERMS, 128, 256), BF),) * 3,
+        out_shape=(sds((ROW_TERMS, 128, 256), BF),) + (sds((1 + ROW_TERMS, 128, 256), BF),) * 3,
         in_specs=[SM] + [VM] * 10,
-        out_specs=(VM,) * 5,
+        out_specs=(VM,) * 4,
         name="backward_last",
         cost_estimate=BACK_COST,
         compiler_params=PARAMS,
     )(table, values, *mine, *others, partial)
+
+
+def kept_kernel(half, offsets, table, values, r1, r2, r3, partial, after, own):
+    del after
+    total = partial[0]
+    for a, part in zip(offsets, (r1, r2, r3)):
+        total = backward_tiles(half, a, 0, table, values, part, total)
+    own[...] = total
+
+
+def kept_quarter(half, offsets, table, values, rest, partial, after):
+    return pl.pallas_call(
+        functools.partial(kept_kernel, half, offsets),
+        out_shape=sds((128, 256), F32),
+        in_specs=[SM] + [VM] * 5 + [AN],
+        out_specs=VM,
+        name="backward_kept",
+        cost_estimate=BACK_COST,
+        compiler_params=PARAMS,
+    )(table, values, *rest, partial, after)
 
 
 def finish_kernel(scale, own, own_term, g3, g1, g2, grad_in, grad_weight):
@@ -380,19 +414,20 @@
     kept = forward("forward_kept", 32, 8, F32, table, values, sources)
     own, *sends = second_sum(kept, other, got)
     got = shift_each(chip_shift, sends, 1, 1)
-    output, message = middle(own, got, weight, cotangent)
+    active, message = middle(own, got, weight, cotangent)
     got = shift_each(chip_shift, [message] * 3, -1, 1)
     message = gather_step(message, got)
     first = message
     rest = shift_each(chip_shift, [message] * 3, -1, 0)
     other_first = swap_cores(first)
-    partial = backward(1, (0,), table, values, (first,), None)
+    partial, output = backward_first(table, values, first, active)
     partial = backward(0, (0,), table, values, (other_first,), partial)
     rest = tie(rest, partial)
     other_rest = [swap_cores(v) for v in rest]
     partial = backward(1, ORDER[-1], table, values, rest, partial)
     mine, others = (first, *rest), (other_first, *other_rest)
-    own, own_term, *sends = last(0, ORDER[-1], table, values, mine, others, partial)
+    own_term, *sends = last(0, ORDER[-1], table, values, mine, others, partial)
+    own = kept_quarter(0, ORDER[-1], table, values, other_rest, partial, own_term)
     got = shift_each(row_shift, sends, -1)
     grad_in, grad_weight = finish(32768.0 ** -0.5, own, own_term, got)
     return output, grad_in, grad_weight

time: 75.7 us -> 75 us (level)
  waiting for transfers between devices: 25.2 us -> 24.1 us
    pallas_call x1 -> x3, Pallas kernels: 0.98 us -> 2.15 us  [the longest x1 1.11 us: backward_first(): pl.pallas_call(backward_first_kernel, out_shape=(sds((4, 128, 256), F32),...]
    pallas_call x3 -> x2, Pallas kernels: 2.49 us -> 1.91 us  [backward(): pl.pallas_call(functools.partial(backward_kernel, half, offsets, partial...]
  transfers between devices with their start and end apart: 24 -> 24, of which waited for: 13 -> 14; matrix products, arithmetic and copies ran while one was open for 0% -> 0% of each run, Pallas kernels for 13% -> 15%
where the time goes in v5:
time: 75 us; the launch traced here: 74.2 us
  starting transfers between devices  33.1 us (44%)
  waiting for transfers between devices  24.1 us (32%)
  Pallas kernels  15.4 us (21%)
  between operations  1.48 us (2%)
    ppermute x12, waiting for transfers between devices, chip_shift(): return lax.ppermute(value, 'col', pairs)  19.1 us
    ppermute x12, starting transfers between devices, chip_shift(): return lax.ppermute(value, 'col', pairs)  17.4 us
    ppermute x6, starting transfers between devices, row_shift(): return lax.ppermute(value, 'row', [(i, (i + k) % 4) for i in range(4)])  8.08 us
    ppermute x6, starting transfers between devices, swap_cores(): return lax.ppermute(value, 'col', [(j, j ^ 1) for j in range(32)])  7.64 us
    pallas_call x4, Pallas kernels, forward(): pl.pallas_call(functools.partial(forward_kernel, start, count // FWD_TILE...  4.99 us
    ppermute x6, waiting for transfers between devices, row_shift(): return lax.ppermute(value, 'row', [(i, (i + k) % 4) for i in range(4)])  4.77 us
    pallas_call x1, Pallas kernels, load(): pl.pallas_call(load_kernel, out_shape=(sds(values.shape, BF), sds(feature...  4.02 us
    pallas_call x2, Pallas kernels, backward(): pl.pallas_call(functools.partial(backward_kernel, half, offsets, partial...  1.91 us
  transfers between devices with their start and end apart: 24, of which 14 were waited for; matrix products, arithmetic and copies ran while one was open for 0% of the time, Pallas kernels for 15%

profile of v5, /device:TPU:1, one launch (start us, length us, event | category | flops | bytes accessed | tf_op | source)
XLA Modules:
  0.0 74.2 jit_solution(5659094066619748937)
XLA Ops:
  0.6 2.2 %collective-permute-start = (bf16[256,128]{1,0:T(8,128)(2,1)}, bf16[256,128]{1,0:T(8,128)(2,1)S(1)}, u32[]{:S(2)}, u32[]{:S(2)}) collective-permute-start(bf16[256,128]{1,0:T(8,128)(2,1)} %features.1), channel_id=1, source_target_pairs={{0,32},{32,64},{64,96},{96,0},{1,33},{33,65},{65,97},{97,1},{2,34}... | collective-permute-start | bytes 196616 | tf_op jit(solution)/shard_map/ppermute | solution.py:377
  2.8 1.5 %collective-permute-start.1 = (bf16[256,128]{1,0:T(8,128)(2,1)}, bf16[256,128]{1,0:T(8,128)(2,1)S(1)}, u32[]{:S(2)}, u32[]{:S(2)}) collective-permute-start(bf16[256,128]{1,0:T(8,128)(2,1)} %features.1), channel_id=1, source_target_pairs={{0,96},{32,0},{64,32},{96,64},{1,97},{33,1},{65,33},{97,65},{2,98}... | collective-permute-start | bytes 196616 | tf_op jit(solution)/shard_map/ppermute | solution.py:377
  4.3 1.6 %collective-permute-start.2 = (bf16[256,128]{1,0:T(8,128)(2,1)}, bf16[256,128]{1,0:T(8,128)(2,1)S(1)}, u32[]{:S(2)}, u32[]{:S(2)}) collective-permute-start(bf16[256,128]{1,0:T(8,128)(2,1)} %features.1), channel_id=1, source_target_pairs={{0,64},{32,96},{64,0},{96,32},{1,65},{33,97},{65,1},{97,33},{2,66}... | collective-permute-start | bytes 196616 | tf_op jit(solution)/shard_map/ppermute | solution.py:377
  6.6 4.0 %load.1 = (bf16[320,128,128]{2,1,0:T(8,128)(2,1)S(1)}, bf16[256,128]{1,0:T(8,128)(2,1)S(1)}, s32[512]{0:T(512)S(4)}) custom-call(bf16[320,128,128]{2,1,0:T(8,128)(2,1)} %bitcast.1, bf16[256,128]{1,0:T(8,128)(2,1)} %features.1, s32[1,1,320]{2,1,0:T(1,128)} %rows_in.1, s32[1,1,320]{2,1,0:T(1,128)} %cols_in.1, s32[1,1]{1,0:T(1,128)S(6)} %copy.16.live), custom_call_target="tpu_custom_call" | custom-call | bytes 11534336 | tf_op jit(solution)/shard_map/load/pallas_call | solution.py:101
  10.6 1.8 %forward_other.1 = bf16[3072,128]{1,0:T(8,128)(2,1)S(1)} custom-call(s32[512]{0:T(512)S(4)} %get-tuple-element.26.table, bf16[320,128,128]{2,1,0:T(8,128)(2,1)S(1)} %get-tuple-element.27.values, bf16[256,128]{1,0:T(8,128)(2,1)S(1)} %get-tuple-element.28.x0, bf16[256,128]{1,0:T(8,128)(2,1)S(1)} %collective-permute-done.x1, ...), custom_call_target="tpu_custom_call" | custom-call | flops 805306368 | bytes 786432 | tf_op jit(solution)/shard_map/forward_other/pallas_call | solution.py:138
  12.4 1.6 %collective-permute-start.4 = (bf16[3072,128]{1,0:T(8,128)(2,1)S(1)}, bf16[3072,128]{1,0:T(8,128)(2,1)S(1)}, u32[]{:S(2)}, u32[]{:S(2)}) collective-permute-start(bf16[3072,128]{1,0:T(8,128)(2,1)S(1)} %forward_other.1), channel_id=1, source_target_pairs={{0,1},{1,0},{2,3},{3,2},{4,5},{5,4},{6,7},{7,6},{8,9},{9,8},{10,11... | collective-permute-start | bytes 2359304 | tf_op jit(solution)/shard_map/ppermute | solution.py:381
  14.0 1.8 %forward_sent.1.refs_0_.kept = f32[3072,128]{1,0:T(8,128)S(1)} custom-call(s32[512]{0:T(512)S(4)} %get-tuple-element.26.table, bf16[320,128,128]{2,1,0:T(8,128)(2,1)S(1)} %get-tuple-element.27.values, bf16[256,128]{1,0:T(8,128)(2,1)S(1)} %get-tuple-element.28.x0, bf16[256,128]{1,0:T(8,128)(2,1)S(1)} %collective-permute-done.x1, ...), custom_call_target="tpu_custom_call" | custom-call | flops 805306368 | bytes 786432 | tf_op jit(solution)/shard_map/forward_sent/pallas_call | solution.py:138
  16.8 1.7 %collective-permute-start.5 = (bf16[1024,128]{1,0:T(8,128)(2,1)S(1)}, bf16[1024,128]{1,0:T(8,128)(2,1)S(1)}, u32[]{:S(2)}, u32[]{:S(2)}) collective-permute-start(bf16[1024,128]{1,0:T(8,128)(2,1)S(1)} %get-tuple-element.29), channel_id=1, source_target_pairs={{0,2},{1,9},{2,4},{3,11},{4,6},{5,13},{6,0},{7,15},{8,10},{9,17},{... | collective-permute-start | bytes 786440 | tf_op jit(solution)/shard_map/ppermute | solution.py:394
  18.5 2.2 %collective-permute-start.6 = (bf16[1024,128]{1,0:T(8,128)(2,1)S(1)}, bf16[1024,128]{1,0:T(8,128)(2,1)S(1)}, u32[]{:S(2)}, u32[]{:S(2)}) collective-permute-start(bf16[1024,128]{1,0:T(8,128)(2,1)S(1)} %get-tuple-element.30), channel_id=1, source_target_pairs={{0,6},{1,25},{2,0},{3,27},{4,2},{5,29},{6,4},{7,31},{8,14},{9,1},{... | collective-permute-start | bytes 786440 | tf_op jit(solution)/shard_map/ppermute | solution.py:394
  20.7 1.2 %collective-permute-start.7 = (bf16[1024,128]{1,0:T(8,128)(2,1)S(1)}, bf16[1024,128]{1,0:T(8,128)(2,1)S(1)}, u32[]{:S(2)}, u32[]{:S(2)}) collective-permute-start(bf16[1024,128]{1,0:T(8,128)(2,1)S(1)} %get-tuple-element.31), channel_id=1, source_target_pairs={{0,4},{1,17},{2,6},{3,19},{4,0},{5,21},{6,2},{7,23},{8,12},{9,25},... | collective-permute-start | bytes 786440 | tf_op jit(solution)/shard_map/ppermute | solution.py:394
  22.6 1.9 %collective-permute-done.5.g1 = bf16[1024,128]{1,0:T(8,128)(2,1)S(1)} collective-permute-done((bf16[1024,128]{1,0:T(8,128)(2,1)S(1)}, bf16[1024,128]{1,0:T(8,128)(2,1)S(1)}, u32[]{:S(2)}, u32[]{:S(2)}) %collective-permute-start.5) | collective-permute-done | bytes 262176 | tf_op jit(solution)/shard_map/ppermute | solution.py:394
  24.5 2.3 %collective-permute-done.6.g3 = bf16[1024,128]{1,0:T(8,128)(2,1)S(1)} collective-permute-done((bf16[1024,128]{1,0:T(8,128)(2,1)S(1)}, bf16[1024,128]{1,0:T(8,128)(2,1)S(1)}, u32[]{:S(2)}, u32[]{:S(2)}) %collective-permute-start.6) | collective-permute-done | bytes 262176 | tf_op jit(solution)/shard_map/ppermute | solution.py:394
  26.8 1.5 %collective-permute-done.7.g2 = bf16[1024,128]{1,0:T(8,128)(2,1)S(1)} collective-permute-done((bf16[1024,128]{1,0:T(8,128)(2,1)S(1)}, bf16[1024,128]{1,0:T(8,128)(2,1)S(1)}, u32[]{:S(2)}, u32[]{:S(2)}) %collective-permute-start.7) | collective-permute-done | bytes 262176 | tf_op jit(solution)/shard_map/ppermute | solution.py:394
  28.5 2.8 %collective-permute-start.10 = (bf16[256,128]{1,0:T(8,128)(2,1)S(1)}, bf16[256,128]{1,0:T(8,128)(2,1)S(1)}, u32[]{:S(2)}, u32[]{:S(2)}) collective-permute-start(bf16[256,128]{1,0:T(8,128)(2,1)S(1)} %get-tuple-element.35), channel_id=1, source_target_pairs={{0,16},{1,5},{2,18},{3,7},{4,20},{5,1},{6,22},{7,3},{8,24},{9,13},... | collective-permute-start | bytes 196616 | tf_op jit(solution)/shard_map/ppermute | solution.py:394
  31.7 2.3 %collective-permute-start.9 = (bf16[256,128]{1,0:T(8,128)(2,1)S(1)}, bf16[256,128]{1,0:T(8,128)(2,1)S(1)}, u32[]{:S(2)}, u32[]{:S(2)}) collective-permute-start(bf16[256,128]{1,0:T(8,128)(2,1)S(1)} %get-tuple-element.34), channel_id=1, source_target_pairs={{0,24},{1,7},{2,26},{3,1},{4,28},{5,3},{6,30},{7,5},{8,0},{9,15},{... | collective-permute-start | bytes 196616 | tf_op jit(solution)/shard_map/ppermute | solution.py:394
  34.0 1.6 %collective-permute-done.8.g1 = bf16[256,128]{1,0:T(8,128)(2,1)S(1)} collective-permute-done((bf16[256,128]{1,0:T(8,128)(2,1)S(1)}, bf16[256,128]{1,0:T(8,128)(2,1)S(1)}, u32[]{:S(2)}, u32[]{:S(2)}) %collective-permute-start.8) | collective-permute-done | bytes 65568 | tf_op jit(solution)/shard_map/ppermute | solution.py:394
  36.3 2.7 %collective-permute-start.12 = (bf16[3,128,256]{2,1,0:T(8,128)(2,1)S(1)}, bf16[3,128,256]{2,1,0:T(8,128)(2,1)S(1)}, u32[]{:S(2)}, u32[]{:S(2)}) collective-permute-start(bf16[3,128,256]{2,1,0:T(8,128)(2,1)S(1)} %get-tuple-element.36.own), channel_id=1, source_target_pairs={{0,24},{1,7},{2,26},{3,1},{4,28},{5,3},{6,30},{7,5},{8,0},{9,15},{... | collective-permute-start | bytes 589832 | tf_op jit(solution)/shard_map/ppermute | solution.py:394
  39.0 1.1 %collective-permute-start.13 = (bf16[3,128,256]{2,1,0:T(8,128)(2,1)S(1)}, bf16[3,128,256]{2,1,0:T(8,128)(2,1)S(1)}, u32[]{:S(2)}, u32[]{:S(2)}) collective-permute-start(bf16[3,128,256]{2,1,0:T(8,128)(2,1)S(1)} %get-tuple-element.36.own), channel_id=1, source_target_pairs={{0,16},{1,5},{2,18},{3,7},{4,20},{5,1},{6,22},{7,3},{8,24},{9,13},... | collective-permute-start | bytes 589832 | tf_op jit(solution)/shard_map/ppermute | solution.py:394
  40.1 1.9 %collective-permute-done.11.g3 = bf16[3,128,256]{2,1,0:T(8,128)(2,1)S(1)} collective-permute-done((bf16[3,128,256]{2,1,0:T(8,128)(2,1)S(1)}, bf16[3,128,256]{2,1,0:T(8,128)(2,1)S(1)}, u32[]{:S(2)}, u32[]{:S(2)}) %collective-permute-start.11) | collective-permute-done | bytes 196640 | tf_op jit(solution)/shard_map/ppermute | solution.py:394
  42.0 1.7 %collective-permute-done.12.g1 = bf16[3,128,256]{2,1,0:T(8,128)(2,1)S(1)} collective-permute-done((bf16[3,128,256]{2,1,0:T(8,128)(2,1)S(1)}, bf16[3,128,256]{2,1,0:T(8,128)(2,1)S(1)}, u32[]{:S(2)}, u32[]{:S(2)}) %collective-permute-start.12) | collective-permute-done | bytes 196640 | tf_op jit(solution)/shard_map/ppermute | solution.py:394
  43.8 1.5 %collective-permute-done.13.g2 = bf16[3,128,256]{2,1,0:T(8,128)(2,1)S(1)} collective-permute-done((bf16[3,128,256]{2,1,0:T(8,128)(2,1)S(1)}, bf16[3,128,256]{2,1,0:T(8,128)(2,1)S(1)}, u32[]{:S(2)}, u32[]{:S(2)}) %collective-permute-start.13) | collective-permute-done | bytes 196640 | tf_op jit(solution)/shard_map/ppermute | solution.py:394
  45.4 4.2 %collective-permute-start.17 = (bf16[5,128,256]{2,1,0:T(8,128)(2,1)S(1)}, bf16[5,128,256]{2,1,0:T(8,128)(2,1)S(1)}, u32[]{:S(2)}, u32[]{:S(2)}) collective-permute-start(bf16[5,128,256]{2,1,0:T(8,128)(2,1)S(1)} %gather_step.1.part.p0), channel_id=1, source_target_pairs={{0,1},{1,0},{2,3},{3,2},{4,5},{5,4},{6,7},{7,6},{8,9},{9,8},{10,11... | collective-permute-start | bytes 983048 | tf_op jit(solution)/shard_map/ppermute | solution.py:381
  50.7 1.6 %collective-permute-start.15 = (bf16[5,128,256]{2,1,0:T(8,128)(2,1)S(1)}, bf16[5,128,256]{2,1,0:T(8,128)(2,1)S(1)}, u32[]{:S(2)}, u32[]{:S(2)}) collective-permute-start(bf16[5,128,256]{2,1,0:T(8,128)(2,1)S(1)} %gather_step.1.part.p0), channel_id=1, source_target_pairs={{0,6},{1,25},{2,0},{3,27},{4,2},{5,29},{6,4},{7,31},{8,14},{9,1},{... | collective-permute-start | bytes 983048 | tf_op jit(solution)/shard_map/ppermute | solution.py:394
  52.5 1.1 %backward_first.1 = (f32[4,128,256]{2,1,0:T(8,128)S(1)}, bf16[256,256]{1,0:T(8,128)(2,1)}) custom-call(s32[512]{0:T(512)S(4)} %get-tuple-element.26.table, bf16[320,128,128]{2,1,0:T(8,128)(2,1)S(1)} %get-tuple-element.27.values, bf16[5,128,256]{2,1,0:T(8,128)(2,1)S(1)} %gather_step.1.part.p0, f32[256,256]{1,0:T(8,128)S(1)} %get-tuple-element.37.active), custom_call_target="tpu_custom_call" | custom-call | flops 1 | bytes 1 | tf_op jit(solution)/shard_map/backward_first/pallas_call | solution.py:283
  54.1 2.9 %collective-permute-done.14.refs_0_ = bf16[5,128,256]{2,1,0:T(8,128)(2,1)S(1)} collective-permute-done((bf16[5,128,256]{2,1,0:T(8,128)(2,1)S(1)}, bf16[5,128,256]{2,1,0:T(8,128)(2,1)S(1)}, u32[]{:S(2)}, u32[]{:S(2)}) %collective-permute-start.14) | collective-permute-done | bytes 327712 | tf_op jit(solution)/shard_map/ppermute | solution.py:394
  57.0 2.8 %collective-permute-done.15.refs_1_ = bf16[5,128,256]{2,1,0:T(8,128)(2,1)S(1)} collective-permute-done((bf16[5,128,256]{2,1,0:T(8,128)(2,1)S(1)}, bf16[5,128,256]{2,1,0:T(8,128)(2,1)S(1)}, u32[]{:S(2)}, u32[]{:S(2)}) %collective-permute-start.15) | collective-permute-done | bytes 327712 | tf_op jit(solution)/shard_map/ppermute | solution.py:394
  60.7 1.3 %collective-permute-start.18 = (bf16[5,128,256]{2,1,0:T(8,128)(2,1)S(1)}, bf16[5,128,256]{2,1,0:T(8,128)(2,1)S(1)}, u32[]{:S(2)}, u32[]{:S(2)}) collective-permute-start(bf16[5,128,256]{2,1,0:T(8,128)(2,1)S(1)} %get-tuple-element.40.refs_0_.p3), channel_id=1, source_target_pairs={{0,1},{1,0},{2,3},{3,2},{4,5},{5,4},{6,7},{7,6},{8,9},{9,8},{10,11... | collective-permute-start | bytes 983048 | tf_op jit(solution)/shard_map/ppermute | solution.py:381
  62.5 1.4 %backward_1_3.1.partial = f32[4,128,256]{2,1,0:T(8,128)S(1)} custom-call(s32[512]{0:T(512)S(4)} %get-tuple-element.26.table, bf16[320,128,128]{2,1,0:T(8,128)(2,1)S(1)} %get-tuple-element.27.values, bf16[5,128,256]{2,1,0:T(8,128)(2,1)S(1)} %get-tuple-element.40.refs_0_.p3, bf16[5,128,256]{2,1,0:T(8,128)(2,1)S(1)} %get-tuple-element.41.refs_1_.p1, ...), custom_call_target="tpu_custom_call" | custom-call | flops 1 | bytes 1 | tf_op jit(solution)/shard_map/backward_1_3/pallas_call | solution.py:265
  64.1 1.2 %backward_last.1 = (bf16[1,128,256]{2,1,0:T(8,128)(2,1)S(1)}, bf16[2,128,256]{2,1,0:T(8,128)(2,1)S(1)}, bf16[2,128,256]{2,1,0:T(8,128)(2,1)S(1)}, bf16[2,128,256]{2,1,0:T(8,128)(2,1)S(1)}) custom-call(s32[512]{0:T(512)S(4)} %get-tuple-element.26.table, bf16[320,128,128]{2,1,0:T(8,128)(2,1)S(1)} %get-tuple-element.27.values, ...), custom_call_target="tpu_custom_call" | custom-call | flops 1 | bytes 1 | tf_op jit(solution)/shard_map/backward_last/pallas_call | solution.py:326
  65.8 2.3 %collective-permute-start.22 = (bf16[2,128,256]{2,1,0:T(8,128)(2,1)S(1)}, bf16[2,128,256]{2,1,0:T(8,128)(2,1)S(1)}, u32[]{:S(2)}, u32[]{:S(2)}) collective-permute-start(bf16[2,128,256]{2,1,0:T(8,128)(2,1)S(1)} %get-tuple-element.45), channel_id=1, source_target_pairs={{0,96},{32,0},{64,32},{96,64},{1,97},{33,1},{65,33},{97,65},{2,98}... | collective-permute-start | bytes 393224 | tf_op jit(solution)/shard_map/ppermute | solution.py:377
  68.7 2.7 %collective-permute-done.21.g3 = bf16[2,128,256]{2,1,0:T(8,128)(2,1)S(1)} collective-permute-done((bf16[2,128,256]{2,1,0:T(8,128)(2,1)S(1)}, bf16[2,128,256]{2,1,0:T(8,128)(2,1)S(1)}, u32[]{:S(2)}, u32[]{:S(2)}) %collective-permute-start.21) | collective-permute-done | bytes 131104 | tf_op jit(solution)/shard_map/ppermute | solution.py:377
  71.4 2.0 %collective-permute-done.23.g2 = bf16[2,128,256]{2,1,0:T(8,128)(2,1)S(1)} collective-permute-done((bf16[2,128,256]{2,1,0:T(8,128)(2,1)S(1)}, bf16[2,128,256]{2,1,0:T(8,128)(2,1)S(1)}, u32[]{:S(2)}, u32[]{:S(2)}) %collective-permute-start.23) | collective-permute-done | bytes 131104 | tf_op jit(solution)/shard_map/ppermute | solution.py:377
  (36 shorter events, 8.3 us)
Async XLA Ops:
  0.6 10.0 %collective-permute-start = (bf16[256,128]{1,0:T(8,128)(2,1)}, bf16[256,128]{1,0:T(8,128)(2,1)S(1)}, u32[]{:S(2)}, u32[]{:S(2)}) collective-permute-start(bf16[256,128]{1,0:T(8,128)(2,1)} %features.1), channel_id=1, source_target_pairs={{0,32},{32,64},{64,96},{96,0},{1,33},{33,65},{65,97},{97,1},{2,34}... | collective-permute-start | bytes 196616 | tf_op jit(solution)/shard_map/ppermute | solution.py:377
  2.8 7.8 %collective-permute-start.1 = (bf16[256,128]{1,0:T(8,128)(2,1)}, bf16[256,128]{1,0:T(8,128)(2,1)S(1)}, u32[]{:S(2)}, u32[]{:S(2)}) collective-permute-start(bf16[256,128]{1,0:T(8,128)(2,1)} %features.1), channel_id=1, source_target_pairs={{0,96},{32,0},{64,32},{96,64},{1,97},{33,1},{65,33},{97,65},{2,98}... | collective-permute-start | bytes 196616 | tf_op jit(solution)/shard_map/ppermute | solution.py:377
  4.3 6.3 %collective-permute-start.2 = (bf16[256,128]{1,0:T(8,128)(2,1)}, bf16[256,128]{1,0:T(8,128)(2,1)S(1)}, u32[]{:S(2)}, u32[]{:S(2)}) collective-permute-start(bf16[256,128]{1,0:T(8,128)(2,1)} %features.1), channel_id=1, source_target_pairs={{0,64},{32,96},{64,0},{96,32},{1,65},{33,97},{65,1},{97,33},{2,66}... | collective-permute-start | bytes 196616 | tf_op jit(solution)/shard_map/ppermute | solution.py:377
  12.4 4.2 %collective-permute-start.4 = (bf16[3072,128]{1,0:T(8,128)(2,1)S(1)}, bf16[3072,128]{1,0:T(8,128)(2,1)S(1)}, u32[]{:S(2)}, u32[]{:S(2)}) collective-permute-start(bf16[3072,128]{1,0:T(8,128)(2,1)S(1)} %forward_other.1), channel_id=1, source_target_pairs={{0,1},{1,0},{2,3},{3,2},{4,5},{5,4},{6,7},{7,6},{8,9},{9,8},{10,11... | collective-permute-start | bytes 2359304 | tf_op jit(solution)/shard_map/ppermute | solution.py:381
  16.5 19.1 %copy-start = (bf16[256,256]{1,0:T(8,128)(2,1)S(1)}, bf16[256,256]{1,0:T(8,128)(2,1)}, u32[]{:S(2)}) copy-start(bf16[256,256]{1,0:T(8,128)(2,1)} %cotangent.1) | copy-start | bytes 393220
  16.5 19.1 %copy-start.1 = (bf16[128,256]{1,0:T(8,128)(2,1)S(1)}, bf16[128,256]{1,0:T(8,128)(2,1)}, u32[]{:S(2)}) copy-start(bf16[128,256]{1,0:T(8,128)(2,1)} %weight.1) | copy-start | bytes 196612
  16.6 6.1 %collective-permute-start.3 = (bf16[1024,128]{1,0:T(8,128)(2,1)S(1)}, bf16[1024,128]{1,0:T(8,128)(2,1)S(1)}, u32[]{:S(2)}, u32[]{:S(2)}) collective-permute-start(bf16[1024,128]{1,0:T(8,128)(2,1)S(1)} %forward_rest.1), channel_id=1, source_target_pairs={{0,1},{1,0},{2,3},{3,2},{4,5},{5,4},{6,7},{7,6},{8,9},{9,8},{10,11... | collective-permute-start | bytes 786440 | tf_op jit(solution)/shard_map/ppermute | solution.py:381
  16.8 7.7 %collective-permute-start.5 = (bf16[1024,128]{1,0:T(8,128)(2,1)S(1)}, bf16[1024,128]{1,0:T(8,128)(2,1)S(1)}, u32[]{:S(2)}, u32[]{:S(2)}) collective-permute-start(bf16[1024,128]{1,0:T(8,128)(2,1)S(1)} %get-tuple-element.29), channel_id=1, source_target_pairs={{0,2},{1,9},{2,4},{3,11},{4,6},{5,13},{6,0},{7,15},{8,10},{9,17},{... | collective-permute-start | bytes 786440 | tf_op jit(solution)/shard_map/ppermute | solution.py:394
  18.5 8.3 %collective-permute-start.6 = (bf16[1024,128]{1,0:T(8,128)(2,1)S(1)}, bf16[1024,128]{1,0:T(8,128)(2,1)S(1)}, u32[]{:S(2)}, u32[]{:S(2)}) collective-permute-start(bf16[1024,128]{1,0:T(8,128)(2,1)S(1)} %get-tuple-element.30), channel_id=1, source_target_pairs={{0,6},{1,25},{2,0},{3,27},{4,2},{5,29},{6,4},{7,31},{8,14},{9,1},{... | collective-permute-start | bytes 786440 | tf_op jit(solution)/shard_map/ppermute | solution.py:394
  20.7 7.7 %collective-permute-start.7 = (bf16[1024,128]{1,0:T(8,128)(2,1)S(1)}, bf16[1024,128]{1,0:T(8,128)(2,1)S(1)}, u32[]{:S(2)}, u32[]{:S(2)}) collective-permute-start(bf16[1024,128]{1,0:T(8,128)(2,1)S(1)} %get-tuple-element.31), channel_id=1, source_target_pairs={{0,4},{1,17},{2,6},{3,19},{4,0},{5,21},{6,2},{7,23},{8,12},{9,25},... | collective-permute-start | bytes 786440 | tf_op jit(solution)/shard_map/ppermute | solution.py:394
  28.5 5.5 %collective-permute-start.10 = (bf16[256,128]{1,0:T(8,128)(2,1)S(1)}, bf16[256,128]{1,0:T(8,128)(2,1)S(1)}, u32[]{:S(2)}, u32[]{:S(2)}) collective-permute-start(bf16[256,128]{1,0:T(8,128)(2,1)S(1)} %get-tuple-element.35), channel_id=1, source_target_pairs={{0,16},{1,5},{2,18},{3,7},{4,20},{5,1},{6,22},{7,3},{8,24},{9,13},... | collective-permute-start | bytes 196616 | tf_op jit(solution)/shard_map/ppermute | solution.py:394
  31.3 4.3 %collective-permute-start.8 = (bf16[256,128]{1,0:T(8,128)(2,1)S(1)}, bf16[256,128]{1,0:T(8,128)(2,1)S(1)}, u32[]{:S(2)}, u32[]{:S(2)}) collective-permute-start(bf16[256,128]{1,0:T(8,128)(2,1)S(1)} %get-tuple-element.33), channel_id=1, source_target_pairs={{0,8},{1,3},{2,10},{3,5},{4,12},{5,7},{6,14},{7,1},{8,16},{9,11},{... | collective-permute-start | bytes 196616 | tf_op jit(solution)/shard_map/ppermute | solution.py:394
  31.7 4.0 %collective-permute-start.9 = (bf16[256,128]{1,0:T(8,128)(2,1)S(1)}, bf16[256,128]{1,0:T(8,128)(2,1)S(1)}, u32[]{:S(2)}, u32[]{:S(2)}) collective-permute-start(bf16[256,128]{1,0:T(8,128)(2,1)S(1)} %get-tuple-element.34), channel_id=1, source_target_pairs={{0,24},{1,7},{2,26},{3,1},{4,28},{5,3},{6,30},{7,5},{8,0},{9,15},{... | collective-permute-start | bytes 196616 | tf_op jit(solution)/shard_map/ppermute | solution.py:394
  36.2 5.8 %collective-permute-start.11 = (bf16[3,128,256]{2,1,0:T(8,128)(2,1)S(1)}, bf16[3,128,256]{2,1,0:T(8,128)(2,1)S(1)}, u32[]{:S(2)}, u32[]{:S(2)}) collective-permute-start(bf16[3,128,256]{2,1,0:T(8,128)(2,1)S(1)} %get-tuple-element.36.own), channel_id=1, source_target_pairs={{0,8},{1,3},{2,10},{3,5},{4,12},{5,7},{6,14},{7,1},{8,16},{9,11},{... | collective-permute-start | bytes 589832 | tf_op jit(solution)/shard_map/ppermute | solution.py:394
  36.3 7.5 %collective-permute-start.12 = (bf16[3,128,256]{2,1,0:T(8,128)(2,1)S(1)}, bf16[3,128,256]{2,1,0:T(8,128)(2,1)S(1)}, u32[]{:S(2)}, u32[]{:S(2)}) collective-permute-start(bf16[3,128,256]{2,1,0:T(8,128)(2,1)S(1)} %get-tuple-element.36.own), channel_id=1, source_target_pairs={{0,24},{1,7},{2,26},{3,1},{4,28},{5,3},{6,30},{7,5},{8,0},{9,15},{... | collective-permute-start | bytes 589832 | tf_op jit(solution)/shard_map/ppermute | solution.py:394
  39.0 6.3 %collective-permute-start.13 = (bf16[3,128,256]{2,1,0:T(8,128)(2,1)S(1)}, bf16[3,128,256]{2,1,0:T(8,128)(2,1)S(1)}, u32[]{:S(2)}, u32[]{:S(2)}) collective-permute-start(bf16[3,128,256]{2,1,0:T(8,128)(2,1)S(1)} %get-tuple-element.36.own), channel_id=1, source_target_pairs={{0,16},{1,5},{2,18},{3,7},{4,20},{5,1},{6,22},{7,3},{8,24},{9,13},... | collective-permute-start | bytes 589832 | tf_op jit(solution)/shard_map/ppermute | solution.py:394
  45.4 8.2 %collective-permute-start.17 = (bf16[5,128,256]{2,1,0:T(8,128)(2,1)S(1)}, bf16[5,128,256]{2,1,0:T(8,128)(2,1)S(1)}, u32[]{:S(2)}, u32[]{:S(2)}) collective-permute-start(bf16[5,128,256]{2,1,0:T(8,128)(2,1)S(1)} %gather_step.1.part.p0), channel_id=1, source_target_pairs={{0,1},{1,0},{2,3},{3,2},{4,5},{5,4},{6,7},{7,6},{8,9},{9,8},{10,11... | collective-permute-start | bytes 983048 | tf_op jit(solution)/shard_map/ppermute | solution.py:381
  49.6 7.4 %collective-permute-start.14 = (bf16[5,128,256]{2,1,0:T(8,128)(2,1)S(1)}, bf16[5,128,256]{2,1,0:T(8,128)(2,1)S(1)}, u32[]{:S(2)}, u32[]{:S(2)}) collective-permute-start(bf16[5,128,256]{2,1,0:T(8,128)(2,1)S(1)} %gather_step.1.part.p0), channel_id=1, source_target_pairs={{0,2},{1,9},{2,4},{3,11},{4,6},{5,13},{6,0},{7,15},{8,10},{9,17},{... | collective-permute-start | bytes 983048 | tf_op jit(solution)/shard_map/ppermute | solution.py:394
  50.7 9.1 %collective-permute-start.15 = (bf16[5,128,256]{2,1,0:T(8,128)(2,1)S(1)}, bf16[5,128,256]{2,1,0:T(8,128)(2,1)S(1)}, u32[]{:S(2)}, u32[]{:S(2)}) collective-permute-start(bf16[5,128,256]{2,1,0:T(8,128)(2,1)S(1)} %gather_step.1.part.p0), channel_id=1, source_target_pairs={{0,6},{1,25},{2,0},{3,27},{4,2},{5,29},{6,4},{7,31},{8,14},{9,1},{... | collective-permute-start | bytes 983048 | tf_op jit(solution)/shard_map/ppermute | solution.py:394
  52.3 8.4 %collective-permute-start.16 = (bf16[5,128,256]{2,1,0:T(8,128)(2,1)S(1)}, bf16[5,128,256]{2,1,0:T(8,128)(2,1)S(1)}, u32[]{:S(2)}, u32[]{:S(2)}) collective-permute-start(bf16[5,128,256]{2,1,0:T(8,128)(2,1)S(1)} %gather_step.1.part.p0), channel_id=1, source_target_pairs={{0,4},{1,17},{2,6},{3,19},{4,0},{5,21},{6,2},{7,23},{8,12},{9,25},... | collective-permute-start | bytes 983048 | tf_op jit(solution)/shard_map/ppermute | solution.py:394
  60.7 3.1 %collective-permute-start.18 = (bf16[5,128,256]{2,1,0:T(8,128)(2,1)S(1)}, bf16[5,128,256]{2,1,0:T(8,128)(2,1)S(1)}, u32[]{:S(2)}, u32[]{:S(2)}) collective-permute-start(bf16[5,128,256]{2,1,0:T(8,128)(2,1)S(1)} %get-tuple-element.40.refs_0_.p3), channel_id=1, source_target_pairs={{0,1},{1,0},{2,3},{3,2},{4,5},{5,4},{6,7},{7,6},{8,9},{9,8},{10,11... | collective-permute-start | bytes 983048 | tf_op jit(solution)/shard_map/ppermute | solution.py:381
  62.0 1.9 %collective-permute-start.19 = (bf16[5,128,256]{2,1,0:T(8,128)(2,1)S(1)}, bf16[5,128,256]{2,1,0:T(8,128)(2,1)S(1)}, u32[]{:S(2)}, u32[]{:S(2)}) collective-permute-start(bf16[5,128,256]{2,1,0:T(8,128)(2,1)S(1)} %get-tuple-element.41.refs_1_.p1), channel_id=1, source_target_pairs={{0,1},{1,0},{2,3},{3,2},{4,5},{5,4},{6,7},{7,6},{8,9},{9,8},{10,11... | collective-permute-start | bytes 983048 | tf_op jit(solution)/shard_map/ppermute | solution.py:381
  62.0 2.2 %collective-permute-start.20 = (bf16[5,128,256]{2,1,0:T(8,128)(2,1)S(1)}, bf16[5,128,256]{2,1,0:T(8,128)(2,1)S(1)}, u32[]{:S(2)}, u32[]{:S(2)}) collective-permute-start(bf16[5,128,256]{2,1,0:T(8,128)(2,1)S(1)} %get-tuple-element.42.refs_2_.p2), channel_id=1, source_target_pairs={{0,1},{1,0},{2,3},{3,2},{4,5},{5,4},{6,7},{7,6},{8,9},{9,8},{10,11... | collective-permute-start | bytes 983048 | tf_op jit(solution)/shard_map/ppermute | solution.py:381
  65.4 6.0 %collective-permute-start.21 = (bf16[2,128,256]{2,1,0:T(8,128)(2,1)S(1)}, bf16[2,128,256]{2,1,0:T(8,128)(2,1)S(1)}, u32[]{:S(2)}, u32[]{:S(2)}) collective-permute-start(bf16[2,128,256]{2,1,0:T(8,128)(2,1)S(1)} %get-tuple-element.44), channel_id=1, source_target_pairs={{0,32},{32,64},{64,96},{96,0},{1,33},{33,65},{65,97},{97,1},{2,34}... | collective-permute-start | bytes 393224 | tf_op jit(solution)/shard_map/ppermute | solution.py:377
  65.8 5.6 %collective-permute-start.22 = (bf16[2,128,256]{2,1,0:T(8,128)(2,1)S(1)}, bf16[2,128,256]{2,1,0:T(8,128)(2,1)S(1)}, u32[]{:S(2)}, u32[]{:S(2)}) collective-permute-start(bf16[2,128,256]{2,1,0:T(8,128)(2,1)S(1)} %get-tuple-element.45), channel_id=1, source_target_pairs={{0,96},{32,0},{64,32},{96,64},{1,97},{33,1},{65,33},{97,65},{2,98}... | collective-permute-start | bytes 393224 | tf_op jit(solution)/shard_map/ppermute | solution.py:377
  68.1 5.3 %collective-permute-start.23 = (bf16[2,128,256]{2,1,0:T(8,128)(2,1)S(1)}, bf16[2,128,256]{2,1,0:T(8,128)(2,1)S(1)}, u32[]{:S(2)}, u32[]{:S(2)}) collective-permute-start(bf16[2,128,256]{2,1,0:T(8,128)(2,1)S(1)} %get-tuple-element.46), channel_id=1, source_target_pairs={{0,64},{32,96},{64,0},{96,32},{1,65},{33,97},{65,1},{97,33},{2,66}... | collective-permute-start | bytes 393224 | tf_op jit(solution)/shard_map/ppermute | solution.py:377

commit v6 on v5

--- a/solution.py
+++ b/solution.py
@@ -334,24 +334,21 @@
     )(table, values, *mine, *others, partial)
 
 
-def kept_kernel(half, offsets, table, values, r1, r2, r3, partial, after, own):
+def kept_kernel(half, offset, table, values, part, partial, after, own):
     del after
-    total = partial[0]
-    for a, part in zip(offsets, (r1, r2, r3)):
-        total = backward_tiles(half, a, 0, table, values, part, total)
-    own[...] = total
-
-
-def kept_quarter(half, offsets, table, values, rest, partial, after):
-    return pl.pallas_call(
-        functools.partial(kept_kernel, half, offsets),
+    own[...] = backward_tiles(half, offset, 0, table, values, part, partial[0])
+
+
+def kept_quarter(half, offset, table, values, part, partial, after):
+    return pl.pallas_call(
+        functools.partial(kept_kernel, half, offset),
         out_shape=sds((128, 256), F32),
-        in_specs=[SM] + [VM] * 5 + [AN],
+        in_specs=[SM] + [VM] * 3 + [AN],
         out_specs=VM,
         name="backward_kept",
         cost_estimate=BACK_COST,
         compiler_params=PARAMS,
-    )(table, values, *rest, partial, after)
+    )(table, values, part, partial, after)
 
 
 def finish_kernel(scale, own, own_term, g3, g1, g2, grad_in, grad_weight):
@@ -426,8 +423,9 @@
     other_rest = [swap_cores(v) for v in rest]
     partial = backward(1, ORDER[-1], table, values, rest, partial)
     mine, others = (first, *rest), (other_first, *other_rest)
-    own_term, *sends = last(0, ORDER[-1], table, values, mine, others, partial)
-    own = kept_quarter(0, ORDER[-1], table, values, other_rest, partial, own_term)
+    partial = backward(0, ORDER[-1][:2], table, values, other_rest[:2], partial)
+    own_term, *sends = last(0, ORDER[-1][2:], table, values, mine, others, partial)
+    own = kept_quarter(0, ORDER[-1][2], table, values, other_rest[2], partial, own_term)
     got = shift_each(row_shift, sends, -1)
     grad_in, grad_weight = finish(32768.0 ** -0.5, own, own_term, got)
     return output, grad_in, grad_weight

time: 75 us -> 75 us (level)
    pallas_call x2 -> x3, Pallas kernels: 1.91 us -> 2.89 us  [backward(): pl.pallas_call(functools.partial(backward_kernel, half, offsets, partial...]
  transfers between devices with their start and end apart: 24 -> 24, of which waited for: 14 -> 12; matrix products, arithmetic and copies ran while one was open for 0% -> 0% of each run, Pallas kernels for 15% -> 16%
where the time goes in v6:
time: 75 us; the launch traced here: 74.7 us
  starting transfers between devices  33.1 us (44%)
  waiting for transfers between devices  24.6 us (33%)
  Pallas kernels  15.5 us (21%)
  between operations  1.49 us (2%)
    ppermute x12, waiting for transfers between devices, chip_shift(): return lax.ppermute(value, 'col', pairs)  19.1 us
    ppermute x12, starting transfers between devices, chip_shift(): return lax.ppermute(value, 'col', pairs)  17.4 us
    ppermute x6, starting transfers between devices, row_shift(): return lax.ppermute(value, 'row', [(i, (i + k) % 4) for i in range(4)])  8.07 us
    ppermute x6, starting transfers between devices, swap_cores(): return lax.ppermute(value, 'col', [(j, j ^ 1) for j in range(32)])  7.64 us
    ppermute x6, waiting for transfers between devices, row_shift(): return lax.ppermute(value, 'row', [(i, (i + k) % 4) for i in range(4)])  5.48 us
    pallas_call x4, Pallas kernels, forward(): pl.pallas_call(functools.partial(forward_kernel, start, count // FWD_TILE...  4.99 us
    pallas_call x1, Pallas kernels, load(): pl.pallas_call(load_kernel, out_shape=(sds(values.shape, BF), sds(feature...  4.02 us
    pallas_call x3, Pallas kernels, backward(): pl.pallas_call(functools.partial(backward_kernel, half, offsets, partial...  2.89 us
  transfers between devices with their start and end apart: 24, of which 12 were waited for; matrix products, arithmetic and copies ran while one was open for 0% of the time, Pallas kernels for 16%

profile of v6, /device:TPU:1, one launch (start us, length us, event | category | flops | bytes accessed | tf_op | source)
XLA Modules:
  0.0 74.7 jit_solution(14503407871258324707)
XLA Ops:
  0.6 2.2 %collective-permute-start = (bf16[256,128]{1,0:T(8,128)(2,1)}, bf16[256,128]{1,0:T(8,128)(2,1)S(1)}, u32[]{:S(2)}, u32[]{:S(2)}) collective-permute-start(bf16[256,128]{1,0:T(8,128)(2,1)} %features.1), channel_id=1, source_target_pairs={{0,32},{32,64},{64,96},{96,0},{1,33},{33,65},{65,97},{97,1},{2,34}... | collective-permute-start | bytes 196616 | tf_op jit(solution)/shard_map/ppermute | solution.py:374
  2.8 1.5 %collective-permute-start.1 = (bf16[256,128]{1,0:T(8,128)(2,1)}, bf16[256,128]{1,0:T(8,128)(2,1)S(1)}, u32[]{:S(2)}, u32[]{:S(2)}) collective-permute-start(bf16[256,128]{1,0:T(8,128)(2,1)} %features.1), channel_id=1, source_target_pairs={{0,96},{32,0},{64,32},{96,64},{1,97},{33,1},{65,33},{97,65},{2,98}... | collective-permute-start | bytes 196616 | tf_op jit(solution)/shard_map/ppermute | solution.py:374
  4.3 1.6 %collective-permute-start.2 = (bf16[256,128]{1,0:T(8,128)(2,1)}, bf16[256,128]{1,0:T(8,128)(2,1)S(1)}, u32[]{:S(2)}, u32[]{:S(2)}) collective-permute-start(bf16[256,128]{1,0:T(8,128)(2,1)} %features.1), channel_id=1, source_target_pairs={{0,64},{32,96},{64,0},{96,32},{1,65},{33,97},{65,1},{97,33},{2,66}... | collective-permute-start | bytes 196616 | tf_op jit(solution)/shard_map/ppermute | solution.py:374
  6.6 4.0 %load.1 = (bf16[320,128,128]{2,1,0:T(8,128)(2,1)S(1)}, bf16[256,128]{1,0:T(8,128)(2,1)S(1)}, s32[512]{0:T(512)S(4)}) custom-call(bf16[320,128,128]{2,1,0:T(8,128)(2,1)} %bitcast.1, bf16[256,128]{1,0:T(8,128)(2,1)} %features.1, s32[1,1,320]{2,1,0:T(1,128)} %rows_in.1, s32[1,1,320]{2,1,0:T(1,128)} %cols_in.1, s32[1,1]{1,0:T(1,128)S(6)} %copy.16.live), custom_call_target="tpu_custom_call" | custom-call | bytes 11534336 | tf_op jit(solution)/shard_map/load/pallas_call | solution.py:101
  10.6 1.8 %forward_other.1 = bf16[3072,128]{1,0:T(8,128)(2,1)S(1)} custom-call(s32[512]{0:T(512)S(4)} %get-tuple-element.26.table, bf16[320,128,128]{2,1,0:T(8,128)(2,1)S(1)} %get-tuple-element.27.values, bf16[256,128]{1,0:T(8,128)(2,1)S(1)} %get-tuple-element.28.x0, bf16[256,128]{1,0:T(8,128)(2,1)S(1)} %collective-permute-done.x1, ...), custom_call_target="tpu_custom_call" | custom-call | flops 805306368 | bytes 786432 | tf_op jit(solution)/shard_map/forward_other/pallas_call | solution.py:138
  12.4 1.6 %collective-permute-start.4 = (bf16[3072,128]{1,0:T(8,128)(2,1)S(1)}, bf16[3072,128]{1,0:T(8,128)(2,1)S(1)}, u32[]{:S(2)}, u32[]{:S(2)}) collective-permute-start(bf16[3072,128]{1,0:T(8,128)(2,1)S(1)} %forward_other.1), channel_id=1, source_target_pairs={{0,1},{1,0},{2,3},{3,2},{4,5},{5,4},{6,7},{7,6},{8,9},{9,8},{10,11... | collective-permute-start | bytes 2359304 | tf_op jit(solution)/shard_map/ppermute | solution.py:378
  14.0 1.8 %forward_sent.1.refs_0_.kept = f32[3072,128]{1,0:T(8,128)S(1)} custom-call(s32[512]{0:T(512)S(4)} %get-tuple-element.26.table, bf16[320,128,128]{2,1,0:T(8,128)(2,1)S(1)} %get-tuple-element.27.values, bf16[256,128]{1,0:T(8,128)(2,1)S(1)} %get-tuple-element.28.x0, bf16[256,128]{1,0:T(8,128)(2,1)S(1)} %collective-permute-done.x1, ...), custom_call_target="tpu_custom_call" | custom-call | flops 805306368 | bytes 786432 | tf_op jit(solution)/shard_map/forward_sent/pallas_call | solution.py:138
  16.8 1.7 %collective-permute-start.5 = (bf16[1024,128]{1,0:T(8,128)(2,1)S(1)}, bf16[1024,128]{1,0:T(8,128)(2,1)S(1)}, u32[]{:S(2)}, u32[]{:S(2)}) collective-permute-start(bf16[1024,128]{1,0:T(8,128)(2,1)S(1)} %get-tuple-element.29), channel_id=1, source_target_pairs={{0,2},{1,9},{2,4},{3,11},{4,6},{5,13},{6,0},{7,15},{8,10},{9,17},{... | collective-permute-start | bytes 786440 | tf_op jit(solution)/shard_map/ppermute | solution.py:391
  18.5 2.2 %collective-permute-start.6 = (bf16[1024,128]{1,0:T(8,128)(2,1)S(1)}, bf16[1024,128]{1,0:T(8,128)(2,1)S(1)}, u32[]{:S(2)}, u32[]{:S(2)}) collective-permute-start(bf16[1024,128]{1,0:T(8,128)(2,1)S(1)} %get-tuple-element.30), channel_id=1, source_target_pairs={{0,6},{1,25},{2,0},{3,27},{4,2},{5,29},{6,4},{7,31},{8,14},{9,1},{... | collective-permute-start | bytes 786440 | tf_op jit(solution)/shard_map/ppermute | solution.py:391
  20.7 1.2 %collective-permute-start.7 = (bf16[1024,128]{1,0:T(8,128)(2,1)S(1)}, bf16[1024,128]{1,0:T(8,128)(2,1)S(1)}, u32[]{:S(2)}, u32[]{:S(2)}) collective-permute-start(bf16[1024,128]{1,0:T(8,128)(2,1)S(1)} %get-tuple-element.31), channel_id=1, source_target_pairs={{0,4},{1,17},{2,6},{3,19},{4,0},{5,21},{6,2},{7,23},{8,12},{9,25},... | collective-permute-start | bytes 786440 | tf_op jit(solution)/shard_map/ppermute | solution.py:391
  22.6 1.9 %collective-permute-done.5.g1 = bf16[1024,128]{1,0:T(8,128)(2,1)S(1)} collective-permute-done((bf16[1024,128]{1,0:T(8,128)(2,1)S(1)}, bf16[1024,128]{1,0:T(8,128)(2,1)S(1)}, u32[]{:S(2)}, u32[]{:S(2)}) %collective-permute-start.5) | collective-permute-done | bytes 262176 | tf_op jit(solution)/shard_map/ppermute | solution.py:391
  24.5 2.3 %collective-permute-done.6.g3 = bf16[1024,128]{1,0:T(8,128)(2,1)S(1)} collective-permute-done((bf16[1024,128]{1,0:T(8,128)(2,1)S(1)}, bf16[1024,128]{1,0:T(8,128)(2,1)S(1)}, u32[]{:S(2)}, u32[]{:S(2)}) %collective-permute-start.6) | collective-permute-done | bytes 262176 | tf_op jit(solution)/shard_map/ppermute | solution.py:391
  26.8 1.5 %collective-permute-done.7.g2 = bf16[1024,128]{1,0:T(8,128)(2,1)S(1)} collective-permute-done((bf16[1024,128]{1,0:T(8,128)(2,1)S(1)}, bf16[1024,128]{1,0:T(8,128)(2,1)S(1)}, u32[]{:S(2)}, u32[]{:S(2)}) %collective-permute-start.7) | collective-permute-done | bytes 262176 | tf_op jit(solution)/shard_map/ppermute | solution.py:391
  28.5 2.8 %collective-permute-start.10 = (bf16[256,128]{1,0:T(8,128)(2,1)S(1)}, bf16[256,128]{1,0:T(8,128)(2,1)S(1)}, u32[]{:S(2)}, u32[]{:S(2)}) collective-permute-start(bf16[256,128]{1,0:T(8,128)(2,1)S(1)} %get-tuple-element.35), channel_id=1, source_target_pairs={{0,16},{1,5},{2,18},{3,7},{4,20},{5,1},{6,22},{7,3},{8,24},{9,13},... | collective-permute-start | bytes 196616 | tf_op jit(solution)/shard_map/ppermute | solution.py:391
  31.7 2.3 %collective-permute-start.9 = (bf16[256,128]{1,0:T(8,128)(2,1)S(1)}, bf16[256,128]{1,0:T(8,128)(2,1)S(1)}, u32[]{:S(2)}, u32[]{:S(2)}) collective-permute-start(bf16[256,128]{1,0:T(8,128)(2,1)S(1)} %get-tuple-element.34), channel_id=1, source_target_pairs={{0,24},{1,7},{2,26},{3,1},{4,28},{5,3},{6,30},{7,5},{8,0},{9,15},{... | collective-permute-start | bytes 196616 | tf_op jit(solution)/shard_map/ppermute | solution.py:391
  34.0 1.6 %collective-permute-done.8.g1 = bf16[256,128]{1,0:T(8,128)(2,1)S(1)} collective-permute-done((bf16[256,128]{1,0:T(8,128)(2,1)S(1)}, bf16[256,128]{1,0:T(8,128)(2,1)S(1)}, u32[]{:S(2)}, u32[]{:S(2)}) %collective-permute-start.8) | collective-permute-done | bytes 65568 | tf_op jit(solution)/shard_map/ppermute | solution.py:391
  36.3 2.7 %collective-permute-start.12 = (bf16[3,128,256]{2,1,0:T(8,128)(2,1)S(1)}, bf16[3,128,256]{2,1,0:T(8,128)(2,1)S(1)}, u32[]{:S(2)}, u32[]{:S(2)}) collective-permute-start(bf16[3,128,256]{2,1,0:T(8,128)(2,1)S(1)} %get-tuple-element.36.own), channel_id=1, source_target_pairs={{0,24},{1,7},{2,26},{3,1},{4,28},{5,3},{6,30},{7,5},{8,0},{9,15},{... | collective-permute-start | bytes 589832 | tf_op jit(solution)/shard_map/ppermute | solution.py:391
  39.0 1.1 %collective-permute-start.13 = (bf16[3,128,256]{2,1,0:T(8,128)(2,1)S(1)}, bf16[3,128,256]{2,1,0:T(8,128)(2,1)S(1)}, u32[]{:S(2)}, u32[]{:S(2)}) collective-permute-start(bf16[3,128,256]{2,1,0:T(8,128)(2,1)S(1)} %get-tuple-element.36.own), channel_id=1, source_target_pairs={{0,16},{1,5},{2,18},{3,7},{4,20},{5,1},{6,22},{7,3},{8,24},{9,13},... | collective-permute-start | bytes 589832 | tf_op jit(solution)/shard_map/ppermute | solution.py:391
  40.1 1.9 %collective-permute-done.11.g3 = bf16[3,128,256]{2,1,0:T(8,128)(2,1)S(1)} collective-permute-done((bf16[3,128,256]{2,1,0:T(8,128)(2,1)S(1)}, bf16[3,128,256]{2,1,0:T(8,128)(2,1)S(1)}, u32[]{:S(2)}, u32[]{:S(2)}) %collective-permute-start.11) | collective-permute-done | bytes 196640 | tf_op jit(solution)/shard_map/ppermute | solution.py:391
  42.0 1.7 %collective-permute-done.12.g1 = bf16[3,128,256]{2,1,0:T(8,128)(2,1)S(1)} collective-permute-done((bf16[3,128,256]{2,1,0:T(8,128)(2,1)S(1)}, bf16[3,128,256]{2,1,0:T(8,128)(2,1)S(1)}, u32[]{:S(2)}, u32[]{:S(2)}) %collective-permute-start.12) | collective-permute-done | bytes 196640 | tf_op jit(solution)/shard_map/ppermute | solution.py:391
  43.8 1.5 %collective-permute-done.13.g2 = bf16[3,128,256]{2,1,0:T(8,128)(2,1)S(1)} collective-permute-done((bf16[3,128,256]{2,1,0:T(8,128)(2,1)S(1)}, bf16[3,128,256]{2,1,0:T(8,128)(2,1)S(1)}, u32[]{:S(2)}, u32[]{:S(2)}) %collective-permute-start.13) | collective-permute-done | bytes 196640 | tf_op jit(solution)/shard_map/ppermute | solution.py:391
  45.4 4.2 %collective-permute-start.17 = (bf16[5,128,256]{2,1,0:T(8,128)(2,1)S(1)}, bf16[5,128,256]{2,1,0:T(8,128)(2,1)S(1)}, u32[]{:S(2)}, u32[]{:S(2)}) collective-permute-start(bf16[5,128,256]{2,1,0:T(8,128)(2,1)S(1)} %gather_step.1.part.p0), channel_id=1, source_target_pairs={{0,1},{1,0},{2,3},{3,2},{4,5},{5,4},{6,7},{7,6},{8,9},{9,8},{10,11... | collective-permute-start | bytes 983048 | tf_op jit(solution)/shard_map/ppermute | solution.py:378
  49.6 1.1 %collective-permute-start.14 = (bf16[5,128,256]{2,1,0:T(8,128)(2,1)S(1)}, bf16[5,128,256]{2,1,0:T(8,128)(2,1)S(1)}, u32[]{:S(2)}, u32[]{:S(2)}) collective-permute-start(bf16[5,128,256]{2,1,0:T(8,128)(2,1)S(1)} %gather_step.1.part.p0), channel_id=1, source_target_pairs={{0,2},{1,9},{2,4},{3,11},{4,6},{5,13},{6,0},{7,15},{8,10},{9,17},{... | collective-permute-start | bytes 983048 | tf_op jit(solution)/shard_map/ppermute | solution.py:391
  50.7 1.6 %collective-permute-start.15 = (bf16[5,128,256]{2,1,0:T(8,128)(2,1)S(1)}, bf16[5,128,256]{2,1,0:T(8,128)(2,1)S(1)}, u32[]{:S(2)}, u32[]{:S(2)}) collective-permute-start(bf16[5,128,256]{2,1,0:T(8,128)(2,1)S(1)} %gather_step.1.part.p0), channel_id=1, source_target_pairs={{0,6},{1,25},{2,0},{3,27},{4,2},{5,29},{6,4},{7,31},{8,14},{9,1},{... | collective-permute-start | bytes 983048 | tf_op jit(solution)/shard_map/ppermute | solution.py:391
  52.5 1.1 %backward_first.1 = (f32[4,128,256]{2,1,0:T(8,128)S(1)}, bf16[256,256]{1,0:T(8,128)(2,1)}) custom-call(s32[512]{0:T(512)S(4)} %get-tuple-element.26.table, bf16[320,128,128]{2,1,0:T(8,128)(2,1)S(1)} %get-tuple-element.27.values, bf16[5,128,256]{2,1,0:T(8,128)(2,1)S(1)} %gather_step.1.part.p0, f32[256,256]{1,0:T(8,128)S(1)} %get-tuple-element.37.active), custom_call_target="tpu_custom_call" | custom-call | flops 1 | bytes 1 | tf_op jit(solution)/shard_map/backward_first/pallas_call | solution.py:283
  54.1 2.9 %collective-permute-done.14.refs_0_ = bf16[5,128,256]{2,1,0:T(8,128)(2,1)S(1)} collective-permute-done((bf16[5,128,256]{2,1,0:T(8,128)(2,1)S(1)}, bf16[5,128,256]{2,1,0:T(8,128)(2,1)S(1)}, u32[]{:S(2)}, u32[]{:S(2)}) %collective-permute-start.14) | collective-permute-done | bytes 327712 | tf_op jit(solution)/shard_map/ppermute | solution.py:391
  57.0 2.8 %collective-permute-done.15.refs_1_ = bf16[5,128,256]{2,1,0:T(8,128)(2,1)S(1)} collective-permute-done((bf16[5,128,256]{2,1,0:T(8,128)(2,1)S(1)}, bf16[5,128,256]{2,1,0:T(8,128)(2,1)S(1)}, u32[]{:S(2)}, u32[]{:S(2)}) %collective-permute-start.15) | collective-permute-done | bytes 327712 | tf_op jit(solution)/shard_map/ppermute | solution.py:391
  60.7 1.3 %collective-permute-start.19 = (bf16[5,128,256]{2,1,0:T(8,128)(2,1)S(1)}, bf16[5,128,256]{2,1,0:T(8,128)(2,1)S(1)}, u32[]{:S(2)}, u32[]{:S(2)}) collective-permute-start(bf16[5,128,256]{2,1,0:T(8,128)(2,1)S(1)} %get-tuple-element.41.refs_0_.p3), channel_id=1, source_target_pairs={{0,1},{1,0},{2,3},{3,2},{4,5},{5,4},{6,7},{7,6},{8,9},{9,8},{10,11... | collective-permute-start | bytes 983048 | tf_op jit(solution)/shard_map/ppermute | solution.py:378
  62.5 1.4 %backward_1_3.1.refs_2_ = f32[4,128,256]{2,1,0:T(8,128)S(1)} custom-call(s32[512]{0:T(512)S(4)} %get-tuple-element.26.table, bf16[320,128,128]{2,1,0:T(8,128)(2,1)S(1)} %get-tuple-element.27.values, bf16[5,128,256]{2,1,0:T(8,128)(2,1)S(1)} %get-tuple-element.41.refs_0_.p3, bf16[5,128,256]{2,1,0:T(8,128)(2,1)S(1)} %get-tuple-element.42.refs_1_.p1, ...), custom_call_target="tpu_custom_call" | custom-call | flops 1 | bytes 1 | tf_op jit(solution)/shard_map/backward_1_3/pallas_call | solution.py:265
  65.9 2.3 %collective-permute-start.22 = (bf16[2,128,256]{2,1,0:T(8,128)(2,1)S(1)}, bf16[2,128,256]{2,1,0:T(8,128)(2,1)S(1)}, u32[]{:S(2)}, u32[]{:S(2)}) collective-permute-start(bf16[2,128,256]{2,1,0:T(8,128)(2,1)S(1)} %get-tuple-element.45), channel_id=1, source_target_pairs={{0,96},{32,0},{64,32},{96,64},{1,97},{33,1},{65,33},{97,65},{2,98}... | collective-permute-start | bytes 393224 | tf_op jit(solution)/shard_map/ppermute | solution.py:374
  68.5 3.1 %collective-permute-done.21.g3 = bf16[2,128,256]{2,1,0:T(8,128)(2,1)S(1)} collective-permute-done((bf16[2,128,256]{2,1,0:T(8,128)(2,1)S(1)}, bf16[2,128,256]{2,1,0:T(8,128)(2,1)S(1)}, u32[]{:S(2)}, u32[]{:S(2)}) %collective-permute-start.21) | collective-permute-done | bytes 131104 | tf_op jit(solution)/shard_map/ppermute | solution.py:374
  71.6 2.3 %collective-permute-done.23.g2 = bf16[2,128,256]{2,1,0:T(8,128)(2,1)S(1)} collective-permute-done((bf16[2,128,256]{2,1,0:T(8,128)(2,1)S(1)}, bf16[2,128,256]{2,1,0:T(8,128)(2,1)S(1)}, u32[]{:S(2)}, u32[]{:S(2)}) %collective-permute-start.23) | collective-permute-done | bytes 131104 | tf_op jit(solution)/shard_map/ppermute | solution.py:374
  (37 shorter events, 8.1 us)
Async XLA Ops:
  0.6 10.0 %collective-permute-start = (bf16[256,128]{1,0:T(8,128)(2,1)}, bf16[256,128]{1,0:T(8,128)(2,1)S(1)}, u32[]{:S(2)}, u32[]{:S(2)}) collective-permute-start(bf16[256,128]{1,0:T(8,128)(2,1)} %features.1), channel_id=1, source_target_pairs={{0,32},{32,64},{64,96},{96,0},{1,33},{33,65},{65,97},{97,1},{2,34}... | collective-permute-start | bytes 196616 | tf_op jit(solution)/shard_map/ppermute | solution.py:374
  2.8 7.8 %collective-permute-start.1 = (bf16[256,128]{1,0:T(8,128)(2,1)}, bf16[256,128]{1,0:T(8,128)(2,1)S(1)}, u32[]{:S(2)}, u32[]{:S(2)}) collective-permute-start(bf16[256,128]{1,0:T(8,128)(2,1)} %features.1), channel_id=1, source_target_pairs={{0,96},{32,0},{64,32},{96,64},{1,97},{33,1},{65,33},{97,65},{2,98}... | collective-permute-start | bytes 196616 | tf_op jit(solution)/shard_map/ppermute | solution.py:374
  4.3 6.3 %collective-permute-start.2 = (bf16[256,128]{1,0:T(8,128)(2,1)}, bf16[256,128]{1,0:T(8,128)(2,1)S(1)}, u32[]{:S(2)}, u32[]{:S(2)}) collective-permute-start(bf16[256,128]{1,0:T(8,128)(2,1)} %features.1), channel_id=1, source_target_pairs={{0,64},{32,96},{64,0},{96,32},{1,65},{33,97},{65,1},{97,33},{2,66}... | collective-permute-start | bytes 196616 | tf_op jit(solution)/shard_map/ppermute | solution.py:374
  12.4 4.2 %collective-permute-start.4 = (bf16[3072,128]{1,0:T(8,128)(2,1)S(1)}, bf16[3072,128]{1,0:T(8,128)(2,1)S(1)}, u32[]{:S(2)}, u32[]{:S(2)}) collective-permute-start(bf16[3072,128]{1,0:T(8,128)(2,1)S(1)} %forward_other.1), channel_id=1, source_target_pairs={{0,1},{1,0},{2,3},{3,2},{4,5},{5,4},{6,7},{7,6},{8,9},{9,8},{10,11... | collective-permute-start | bytes 2359304 | tf_op jit(solution)/shard_map/ppermute | solution.py:378
  16.5 19.1 %copy-start = (bf16[256,256]{1,0:T(8,128)(2,1)S(1)}, bf16[256,256]{1,0:T(8,128)(2,1)}, u32[]{:S(2)}) copy-start(bf16[256,256]{1,0:T(8,128)(2,1)} %cotangent.1) | copy-start | bytes 393220
  16.5 19.1 %copy-start.1 = (bf16[128,256]{1,0:T(8,128)(2,1)S(1)}, bf16[128,256]{1,0:T(8,128)(2,1)}, u32[]{:S(2)}) copy-start(bf16[128,256]{1,0:T(8,128)(2,1)} %weight.1) | copy-start | bytes 196612
  16.6 6.1 %collective-permute-start.3 = (bf16[1024,128]{1,0:T(8,128)(2,1)S(1)}, bf16[1024,128]{1,0:T(8,128)(2,1)S(1)}, u32[]{:S(2)}, u32[]{:S(2)}) collective-permute-start(bf16[1024,128]{1,0:T(8,128)(2,1)S(1)} %forward_rest.1), channel_id=1, source_target_pairs={{0,1},{1,0},{2,3},{3,2},{4,5},{5,4},{6,7},{7,6},{8,9},{9,8},{10,11... | collective-permute-start | bytes 786440 | tf_op jit(solution)/shard_map/ppermute | solution.py:378
  16.8 7.7 %collective-permute-start.5 = (bf16[1024,128]{1,0:T(8,128)(2,1)S(1)}, bf16[1024,128]{1,0:T(8,128)(2,1)S(1)}, u32[]{:S(2)}, u32[]{:S(2)}) collective-permute-start(bf16[1024,128]{1,0:T(8,128)(2,1)S(1)} %get-tuple-element.29), channel_id=1, source_target_pairs={{0,2},{1,9},{2,4},{3,11},{4,6},{5,13},{6,0},{7,15},{8,10},{9,17},{... | collective-permute-start | bytes 786440 | tf_op jit(solution)/shard_map/ppermute | solution.py:391
  18.5 8.3 %collective-permute-start.6 = (bf16[1024,128]{1,0:T(8,128)(2,1)S(1)}, bf16[1024,128]{1,0:T(8,128)(2,1)S(1)}, u32[]{:S(2)}, u32[]{:S(2)}) collective-permute-start(bf16[1024,128]{1,0:T(8,128)(2,1)S(1)} %get-tuple-element.30), channel_id=1, source_target_pairs={{0,6},{1,25},{2,0},{3,27},{4,2},{5,29},{6,4},{7,31},{8,14},{9,1},{... | collective-permute-start | bytes 786440 | tf_op jit(solution)/shard_map/ppermute | solution.py:391
  20.7 7.7 %collective-permute-start.7 = (bf16[1024,128]{1,0:T(8,128)(2,1)S(1)}, bf16[1024,128]{1,0:T(8,128)(2,1)S(1)}, u32[]{:S(2)}, u32[]{:S(2)}) collective-permute-start(bf16[1024,128]{1,0:T(8,128)(2,1)S(1)} %get-tuple-element.31), channel_id=1, source_target_pairs={{0,4},{1,17},{2,6},{3,19},{4,0},{5,21},{6,2},{7,23},{8,12},{9,25},... | collective-permute-start | bytes 786440 | tf_op jit(solution)/shard_map/ppermute | solution.py:391
  28.5 5.5 %collective-permute-start.10 = (bf16[256,128]{1,0:T(8,128)(2,1)S(1)}, bf16[256,128]{1,0:T(8,128)(2,1)S(1)}, u32[]{:S(2)}, u32[]{:S(2)}) collective-permute-start(bf16[256,128]{1,0:T(8,128)(2,1)S(1)} %get-tuple-element.35), channel_id=1, source_target_pairs={{0,16},{1,5},{2,18},{3,7},{4,20},{5,1},{6,22},{7,3},{8,24},{9,13},... | collective-permute-start | bytes 196616 | tf_op jit(solution)/shard_map/ppermute | solution.py:391
  31.3 4.3 %collective-permute-start.8 = (bf16[256,128]{1,0:T(8,128)(2,1)S(1)}, bf16[256,128]{1,0:T(8,128)(2,1)S(1)}, u32[]{:S(2)}, u32[]{:S(2)}) collective-permute-start(bf16[256,128]{1,0:T(8,128)(2,1)S(1)} %get-tuple-element.33), channel_id=1, source_target_pairs={{0,8},{1,3},{2,10},{3,5},{4,12},{5,7},{6,14},{7,1},{8,16},{9,11},{... | collective-permute-start | bytes 196616 | tf_op jit(solution)/shard_map/ppermute | solution.py:391
  31.7 4.0 %collective-permute-start.9 = (bf16[256,128]{1,0:T(8,128)(2,1)S(1)}, bf16[256,128]{1,0:T(8,128)(2,1)S(1)}, u32[]{:S(2)}, u32[]{:S(2)}) collective-permute-start(bf16[256,128]{1,0:T(8,128)(2,1)S(1)} %get-tuple-element.34), channel_id=1, source_target_pairs={{0,24},{1,7},{2,26},{3,1},{4,28},{5,3},{6,30},{7,5},{8,0},{9,15},{... | collective-permute-start | bytes 196616 | tf_op jit(solution)/shard_map/ppermute | solution.py:391
  36.2 5.8 %collective-permute-start.11 = (bf16[3,128,256]{2,1,0:T(8,128)(2,1)S(1)}, bf16[3,128,256]{2,1,0:T(8,128)(2,1)S(1)}, u32[]{:S(2)}, u32[]{:S(2)}) collective-permute-start(bf16[3,128,256]{2,1,0:T(8,128)(2,1)S(1)} %get-tuple-element.36.own), channel_id=1, source_target_pairs={{0,8},{1,3},{2,10},{3,5},{4,12},{5,7},{6,14},{7,1},{8,16},{9,11},{... | collective-permute-start | bytes 589832 | tf_op jit(solution)/shard_map/ppermute | solution.py:391
  36.3 7.5 %collective-permute-start.12 = (bf16[3,128,256]{2,1,0:T(8,128)(2,1)S(1)}, bf16[3,128,256]{2,1,0:T(8,128)(2,1)S(1)}, u32[]{:S(2)}, u32[]{:S(2)}) collective-permute-start(bf16[3,128,256]{2,1,0:T(8,128)(2,1)S(1)} %get-tuple-element.36.own), channel_id=1, source_target_pairs={{0,24},{1,7},{2,26},{3,1},{4,28},{5,3},{6,30},{7,5},{8,0},{9,15},{... | collective-permute-start | bytes 589832 | tf_op jit(solution)/shard_map/ppermute | solution.py:391
  39.0 6.3 %collective-permute-start.13 = (bf16[3,128,256]{2,1,0:T(8,128)(2,1)S(1)}, bf16[3,128,256]{2,1,0:T(8,128)(2,1)S(1)}, u32[]{:S(2)}, u32[]{:S(2)}) collective-permute-start(bf16[3,128,256]{2,1,0:T(8,128)(2,1)S(1)} %get-tuple-element.36.own), channel_id=1, source_target_pairs={{0,16},{1,5},{2,18},{3,7},{4,20},{5,1},{6,22},{7,3},{8,24},{9,13},... | collective-permute-start | bytes 589832 | tf_op jit(solution)/shard_map/ppermute | solution.py:391
  45.4 8.2 %collective-permute-start.17 = (bf16[5,128,256]{2,1,0:T(8,128)(2,1)S(1)}, bf16[5,128,256]{2,1,0:T(8,128)(2,1)S(1)}, u32[]{:S(2)}, u32[]{:S(2)}) collective-permute-start(bf16[5,128,256]{2,1,0:T(8,128)(2,1)S(1)} %gather_step.1.part.p0), channel_id=1, source_target_pairs={{0,1},{1,0},{2,3},{3,2},{4,5},{5,4},{6,7},{7,6},{8,9},{9,8},{10,11... | collective-permute-start | bytes 983048 | tf_op jit(solution)/shard_map/ppermute | solution.py:378
  49.6 7.4 %collective-permute-start.14 = (bf16[5,128,256]{2,1,0:T(8,128)(2,1)S(1)}, bf16[5,128,256]{2,1,0:T(8,128)(2,1)S(1)}, u32[]{:S(2)}, u32[]{:S(2)}) collective-permute-start(bf16[5,128,256]{2,1,0:T(8,128)(2,1)S(1)} %gather_step.1.part.p0), channel_id=1, source_target_pairs={{0,2},{1,9},{2,4},{3,11},{4,6},{5,13},{6,0},{7,15},{8,10},{9,17},{... | collective-permute-start | bytes 983048 | tf_op jit(solution)/shard_map/ppermute | solution.py:391
  50.7 9.1 %collective-permute-start.15 = (bf16[5,128,256]{2,1,0:T(8,128)(2,1)S(1)}, bf16[5,128,256]{2,1,0:T(8,128)(2,1)S(1)}, u32[]{:S(2)}, u32[]{:S(2)}) collective-permute-start(bf16[5,128,256]{2,1,0:T(8,128)(2,1)S(1)} %gather_step.1.part.p0), channel_id=1, source_target_pairs={{0,6},{1,25},{2,0},{3,27},{4,2},{5,29},{6,4},{7,31},{8,14},{9,1},{... | collective-permute-start | bytes 983048 | tf_op jit(solution)/shard_map/ppermute | solution.py:391
  52.3 8.4 %collective-permute-start.16 = (bf16[5,128,256]{2,1,0:T(8,128)(2,1)S(1)}, bf16[5,128,256]{2,1,0:T(8,128)(2,1)S(1)}, u32[]{:S(2)}, u32[]{:S(2)}) collective-permute-start(bf16[5,128,256]{2,1,0:T(8,128)(2,1)S(1)} %gather_step.1.part.p0), channel_id=1, source_target_pairs={{0,4},{1,17},{2,6},{3,19},{4,0},{5,21},{6,2},{7,23},{8,12},{9,25},... | collective-permute-start | bytes 983048 | tf_op jit(solution)/shard_map/ppermute | solution.py:391
  60.7 3.1 %collective-permute-start.19 = (bf16[5,128,256]{2,1,0:T(8,128)(2,1)S(1)}, bf16[5,128,256]{2,1,0:T(8,128)(2,1)S(1)}, u32[]{:S(2)}, u32[]{:S(2)}) collective-permute-start(bf16[5,128,256]{2,1,0:T(8,128)(2,1)S(1)} %get-tuple-element.41.refs_0_.p3), channel_id=1, source_target_pairs={{0,1},{1,0},{2,3},{3,2},{4,5},{5,4},{6,7},{7,6},{8,9},{9,8},{10,11... | collective-permute-start | bytes 983048 | tf_op jit(solution)/shard_map/ppermute | solution.py:378
  62.0 1.9 %collective-permute-start.20 = (bf16[5,128,256]{2,1,0:T(8,128)(2,1)S(1)}, bf16[5,128,256]{2,1,0:T(8,128)(2,1)S(1)}, u32[]{:S(2)}, u32[]{:S(2)}) collective-permute-start(bf16[5,128,256]{2,1,0:T(8,128)(2,1)S(1)} %get-tuple-element.42.refs_1_.p1), channel_id=1, source_target_pairs={{0,1},{1,0},{2,3},{3,2},{4,5},{5,4},{6,7},{7,6},{8,9},{9,8},{10,11... | collective-permute-start | bytes 983048 | tf_op jit(solution)/shard_map/ppermute | solution.py:378
  62.0 2.9 %collective-permute-start.18 = (bf16[5,128,256]{2,1,0:T(8,128)(2,1)S(1)}, bf16[5,128,256]{2,1,0:T(8,128)(2,1)S(1)}, u32[]{:S(2)}, u32[]{:S(2)}) collective-permute-start(bf16[5,128,256]{2,1,0:T(8,128)(2,1)S(1)} %get-tuple-element.40.refs_2_.p2), channel_id=1, source_target_pairs={{0,1},{1,0},{2,3},{3,2},{4,5},{5,4},{6,7},{7,6},{8,9},{9,8},{10,11... | collective-permute-start | bytes 983048 | tf_op jit(solution)/shard_map/ppermute | solution.py:378
  65.4 6.2 %collective-permute-start.21 = (bf16[2,128,256]{2,1,0:T(8,128)(2,1)S(1)}, bf16[2,128,256]{2,1,0:T(8,128)(2,1)S(1)}, u32[]{:S(2)}, u32[]{:S(2)}) collective-permute-start(bf16[2,128,256]{2,1,0:T(8,128)(2,1)S(1)} %get-tuple-element.44), channel_id=1, source_target_pairs={{0,32},{32,64},{64,96},{96,0},{1,33},{33,65},{65,97},{97,1},{2,34}... | collective-permute-start | bytes 393224 | tf_op jit(solution)/shard_map/ppermute | solution.py:374
  65.9 5.7 %collective-permute-start.22 = (bf16[2,128,256]{2,1,0:T(8,128)(2,1)S(1)}, bf16[2,128,256]{2,1,0:T(8,128)(2,1)S(1)}, u32[]{:S(2)}, u32[]{:S(2)}) collective-permute-start(bf16[2,128,256]{2,1,0:T(8,128)(2,1)S(1)} %get-tuple-element.45), channel_id=1, source_target_pairs={{0,96},{32,0},{64,32},{96,64},{1,97},{33,1},{65,33},{97,65},{2,98}... | collective-permute-start | bytes 393224 | tf_op jit(solution)/shard_map/ppermute | solution.py:374
  68.2 5.8 %collective-permute-start.23 = (bf16[2,128,256]{2,1,0:T(8,128)(2,1)S(1)}, bf16[2,128,256]{2,1,0:T(8,128)(2,1)S(1)}, u32[]{:S(2)}, u32[]{:S(2)}) collective-permute-start(bf16[2,128,256]{2,1,0:T(8,128)(2,1)S(1)} %get-tuple-element.46), channel_id=1, source_target_pairs={{0,64},{32,96},{64,0},{96,32},{1,65},{33,97},{65,1},{97,33},{2,66}... | collective-permute-start | bytes 393224 | tf_op jit(solution)/shard_map/ppermute | solution.py:374
